TPU v7x, 128 devices: a whole 4x4x4 slice. The times are simulated.
128 devices in a mesh: blk: 8 (over z, y_lo), group: 16 (over y_hi, x, core).
Axes of the slice: x: 4, y: 4 (y_hi: 2, y_lo: 2; y = y_hi * 2 + y_lo), z: 4, core: 2. Of those that a mesh axis runs over, the one named last changes fastest.
Arguments:
- image_embeds: float32 [32768, 1152], P(('blk', 'group')), may hold values from -8.5 to 8.5
- text_embeds: float32 [32768, 1152], P(('blk', 'group')), may hold values from -8.5 to 8.5
- log_scale: float32 [1], replicated, may hold values from 4 to 4.8
- bias: float32 [1], replicated, may hold values from -6 to -3
Outputs:
- loss: float32 [1], replicated
- grad_image: float32 [32768, 1152], P(('blk', 'group'))
- grad_text: float32 [32768, 1152], P(('blk', 'group'))
- grad_log_scale: float32 [1], replicated
- grad_bias: float32 [1], replicated
All inputs are finite; a program needn't handle non-finite values.
Results may differ from a plain program's by a relative error of at most 0.00045.
Values may be sent and summed in bfloat16 or wider, within the bound.
No kernel may reach another device: no remote copies, remote signals or barrier semaphores. Data moves between devices by JAX's collectives and lax.ppermute only.
A program may use at most 192 MiB of HBM per device.

v0:
```python
import jax
import jax.numpy as jnp
from jax import lax
from jax.sharding import PartitionSpec as P

STEPS = 2


eps = 1e-06


def from_behind(value, axis, steps):
    count = lax.axis_size(axis)
    pairs = [(source, (source + steps) % count) for source in range(count)]
    return lax.ppermute(value, axis, pairs)


def unit_rows(embeds):
    length = jnp.sqrt(jnp.sum(embeds * embeds, axis=1, keepdims=True) + eps)
    return (embeds / length, length)


def pair_terms(image_block, text_block, scale_value, bias_value, marked):
    dots = lax.dot_general(
        image_block, text_block, (((1,), (1,)), ((), ())), preferred_element_type=jnp.float32
    )
    logits = scale_value * dots + bias_value
    signs = jnp.where(marked, jnp.float32(1.0), jnp.float32(-1.0))
    loss_part = jnp.sum(jax.nn.softplus(-signs * logits))
    weights = -signs * jax.nn.sigmoid(-signs * logits)
    return (weights.astype(jnp.bfloat16), loss_part, jnp.sum(weights), jnp.sum(weights * dots))


def back_rows(weights_half, rows_half):
    return lax.dot_general(
        weights_half, rows_half, (((0,), (0,)), ((), ())), preferred_element_type=jnp.float32
    )


def tangent_part(scale_value, unit, length, accum):
    return scale_value * (accum - unit * jnp.sum(unit * accum, axis=1, keepdims=True)) / length


def on_device(image_embeds, text_embeds, log_scale, bias):
    image_unit, image_length = unit_rows(image_embeds)
    text_unit, text_length = unit_rows(text_embeds)
    image_half = image_unit.astype(jnp.bfloat16)
    text_half = text_unit.astype(jnp.bfloat16)
    scale_value = jnp.exp(log_scale[0])
    bias_value = bias[0]
    text_group = lax.all_gather(text_half, "group", axis=0, tiled=True)
    own_rows = image_half.shape[0]
    group_rows = text_group.shape[0]
    width = image_half.shape[1]
    offset = lax.axis_index("group") * own_rows
    row_ids = lax.broadcasted_iota(jnp.int32, (own_rows, group_rows), 0)
    col_ids = lax.broadcasted_iota(jnp.int32, (own_rows, group_rows), 1)
    diagonal = col_ids == row_ids + offset
    no_pairs = jnp.zeros_like(diagonal)
    loss_sum = jnp.float32(0.0)
    weight_sum = jnp.float32(0.0)
    dot_sum = jnp.float32(0.0)
    text_acc = jnp.zeros((group_rows, width), jnp.float32)
    visiting = image_half
    moving_acc = jnp.zeros((own_rows, width), jnp.float32)
    for section_num in range(STEPS):
        marked = diagonal if section_num == 0 else no_pairs
        weights_half, loss_part, weight_part, dot_part = pair_terms(
            visiting, text_group, scale_value, bias_value, marked
        )
        loss_sum = loss_sum + loss_part
        weight_sum = weight_sum + weight_part
        dot_sum = dot_sum + dot_part
        moving_acc = moving_acc + jnp.dot(
            weights_half, text_group, preferred_element_type=jnp.float32
        )
        text_acc = text_acc + back_rows(weights_half, visiting)
        if section_num + 1 < STEPS:
            visiting = from_behind(visiting, "blk", -1)
            moving_acc = from_behind(moving_acc, "blk", -1)
    image_grad = from_behind(moving_acc, "blk", STEPS - 1)
    text_grad = lax.psum_scatter(text_acc, "group", scatter_dimension=0, tiled=True)
    totals = lax.psum((loss_sum, weight_sum, dot_sum), ("blk", "group"))
    total_rows = own_rows * lax.axis_size("blk") * lax.axis_size("group")
    grad_image = tangent_part(scale_value, image_unit, image_length, image_grad)
    grad_text = tangent_part(scale_value, text_unit, text_length, text_grad)
    loss = (totals[0] / total_rows).reshape(1)
    grad_log_scale = (scale_value * totals[2] / total_rows).reshape(1)
    grad_bias = (totals[1] / total_rows).reshape(1)
    return (loss, grad_image, grad_text, grad_log_scale, grad_bias)


def solution(mesh):
    return jax.shard_map(
        on_device,
        mesh=mesh,
        in_specs=(P(("blk", "group"), None), P(("blk", "group"), None), P(), P()),
        out_specs=(P(), P(("blk", "group"), None), P(("blk", "group"), None), P(), P()),
        check_vma=False,
    )
```

profile of v0, /device:TPU:0, one launch (start us, length us, event | category | flops | bytes accessed | tf_op | source)
XLA Modules:
  0.0 319.4 jit_solution(9076742447146002385)
XLA Ops:
  7.2 0.0 all-gather.2.cloned.1.call-start
  7.2 1.5 multiply_reduce_fusion.4
  8.7 2.2 fusion.9
  11.0 0.0 reduce-scatter.2.cloned.1.call-start
  11.1 0.2 multiply_reduce_fusion.5
  11.2 0.1 fusion.8
  11.4 5.2 %collective-permute-start = (bf16[256,1152]{1,0:T(8,128)(2,1)S(1)}, bf16[256,1152]{1,0:T(8,128)(2,1)S(1)}, u32[]{:S(2)}, u32[]{:S(2)}) collective-permute-start(bf16[256,1152]{1,0:T(8,128)(2,1)S(1)} %fusion.8), channel_id=1, source_target_pairs={{0,112},{16,0},{32,16},{48,32},{64,48},{80,64},{96,80},{112,96},{1... | collective-permute-start | bytes 1769480 | tf_op jit(solution)/shard_map/ppermute | solution.py:15
  17.9 73.6 %all-gather.2.cloned.1.call-done = bf16[4096,1152]{1,0:T(8,128)(2,1)} async-done(((bf16[256,1152]{1,0:T(8,128)(2,1)}), bf16[4096,1152]{1,0:T(8,128)(2,1)}) %all-gather.2.cloned.1.call-update) | async-done | bytes 9437200 | tf_op jit(solution)/shard_map/all_gather | solution.py:51
  91.6 10.0 %fusion.11 = (f32[]{:T(128)}, f32[]{:T(128)}, f32[]{:T(128)}, f32[256,4096]{1,0:T(8,128)S(1)}) fusion(f32[]{:T(128)} %bitcast.14, f32[]{:T(128)} %bitcast, s32[256]{0:T(256)S(1)} %iota_add_fusion, bf16[256,1152]{1,0:T(8,128)(2,1)S(1)} %fusion.8, bf16[4096,1152]{1,0:T(8,128)(2,1)} %all-gather.2.cloned.1.call-done), kind=kOutput, calls=%fused_computation.34 | convolution fusion | flops 2436890624 | bytes 14222356 | tf_op jit(solution)/shard_map/dot_general | solution.py:24
  101.6 8.8 %fusion.4 = f32[4096,1152]{1,0:T(8,128)} fusion(bf16[256,1152]{1,0:T(8,128)(2,1)S(1)} %fusion.8, f32[256,4096]{1,0:T(8,128)S(1)} %get-tuple-element.14, f32[]{:T(128)} %bitcast.15, f32[]{:T(128)} %bitcast, s32[256]{0:T(256)S(1)} %iota_add_fusion), kind=kOutput, calls=%fused_computation.22 | convolution fusion | flops 2427453440 | bytes 23659528 | tf_op jit(solution)/shard_map/dot_general | solution.py:35
  110.4 6.4 %fusion.10 = (f32[]{:T(128)}, f32[]{:T(128)}, f32[]{:T(128)}, f32[256,4096]{1,0:T(8,128)S(1)}) fusion(f32[]{:T(128)} %bitcast.18, f32[]{:T(128)} %bitcast, bf16[256,1152]{1,0:T(8,128)(2,1)S(1)} %collective-permute-done, bf16[4096,1152]{1,0:T(8,128)(2,1)S(1)} %bitcast.20), kind=kOutput, calls=%fused_computation.33 | convolution fusion | flops 2431647744 | bytes 14221332 | tf_op jit(solution)/shard_map/dot_general | solution.py:24
  116.9 2.0 copy-done.2
  118.8 12.0 %convolution_add_fusion = f32[4096,1152]{1,0:T(8,128)} fusion(f32[4096,1152]{1,0:T(8,128)} %fusion.4, bf16[256,1152]{1,0:T(8,128)(2,1)S(1)} %collective-permute-done, f32[256,4096]{1,0:T(8,128)S(1)} %get-tuple-element.15, f32[]{:T(128)} %bitcast.17, f32[]{:T(128)} %bitcast), kind=kOutput, calls=%fused_computation | convolution fusion | flops 2426929152 | bytes 42532872 | tf_op jit(solution)/shard_map/dot_general | solution.py:35
  130.9 8.7 %fusion.6 = f32[256,1152]{1,0:T(8,128)S(1)} fusion(bf16[4096,1152]{1,0:T(8,128)(2,1)} %all-gather.2.cloned.1.call-done, f32[256,4096]{1,0:T(8,128)} %copy-done.4, f32[]{:T(128)} %bitcast.13, f32[]{:T(128)} %bitcast, s32[256]{0:T(256)S(1)} %iota_add_fusion), kind=kOutput, calls=%fused_computation.24 | convolution fusion | flops 2427453440 | bytes 14812168 | tf_op jit(solution)/shard_map/dot_general | solution.py:74
  139.6 3.0 collective-permute-start.1
  142.7 25.6 %collective-permute-done.1 = f32[256,1152]{1,0:T(8,128)S(1)} collective-permute-done((f32[256,1152]{1,0:T(8,128)S(1)}, f32[256,1152]{1,0:T(8,128)S(1)}, u32[]{:S(2)}, u32[]{:S(2)}) %collective-permute-start.1) | collective-permute-done | bytes 1179680 | tf_op jit(solution)/shard_map/ppermute | solution.py:15
  168.3 7.7 %convolution_add_fusion.1 = f32[256,1152]{1,0:T(8,128)} fusion(f32[256,1152]{1,0:T(8,128)S(1)} %collective-permute-done.1, bf16[4096,1152]{1,0:T(8,128)(2,1)} %all-gather.2.cloned.1.call-done, f32[256,4096]{1,0:T(8,128)S(1)} %copy-done.3, f32[]{:T(128)} %bitcast.16, f32[]{:T(128)} %bitcast), kind=kOutput, calls=%fused_computation.13 | convolution fusion | flops 2422505472 | bytes 15990792 | tf_op jit(solution)/shard_map/dot_general | solution.py:74
  175.9 1.0 collective-permute-start.2
  180.9 100.2 %all-reduce = (f32[]{:T(128)}, f32[]{:T(128)}, f32[]{:T(128)}) all-reduce(f32[]{:T(128)S(6)} %add.78, f32[]{:T(128)S(6)} %add.83, f32[]{:T(128)S(6)} %add.84), channel_id=1, replica_groups=mesh['blk'=8,'group'=16] {'blk','group'}, use_global_device_ids=true, to_apply=%region_4.5 | all-reduce | flops 3 | bytes 24 | tf_op jit(solution)/shard_map/psum | solution.py:83
  283.1 0.3 multiply_reduce_fusion.3
  283.4 1.3 multiply_divide_fusion.1
  284.7 20.3 %reduce-scatter.2.cloned.1.call-done = f32[256,1152]{1,0:T(8,128)} async-done(((f32[4096,1152]{1,0:T(8,128)}), f32[256,1152]{1,0:T(8,128)}) %reduce-scatter.2.cloned.1.call-update) | async-done | bytes 1179664 | tf_op jit(solution)/shard_map/reduce_scatter | solution.py:82
  305.1 1.6 multiply_reduce_fusion.2
  306.6 2.6 multiply_divide_fusion
  (23 shorter events, 0.1 us)
Async XLA Ops:
  7.2 3.9 %copy-start = (f32[256,1152]{1,0:T(8,128)S(1)}, f32[256,1152]{1,0:T(8,128)}, u32[]{:S(2)}) copy-start(f32[256,1152]{1,0:T(8,128)} %param.4) | copy-start | bytes 3538948
  7.2 84.4 %all-gather.2.cloned.1.call-start = ((), (), s32[]{:S(2)}) async-start(), calls=%async_computation.1 | async-start | bytes 10027008 | tf_op jit(solution)/shard_map/all_gather | solution.py:51
  11.0 294.1 %reduce-scatter.2.cloned.1.call-start = ((), (), s32[]{:S(2)}) async-start(), calls=%async_computation.2 | async-start | bytes 20054016 | tf_op jit(solution)/shard_map/reduce_scatter | solution.py:82
  11.4 99.0 %collective-permute-start = (bf16[256,1152]{1,0:T(8,128)(2,1)S(1)}, bf16[256,1152]{1,0:T(8,128)(2,1)S(1)}, u32[]{:S(2)}, u32[]{:S(2)}) collective-permute-start(bf16[256,1152]{1,0:T(8,128)(2,1)S(1)} %fusion.8), channel_id=1, source_target_pairs={{0,112},{16,0},{32,16},{48,32},{64,48},{80,64},{96,80},{112,96},{1... | collective-permute-start | bytes 1769480 | tf_op jit(solution)/shard_map/ppermute | solution.py:15
  91.6 18.8 %slice-start = ((s8[9437184]{0:T(1024)(128)(4,1)}), s8[4194304]{0:T(1024)(128)(4,1)S(1)}, s32[]{:S(2)}) async-start(s8[9437184]{0:T(1024)(128)(4,1)} %bitcast.19), calls=%async_computation.3 | async-start | bytes 8388608
  91.6 18.8 %slice-start.1 = ((s8[9437184]{0:T(1024)(128)(4,1)}), s8[1048576]{0:T(1024)(128)(4,1)S(1)}, s32[]{:S(2)}) async-start(s8[9437184]{0:T(1024)(128)(4,1)} %bitcast.19), calls=%async_computation.4 | async-start | bytes 2097152
  101.6 8.8 %copy-start.4 = (f32[256,4096]{1,0:T(8,128)}, f32[256,4096]{1,0:T(8,128)S(1)}, u32[]{:S(2)}) copy-start(f32[256,4096]{1,0:T(8,128)S(1)} %get-tuple-element.14) | copy-start | bytes 12582916
  101.6 8.9 %slice-start.2 = ((s8[9437184]{0:T(1024)(128)(4,1)}), s8[4194304]{0:T(1024)(128)(4,1)S(1)}, s32[]{:S(2)}) async-start(s8[9437184]{0:T(1024)(128)(4,1)} %bitcast.19), calls=%async_computation.5 | async-start | bytes 8388608
  116.8 2.0 copy-start.2
  130.9 37.4 %copy-start.3 = (f32[256,4096]{1,0:T(8,128)S(1)}, f32[256,4096]{1,0:T(8,128)}, u32[]{:S(2)}) copy-start(f32[256,4096]{1,0:T(8,128)} %copy-done.2) | copy-start | bytes 12582916
  139.6 28.7 %collective-permute-start.1 = (f32[256,1152]{1,0:T(8,128)S(1)}, f32[256,1152]{1,0:T(8,128)S(1)}, u32[]{:S(2)}, u32[]{:S(2)}) collective-permute-start(f32[256,1152]{1,0:T(8,128)S(1)} %fusion.6), channel_id=1, source_target_pairs={{0,112},{16,0},{32,16},{48,32},{64,48},{80,64},{96,80},{112,96},{1... | collective-permute-start | bytes 3538952 | tf_op jit(solution)/shard_map/ppermute | solution.py:15
  175.9 129.1 %copy-start.1 = (f32[256,1152]{1,0:T(8,128)S(1)}, f32[256,1152]{1,0:T(8,128)}, u32[]{:S(2)}) copy-start(f32[256,1152]{1,0:T(8,128)} %param.5) | copy-start | bytes 3538948
  175.9 107.1 %collective-permute-start.2 = (f32[256,1152]{1,0:T(8,128)}, f32[256,1152]{1,0:T(8,128)S(1)}, u32[]{:S(2)}, u32[]{:S(2)}) collective-permute-start(f32[256,1152]{1,0:T(8,128)} %convolution_add_fusion.1), channel_id=1, source_target_pairs={{0,16},{16,32},{32,48},{48,64},{64,80},{80,96},{96,112},{112,0},{1... | collective-permute-start | bytes 3538952 | tf_op jit(solution)/shard_map/ppermute | solution.py:15
Sparse Core Ops, SparseCore 0:
  11.1 80.4 all-gather.1
  131.0 174.0 reduce-scatter.1
where the time goes:
time: 320 us; the launch traced here: 319 us
  waiting for transfers between devices  120 us (38%)
  blocking collectives  100 us (31%)
  matrix products  53.6 us (17%)
  between operations  24.7 us (8%)
  other arithmetic  9.86 us (3%)
  starting transfers between devices  9.34 us (3%)
    psum x1, blocking collectives, on_device(): totals = lax.psum((loss_sum, weight_sum, dot_sum), ('blk', 'group'))  100 us
    all_gather x1, waiting for transfers between devices, on_device(): text_group = lax.all_gather(text_half, 'group', axis=0, tiled=True)  73.6 us
    ppermute x3, waiting for transfers between devices, from_behind(): return lax.ppermute(value, axis, pairs)  25.6 us
    dot_general x2, matrix products, back_rows(): lax.dot_general(weights_half, rows_half, (((0,), (0,)), ((), ())), prefer...  20.9 us
    reduce_scatter x1, waiting for transfers between devices, on_device(): lax.psum_scatter(text_acc, 'group', scatter_dimension=0, tiled=True)  20.3 us
    dot_general x2, matrix products, on_device(): jnp.dot(weights_half, text_group, preferred_element_type=jnp.float32)  16.4 us
    dot_general x2, matrix products, pair_terms(): lax.dot_general(image_block, text_block, (((1,), (1,)), ((), ())), prefer...  16.4 us
    ppermute x3, starting transfers between devices, from_behind(): return lax.ppermute(value, axis, pairs)  9.26 us
  transfers between devices with their start and end apart: 5, of which 3 were waited for; matrix products, arithmetic and copies ran while one was open for 12% of the time, Pallas kernels for 0%

commit v1 on v0

v1 whole, which is shorter than its diff:
```python
import jax
import jax.numpy as jnp
from jax import lax
from jax.experimental import pallas as pl
from jax.experimental.pallas import tpu as pltpu
from jax.sharding import PartitionSpec as P

AXES = ("blk", "group")
EPS = 1e-06
LOG2E = 1.4426950408889634
LN2 = 0.6931471805599453
ROWS = 256
CHUNK = 16
LANES = 256
VMEM_LIMIT = 60 * 1024 * 1024


def place_index(z, y, x, core):
    z, y, x, core = z % 4, y % 4, x % 4, core % 2
    return (z * 2 + y % 2) * 16 + (y // 2) * 8 + x * 2 + core


def places():
    return [(z, y, x, c) for z in range(4) for y in range(4) for x in range(4) for c in range(2)]


def send(value, moved, back=False):
    pairs = [(place_index(*place), place_index(*moved(*place))) for place in places()]
    if back:
        pairs = [(target, source) for source, target in pairs]
    return lax.ppermute(value, AXES, pairs)


def other_core(z, y, x, c):
    return z, y, x, 1 - c


def x_up(z, y, x, c):
    return z, y, x + 1, c


def x_down(z, y, x, c):
    return z, y, x - 1, c


def x_far(z, y, x, c):
    return z, y, x + 2, c


def y_far(z, y, x, c):
    return z, y + 2, x, c


def before_up(z, y, x, c):
    return (z, y + 1, x, c) if y % 2 else (z - 1, y + 1, x, c)


def before_down(z, y, x, c):
    return (z, y - 1, x, c) if y % 2 else (z - 1, y - 1, x, c)


def z_up(z, y, x, c):
    return z + 1, y, x, c


def z_down(z, y, x, c):
    return z - 1, y, x, c


def z_far(z, y, x, c):
    return z + 2, y, x, c


TEXT_MOVES = (x_up, x_down, x_far)
IMAGE_MOVES = (y_far, before_up, before_down)
Z_MOVES = (z_up, z_down, z_far)


def halves_kernel(image_ref, text_ref, image_half_ref, text_half_ref):
    for ref, half_ref in ((image_ref, image_half_ref), (text_ref, text_half_ref)):
        rows = ref[...]
        length = jnp.sqrt(jnp.sum(rows * rows, axis=1, keepdims=True) + EPS)
        half_ref[...] = (rows / length).astype(jnp.bfloat16)


def halves(image_embeds, text_embeds):
    shape = jax.ShapeDtypeStruct(image_embeds.shape, jnp.bfloat16)
    return pl.pallas_call(
        halves_kernel,
        out_shape=(shape, shape),
        compiler_params=pltpu.CompilerParams(vmem_limit_bytes=VMEM_LIMIT),
        name="halves",
    )(image_embeds, text_embeds)


def log1p(value):
    small = value * (1.0 - value * (0.5 - value * (1.0 / 3.0)))
    return jnp.where(value < 1e-3, small, jnp.log(1.0 + value))


def fold_lanes(value):
    total = value[:, 0:128]
    for first in range(128, value.shape[1], 128):
        total = total + value[:, first : first + 128]
    return total


def pair_terms(dots_ref, weights_ref, first_row, rows, first_col, cols, scale, shift, sums_ref, marked):
    def body(step, carry):
        relu, weight_sum, dot_sum, product = carry
        start = pl.multiple_of(first_row + step * CHUNK, CHUNK)
        dots = dots_ref[pl.ds(start, CHUNK), first_col : first_col + cols]
        logits = dots * scale + shift
        decay = jnp.exp2(jnp.minimum(logits, -logits))
        above = 1.0 + decay
        share = pl.reciprocal(above, approx=True)
        share = share * (2.0 - above * share)
        if marked:
            row = lax.broadcasted_iota(jnp.int32, (CHUNK, cols), 0) + step * CHUNK
            same = row == lax.broadcasted_iota(jnp.int32, (CHUNK, cols), 1)
            logits = jnp.where(same, -logits, logits)
        weights = jnp.where(logits >= 0, share, decay * share)
        if marked:
            weights = jnp.where(same, -weights, weights)
        weights_ref[pl.ds(start, CHUNK), first_col : first_col + cols] = weights.astype(jnp.bfloat16)
        positive = jnp.maximum(logits, 0.0)
        weighted = weights * dots
        for first in range(0, CHUNK, 8):
            part = slice(first, first + 8)
            relu = relu + positive[part]
            weight_sum = weight_sum + weights[part]
            dot_sum = dot_sum + weighted[part]
            product = product * above[part] + decay[part]
        return relu, weight_sum, dot_sum, product

    zero = jnp.zeros((8, cols), jnp.float32)
    relu, weight_sum, dot_sum, product = lax.fori_loop(
        0, rows // CHUNK, body, (zero, zero, zero, zero), unroll=4
    )
    sums_ref[0] += fold_lanes(relu) * LN2 + fold_lanes(log1p(product))
    sums_ref[1] += fold_lanes(weight_sum)
    sums_ref[2] += fold_lanes(dot_sum)


def largest(value):
    return fold_max(jnp.max(jnp.abs(value).reshape(value.shape[0] // 8, 8, value.shape[1]), axis=0))


def fold_max(value):
    total = value[:, 0:128]
    for first in range(128, value.shape[1], 128):
        total = jnp.maximum(total, value[:, first : first + 128])
    return total


def pairs_kernel(
    scalars_ref, text_ref, mine_ref, other_ref,
    text_acc_ref, mine_acc_ref, other_acc_ref, sums_ref,
    dots_ref, weights_ref,
):
    step = pl.program_id(0)
    scale, shift = scalars_ref[0], scalars_ref[1]
    texts = text_ref.shape[0]

    @pl.when(step == 0)
    def _():
        sums_ref[...] = jnp.zeros_like(sums_ref)

    for place, ref in enumerate((mine_ref, other_ref)):
        dots_ref[place * ROWS : (place + 1) * ROWS, :] = lax.dot_general(
            ref[...], text_ref[...], (((1,), (1,)), ((), ())), preferred_element_type=jnp.float32
        )

    @pl.when(step == 0)
    def _():
        pair_terms(dots_ref, weights_ref, 0, ROWS, 0, LANES, scale, shift, sums_ref, True)

    @pl.when(step != 0)
    def _():
        pair_terms(dots_ref, weights_ref, 0, ROWS, 0, LANES, scale, shift, sums_ref, False)

    for first in range(LANES, texts, LANES):
        pair_terms(dots_ref, weights_ref, 0, ROWS, first, LANES, scale, shift, sums_ref, False)
    for first in range(0, texts, LANES):
        pair_terms(dots_ref, weights_ref, ROWS, ROWS, first, LANES, scale, shift, sums_ref, False)

    back = jnp.zeros((texts, text_ref.shape[1]), jnp.float32)
    for place, (ref, acc_ref) in enumerate(((mine_ref, mine_acc_ref), (other_ref, other_acc_ref))):
        weights = weights_ref[place * ROWS : (place + 1) * ROWS, :]
        acc = jnp.dot(weights, text_ref[...], preferred_element_type=jnp.float32)
        acc_ref[...] = acc
        sums_ref[3] = jnp.maximum(sums_ref[3], largest(acc))
        back = back + lax.dot_general(
            weights, ref[...], (((0,), (0,)), ((), ())), preferred_element_type=jnp.float32
        )

    @pl.when(step == 0)
    def _():
        text_acc_ref[...] = back

    @pl.when(step != 0)
    def _():
        text_acc_ref[...] += back

    @pl.when(step == pl.num_programs(0) - 1)
    def _():
        sums_ref[4] = largest(text_acc_ref[...])


def pairs(scalars, texts, mine, other):
    count, width = texts.shape
    steps = mine.shape[0] // ROWS
    rows = pl.BlockSpec((ROWS, width), lambda k: (k, 0))
    whole = pl.BlockSpec((count, width), lambda k: (0, 0))
    return pl.pallas_call(
        pairs_kernel,
        grid=(steps,),
        in_specs=[pl.BlockSpec(memory_space=pltpu.SMEM), whole, rows, rows],
        out_specs=[whole, rows, rows, pl.BlockSpec((5, 8, 128), lambda k: (0, 0, 0))],
        out_shape=[
            jax.ShapeDtypeStruct((count, width), jnp.float32),
            jax.ShapeDtypeStruct(mine.shape, jnp.float32),
            jax.ShapeDtypeStruct(other.shape, jnp.float32),
            jax.ShapeDtypeStruct((5, 8, 128), jnp.float32),
        ],
        scratch_shapes=[
            pltpu.VMEM((2 * ROWS, count), jnp.float32),
            pltpu.VMEM((2 * ROWS, count), jnp.bfloat16),
        ],
        compiler_params=pltpu.CompilerParams(vmem_limit_bytes=VMEM_LIMIT),
        cost_estimate=pl.CostEstimate(
            flops=6 * count * 2 * mine.shape[0] * width, bytes_accessed=20_000_000, transcendentals=4_000_000
        ),
        name="pairs",
    )(scalars, texts, mine, other)


def tangent_part(scale_value, embeds, accum):
    length = jnp.sqrt(jnp.sum(embeds * embeds, axis=1, keepdims=True) + EPS)
    unit = embeds / length
    return scale_value * (accum - unit * jnp.sum(unit * accum, axis=1, keepdims=True)) / length


def factor_of(limit):
    return 1024.0 / jnp.maximum(limit, 1e-35)


def packed(value, factor):
    return (value * factor).astype(jnp.float16)


def on_device(image_embeds, text_embeds, log_scale, bias):
    image_half, text_half = halves(image_embeds, text_embeds)
    scale_value = jnp.exp(log_scale[0])
    scalars = jnp.stack([scale_value * LOG2E, bias[0] * LOG2E])
    texts = jnp.concatenate([text_half] + [send(text_half, move) for move in TEXT_MOVES], axis=0)
    mine = jnp.concatenate([image_half] + [send(image_half, move) for move in IMAGE_MOVES], axis=0)
    other = send(mine, other_core)
    text_acc, mine_acc, other_acc, sums = pairs(scalars, texts, mine, other)

    folded = jnp.concatenate([jnp.sum(sums[:3], axis=(1, 2)), jnp.max(sums[3:], axis=(1, 2))])
    neighbour = send(jnp.broadcast_to(folded[:, None], (5, 128)), other_core)[:, 0]
    totals = folded[:3] + neighbour[:3]
    image_factor = factor_of(folded[3] + neighbour[3])
    text_factor = factor_of(folded[4])

    text_back = []
    small = jnp.broadcast_to(jnp.concatenate([totals, 1.0 / text_factor[None]])[:, None], (4, 128))
    for place, move in enumerate(TEXT_MOVES):
        rows = text_acc[(place + 1) * ROWS : (place + 2) * ROWS]
        text_back.append((send(packed(rows, text_factor), move, back=True), send(small, move, back=True)[:, 0]))

    mine_acc = mine_acc + send(other_acc, other_core)
    totals = (totals + text_back[2][1][:3]) + (text_back[0][1][:3] + text_back[1][1][:3])
    image_back = []
    small = jnp.broadcast_to(jnp.concatenate([totals, 1.0 / image_factor[None]])[:, None], (4, 128))
    for place, move in enumerate(IMAGE_MOVES):
        rows = mine_acc[(place + 1) * ROWS : (place + 2) * ROWS]
        image_back.append((send(packed(rows, image_factor), move, back=True), send(small, move, back=True)[:, 0]))
    own_parity = totals + image_back[0][1][:3]
    other_parity = image_back[1][1][:3] + image_back[2][1][:3]
    odd = lax.axis_index("blk") % 2 == 1
    totals = jnp.concatenate(
        [jnp.where(odd, other_parity, own_parity), jnp.where(odd, own_parity, other_parity)]
    )
    small = jnp.broadcast_to(totals[:, None], (6, 128))
    from_up, from_down, from_far = (send(small, move)[:, 0] for move in Z_MOVES)
    totals = (totals + from_far) + (from_up + from_down)
    totals = totals[:3] + totals[3:]

    text_sum, image_sum = text_acc[:ROWS], mine_acc[:ROWS]
    for rows, numbers in text_back:
        text_sum = text_sum + rows.astype(jnp.float32) * numbers[3]
    for rows, numbers in image_back:
        image_sum = image_sum + rows.astype(jnp.float32) * numbers[3]
    grad_text = tangent_part(scale_value, text_embeds, text_sum)
    grad_image = tangent_part(scale_value, image_embeds, image_sum)
    total_rows = ROWS * lax.axis_size("blk") * lax.axis_size("group")
    loss = (totals[0] / total_rows).reshape(1)
    grad_bias = (totals[1] / total_rows).reshape(1)
    grad_log_scale = (scale_value * totals[2] / total_rows).reshape(1)
    return (loss, grad_image, grad_text, grad_log_scale, grad_bias)


def solution(mesh):
    return jax.shard_map(
        on_device,
        mesh=mesh,
        in_specs=(P(AXES, None), P(AXES, None), P(), P()),
        out_specs=(P(), P(AXES, None), P(AXES, None), P(), P()),
        check_vma=False,
    )
```

time: 320 us -> 227 us (0.71)
  blocking collectives: 100 us -> 0 us
  matrix products: 53.6 us -> 0 us
  Pallas kernels: 0 us -> 35.2 us
  starting transfers between devices: 9.34 us -> 38.6 us
  waiting for transfers between devices: 120 us -> 98.4 us
  other arithmetic: 9.86 us -> 28.1 us
  between operations: 24.7 us -> 9.54 us
  local copies, waits for them, and re-layouts: 1.99 us -> 14.8 us
    psum x1 -> x0, blocking collectives: 100 us -> none  [on_device(): totals = lax.psum((loss_sum, weight_sum, dot_sum), ('blk', 'group'))]
    all_gather x1 -> x0, waiting for transfers between devices: 73.6 us -> none  [on_device(): text_group = lax.all_gather(text_half, 'group', axis=0, tiled=True)]
    ppermute x3 -> x24, waiting for transfers between devices: 25.6 us -> 98.4 us  [send(): return lax.ppermute(value, AXES, pairs)]
    dot_general x6 -> x0, matrix products: 53.6 us -> none  [the longest x2 20.9 us: back_rows(): lax.dot_general(weights_half, rows_half, (((0,), (0,)), ((), ())), prefer...]
    pallas_call x0 -> x2, Pallas kernels: none -> 35.2 us  [the longest x1 32.3 us: pairs(): pl.pallas_call(pairs_kernel, grid=(steps,), in_specs=[pl.BlockSpec(memory...]
    ppermute x3 -> x24, starting transfers between devices: 9.26 us -> 38.6 us  [send(): return lax.ppermute(value, AXES, pairs)]
    reduce_scatter x1 -> x0, waiting for transfers between devices: 20.3 us -> none  [on_device(): lax.psum_scatter(text_acc, 'group', scatter_dimension=0, tiled=True)]
    slice x0 -> x9, local copies, waits for them, and re-layouts: none -> 9.49 us  [the longest x3 3.87 us: on_device(): text_sum = text_sum + rows.astype(jnp.float32) * numbers[3]]
  transfers between devices with their start and end apart: 5 -> 24, of which waited for: 3 -> 12; matrix products, arithmetic and copies ran while one was open for 12% -> 14% of each run, Pallas kernels for 0% -> 0%
where the time goes in v1:
time: 227 us; the launch traced here: 225 us
  waiting for transfers between devices  98.4 us (43%)
  starting transfers between devices  38.6 us (17%)
  Pallas kernels  35.2 us (16%)
  other arithmetic  28.1 us (12%)
  local copies, waits for them, and re-layouts  14.8 us (7%)
  between operations  9.54 us (4%)
    ppermute x24, waiting for transfers between devices, send(): return lax.ppermute(value, AXES, pairs)  98.4 us
    ppermute x24, starting transfers between devices, send(): return lax.ppermute(value, AXES, pairs)  38.6 us
    pallas_call x1, Pallas kernels, pairs(): pl.pallas_call(pairs_kernel, grid=(steps,), in_specs=[pl.BlockSpec(memory...  32.3 us
    div x2, other arithmetic, tangent_part(): scale_value * (accum - unit * jnp.sum(unit * accum, axis=1, keepdims=True))  8.42 us
    reduce_sum x2, other arithmetic, tangent_part(): jnp.sum(unit * accum, axis=1, keepdims=True)  6.39 us
  transfers between devices with their start and end apart: 24, of which 12 were waited for; matrix products, arithmetic and copies ran while one was open for 14% of the time, Pallas kernels for 0%

profile of v1, /device:TPU:0, one launch (start us, length us, event | category | flops | bytes accessed | tf_op | source)
XLA Modules:
  0.0 224.6 jit_solution(4689478182979731845)
XLA Ops:
  0.6 2.9 %halves.1 = (bf16[256,1152]{1,0:T(8,128)(2,1)}, bf16[256,1152]{1,0:T(8,128)(2,1)}) custom-call(f32[256,1152]{1,0:T(8,128)} %image_ref.1, f32[256,1152]{1,0:T(8,128)} %text_ref.1), custom_call_target="tpu_custom_call" | custom-call | tf_op jit(solution)/shard_map/halves/pallas_call | solution.py:88
  3.5 3.3 %collective-permute-start.3 = (bf16[256,1152]{1,0:T(8,128)(2,1)}, bf16[256,1152]{1,0:T(8,128)(2,1)S(1)}, u32[]{:S(2)}, u32[]{:S(2)}) collective-permute-start(bf16[256,1152]{1,0:T(8,128)(2,1)} %get-tuple-element.12), channel_id=1, source_target_pairs={{0,8},{1,9},{2,10},{3,11},{4,12},{5,13},{6,14},{7,15},{16,24},{17,... | collective-permute-start | bytes 1769480 | tf_op jit(solution)/shard_map/ppermute | solution.py:31
  6.8 4.2 %collective-permute-start.4 = (bf16[256,1152]{1,0:T(8,128)(2,1)}, bf16[256,1152]{1,0:T(8,128)(2,1)S(1)}, u32[]{:S(2)}, u32[]{:S(2)}) collective-permute-start(bf16[256,1152]{1,0:T(8,128)(2,1)} %get-tuple-element.12), channel_id=1, source_target_pairs={{0,112},{1,113},{2,114},{3,115},{4,116},{5,117},{6,118},{7,119},{1... | collective-permute-start | bytes 1769480 | tf_op jit(solution)/shard_map/ppermute | solution.py:31
  11.0 2.6 %collective-permute-start.5 = (bf16[256,1152]{1,0:T(8,128)(2,1)}, bf16[256,1152]{1,0:T(8,128)(2,1)S(1)}, u32[]{:S(2)}, u32[]{:S(2)}) collective-permute-start(bf16[256,1152]{1,0:T(8,128)(2,1)} %get-tuple-element.12), channel_id=1, source_target_pairs={{0,120},{1,121},{2,122},{3,123},{4,124},{5,125},{6,126},{7,127},{1... | collective-permute-start | bytes 1769480 | tf_op jit(solution)/shard_map/ppermute | solution.py:31
  15.5 6.0 %collective-permute-done.3 = bf16[256,1152]{1,0:T(8,128)(2,1)S(1)} collective-permute-done((bf16[256,1152]{1,0:T(8,128)(2,1)}, bf16[256,1152]{1,0:T(8,128)(2,1)S(1)}, u32[]{:S(2)}, u32[]{:S(2)}) %collective-permute-start.3) | collective-permute-done | bytes 589856 | tf_op jit(solution)/shard_map/ppermute | solution.py:31
  22.3 20.6 %collective-permute-done.4 = bf16[256,1152]{1,0:T(8,128)(2,1)S(1)} collective-permute-done((bf16[256,1152]{1,0:T(8,128)(2,1)}, bf16[256,1152]{1,0:T(8,128)(2,1)S(1)}, u32[]{:S(2)}, u32[]{:S(2)}) %collective-permute-start.4) | collective-permute-done | bytes 589856 | tf_op jit(solution)/shard_map/ppermute | solution.py:31
  51.7 10.0 %collective-permute-done = bf16[256,1152]{1,0:T(8,128)(2,1)S(1)} collective-permute-done((bf16[256,1152]{1,0:T(8,128)(2,1)S(1)}, bf16[256,1152]{1,0:T(8,128)(2,1)S(1)}, u32[]{:S(2)}, u32[]{:S(2)}) %collective-permute-start) | collective-permute-done | bytes 589856 | tf_op jit(solution)/shard_map/ppermute | solution.py:31
  61.6 11.9 %collective-permute-done.1 = bf16[256,1152]{1,0:T(8,128)(2,1)S(1)} collective-permute-done((bf16[256,1152]{1,0:T(8,128)(2,1)S(1)}, bf16[256,1152]{1,0:T(8,128)(2,1)S(1)}, u32[]{:S(2)}, u32[]{:S(2)}) %collective-permute-start.1) | collective-permute-done | bytes 589856 | tf_op jit(solution)/shard_map/ppermute | solution.py:31
  76.9 32.3 %pairs.1 = (f32[1024,1152]{1,0:T(8,128)}, f32[1024,1152]{1,0:T(8,128)}, f32[1024,1152]{1,0:T(8,128)}, f32[5,8,128]{2,1,0:T(8,128)}) custom-call(f32[2]{0:T(128)} %pad_maximum_fusion.1.scalars_ref, bf16[1024,1152]{1,0:T(8,128)(2,1)} %pad_maximum_fusion.text_ref, bf16[1024,1152]{1,0:T(8,128)(2,1)} %constant_dynamic-update-slice_fusion.mine_ref, ...), custom_call_target="tpu_custom_call" | custom-call | flops 14495514624 | bytes 20000000 | tf_op jit(solution)/shard_map/pairs/pallas_call | solution.py:215
  112.9 4.4 %collective-permute-done.7 = f32[5,128]{0,1:T(8,128)S(1)} collective-permute-done((f32[5,128]{0,1:T(8,128)S(1)}, f32[5,128]{0,1:T(8,128)S(1)}, u32[]{:S(2)}, u32[]{:S(2)}) %collective-permute-start.7) | collective-permute-done | bytes 2592 | tf_op jit(solution)/shard_map/ppermute | solution.py:31
  122.8 3.0 %collective-permute-done.10 = f32[4,128]{0,1:T(8,128)S(1)} collective-permute-done((f32[4,128]{0,1:T(8,128)S(1)}, f32[4,128]{0,1:T(8,128)S(1)}, u32[]{:S(2)}, u32[]{:S(2)}) %collective-permute-start.10) | collective-permute-done | bytes 2080 | tf_op jit(solution)/shard_map/ppermute | solution.py:31
  128.2 5.0 %collective-permute-start.11 = (f32[4,128]{0,1:T(8,128)S(1)}, f32[4,128]{0,1:T(8,128)S(1)}, u32[]{:S(2)}, u32[]{:S(2)}) collective-permute-start(f32[4,128]{0,1:T(8,128)S(1)} %broadcast_in_dim.10), channel_id=1, source_target_pairs={{112,0},{113,1},{114,2},{115,3},{116,4},{117,5},{118,6},{119,7},{8... | collective-permute-start | bytes 6152 | tf_op jit(solution)/shard_map/ppermute | solution.py:31
  135.2 5.6 %collective-permute-done.12 = f32[4,128]{0,1:T(8,128)S(1)} collective-permute-done((f32[4,128]{0,1:T(8,128)S(1)}, f32[4,128]{0,1:T(8,128)S(1)}, u32[]{:S(2)}, u32[]{:S(2)}) %collective-permute-start.12) | collective-permute-done | bytes 2080 | tf_op jit(solution)/shard_map/ppermute | solution.py:31
  143.9 3.3 %multiply_convert_fusion.2 = (f16[256,1152]{1,0:T(8,128)(2,1)}, f16[256,1152]{1,0:T(8,128)(2,1)}, f16[256,1152]{1,0:T(8,128)(2,1)}) fusion(f32[1024,1152]{1,0:T(8,128)} %get-tuple-element.16, f32[]{:T(128)} %bitcast.15), kind=kLoop, calls=%fused_computation.16 | loop fusion | flops 1769472 | bytes 5308420 | tf_op jit(solution)/shard_map/convert_element_type | solution.py:249
  147.2 2.6 %collective-permute-start.21 = (f16[256,1152]{1,0:T(8,128)(2,1)}, f16[256,1152]{1,0:T(8,128)(2,1)S(1)}, u32[]{:S(2)}, u32[]{:S(2)}) collective-permute-start(f16[256,1152]{1,0:T(8,128)(2,1)} %get-tuple-element.17), channel_id=1, source_target_pairs={{2,0},{3,1},{4,2},{5,3},{6,4},{7,5},{0,6},{1,7},{18,16},{19,17},{2... | collective-permute-start | bytes 1769480 | tf_op jit(solution)/shard_map/ppermute | solution.py:31
  151.4 3.3 %collective-permute-start.16 = (f32[6,128]{0,1:T(8,128)}, f32[6,128]{0,1:T(8,128)}, u32[]{:S(2)}, u32[]{:S(2)}) collective-permute-start(f32[6,128]{0,1:T(8,128)} %broadcast_in_dim.11), channel_id=1, source_target_pairs={{0,96},{1,97},{2,98},{3,99},{4,100},{5,101},{6,102},{7,103},{16,11... | collective-permute-start | bytes 9224 | tf_op jit(solution)/shard_map/ppermute | solution.py:31
  165.9 9.4 %collective-permute-done.22 = f16[256,1152]{1,0:T(8,128)(2,1)S(1)} collective-permute-done((f16[256,1152]{1,0:T(8,128)(2,1)}, f16[256,1152]{1,0:T(8,128)(2,1)S(1)}, u32[]{:S(2)}, u32[]{:S(2)}) %collective-permute-start.22) | collective-permute-done | bytes 589856 | tf_op jit(solution)/shard_map/ppermute | solution.py:31
  175.3 4.0 %multiply_reduce_fusion = f32[256]{0:T(256)S(1)} fusion(f32[256,1152]{1,0:T(8,128)S(1)} %copy-done, f32[256]{0:T(256)S(1)} %add_sqrt_fusion, f32[]{:T(128)} %bitcast.18, f16[256,1152]{1,0:T(8,128)(2,1)} %collective-permute-done.23, f32[]{:T(128)} %bitcast.17, f16[256,1152]{1,0:T(8,128)(2,1)S(1)} %collective-permute-done.22, f32[]{:T(128)} %bitcast.16, ...), kind=kLoop, calls=%fused_computation.11 | loop fusion | flops 3538688 | bytes 4130828 | tf_op jit(solution)/shard_map/reduce_sum | solution.py:241
  179.3 4.3 %add.98 = f32[1024,1152]{1,0:T(8,128)S(1)} add(f32[1024,1152]{1,0:T(8,128)} %get-tuple-element.14, f32[1024,1152]{1,0:T(8,128)} %collective-permute-done.17) | non-fusion elementwise | flops 1179648 | bytes 14155776 | tf_op jit(solution)/shard_map/add | solution.py:273
  186.3 5.0 %multiply_divide_fusion = f32[256,1152]{1,0:T(8,128)} fusion(f32[256]{0:T(256)S(1)} %multiply_reduce_fusion, f32[256]{0:T(256)S(1)} %add_sqrt_fusion, f32[]{:T(128)} %bitcast, f32[256,1152]{1,0:T(8,128)S(1)} %copy-done, f32[]{:T(128)} %bitcast.18, f16[256,1152]{1,0:T(8,128)(2,1)} %collective-permute-done.23, f32[]{:T(128)} %bitcast.17, ...), kind=kLoop, calls=%fused_computation.10 | loop fusion | flops 4128768 | bytes 5310480 | tf_op jit(solution)/shard_map/div | solution.py:241
  191.3 10.0 %collective-permute-done.18 = f16[256,1152]{1,0:T(8,128)(2,1)S(1)} collective-permute-done((f16[256,1152]{1,0:T(8,128)(2,1)S(1)}, f16[256,1152]{1,0:T(8,128)(2,1)S(1)}, u32[]{:S(2)}, u32[]{:S(2)}) %collective-permute-start.18) | collective-permute-done | bytes 589856 | tf_op jit(solution)/shard_map/ppermute | solution.py:31
  201.3 14.1 %collective-permute-done.19 = f16[256,1152]{1,0:T(8,128)(2,1)S(1)} collective-permute-done((f16[256,1152]{1,0:T(8,128)(2,1)S(1)}, f16[256,1152]{1,0:T(8,128)(2,1)S(1)}, u32[]{:S(2)}, u32[]{:S(2)}) %collective-permute-start.19) | collective-permute-done | bytes 589856 | tf_op jit(solution)/shard_map/ppermute | solution.py:31
  215.4 2.4 %multiply_reduce_fusion.2 = f32[256]{0:T(256)S(1)} fusion(f32[256,1152]{1,0:T(8,128)S(1)} %copy-done.1, f32[256]{0:T(256)S(1)} %add_sqrt_fusion.1, f32[]{:T(128)} %bitcast.14, f16[256,1152]{1,0:T(8,128)(2,1)S(1)} %collective-permute-done.20, f32[]{:T(128)} %bitcast.13, f16[256,1152]{1,0:T(8,128)(2,1)S(1)} %collective-permute-done.19, f32[]{:T(128)} %bitcast.12, ...), kind=kLoop, calls=%fused_computation.18 | loop fusion | flops 3538688 | bytes 4130828 | tf_op jit(solution)/shard_map/reduce_sum | solution.py:241
  217.8 3.4 %multiply_divide_fusion.1 = f32[256,1152]{1,0:T(8,128)} fusion(f32[256]{0:T(256)S(1)} %multiply_reduce_fusion.2, f32[256]{0:T(256)S(1)} %add_sqrt_fusion.1, f32[]{:T(128)} %bitcast, f32[256,1152]{1,0:T(8,128)S(1)} %copy-done.1, f32[]{:T(128)} %bitcast.14, f16[256,1152]{1,0:T(8,128)(2,1)S(1)} %collective-permute-done.20, f32[]{:T(128)} %bitcast.13, ...), kind=kLoop, calls=%fused_computation.17 | loop fusion | flops 4128768 | bytes 5310480 | tf_op jit(solution)/shard_map/div | solution.py:241
  (91 shorter events, 41.6 us)
Async XLA Ops:
  3.5 18.0 %collective-permute-start.3 = (bf16[256,1152]{1,0:T(8,128)(2,1)}, bf16[256,1152]{1,0:T(8,128)(2,1)S(1)}, u32[]{:S(2)}, u32[]{:S(2)}) collective-permute-start(bf16[256,1152]{1,0:T(8,128)(2,1)} %get-tuple-element.12), channel_id=1, source_target_pairs={{0,8},{1,9},{2,10},{3,11},{4,12},{5,13},{6,14},{7,15},{16,24},{17,... | collective-permute-start | bytes 1769480 | tf_op jit(solution)/shard_map/ppermute | solution.py:31
  6.8 36.1 %collective-permute-start.4 = (bf16[256,1152]{1,0:T(8,128)(2,1)}, bf16[256,1152]{1,0:T(8,128)(2,1)S(1)}, u32[]{:S(2)}, u32[]{:S(2)}) collective-permute-start(bf16[256,1152]{1,0:T(8,128)(2,1)} %get-tuple-element.12), channel_id=1, source_target_pairs={{0,112},{1,113},{2,114},{3,115},{4,116},{5,117},{6,118},{7,119},{1... | collective-permute-start | bytes 1769480 | tf_op jit(solution)/shard_map/ppermute | solution.py:31
  11.0 32.9 %collective-permute-start.5 = (bf16[256,1152]{1,0:T(8,128)(2,1)}, bf16[256,1152]{1,0:T(8,128)(2,1)S(1)}, u32[]{:S(2)}, u32[]{:S(2)}) collective-permute-start(bf16[256,1152]{1,0:T(8,128)(2,1)} %get-tuple-element.12), channel_id=1, source_target_pairs={{0,120},{1,121},{2,122},{3,123},{4,124},{5,125},{6,126},{7,127},{1... | collective-permute-start | bytes 1769480 | tf_op jit(solution)/shard_map/ppermute | solution.py:31
  44.7 32.2 %collective-permute-start.6 = (bf16[1024,1152]{1,0:T(8,128)(2,1)}, bf16[1024,1152]{1,0:T(8,128)(2,1)}, u32[]{:S(2)}, u32[]{:S(2)}) collective-permute-start(bf16[1024,1152]{1,0:T(8,128)(2,1)} %constant_dynamic-update-slice_fusion.mine_ref), channel_id=1, source_target_pairs={{0,1},{1,0},{2,3},{3,2},{4,5},{5,4},{6,7},{7,6},{16,17},{17,16},{1... | collective-permute-start | bytes 7077896 | tf_op jit(solution)/shard_map/ppermute | solution.py:31
  44.7 17.0 %collective-permute-start = (bf16[256,1152]{1,0:T(8,128)(2,1)S(1)}, bf16[256,1152]{1,0:T(8,128)(2,1)S(1)}, u32[]{:S(2)}, u32[]{:S(2)}) collective-permute-start(bf16[256,1152]{1,0:T(8,128)(2,1)S(1)} %copy-done.2), channel_id=1, source_target_pairs={{0,2},{1,3},{2,4},{3,5},{4,6},{5,7},{6,0},{7,1},{16,18},{17,19},{1... | collective-permute-start | bytes 1769480 | tf_op jit(solution)/shard_map/ppermute | solution.py:31
  46.2 27.4 %collective-permute-start.1 = (bf16[256,1152]{1,0:T(8,128)(2,1)S(1)}, bf16[256,1152]{1,0:T(8,128)(2,1)S(1)}, u32[]{:S(2)}, u32[]{:S(2)}) collective-permute-start(bf16[256,1152]{1,0:T(8,128)(2,1)S(1)} %copy-done.2), channel_id=1, source_target_pairs={{0,6},{1,7},{2,0},{3,1},{4,2},{5,3},{6,4},{7,5},{16,22},{17,23},{1... | collective-permute-start | bytes 1769480 | tf_op jit(solution)/shard_map/ppermute | solution.py:31
  47.9 27.3 %collective-permute-start.2 = (bf16[256,1152]{1,0:T(8,128)(2,1)S(1)}, bf16[256,1152]{1,0:T(8,128)(2,1)S(1)}, u32[]{:S(2)}, u32[]{:S(2)}) collective-permute-start(bf16[256,1152]{1,0:T(8,128)(2,1)S(1)} %copy-done.2), channel_id=1, source_target_pairs={{0,4},{1,5},{2,6},{3,7},{4,0},{5,1},{6,2},{7,3},{16,20},{17,21},{1... | collective-permute-start | bytes 1769480 | tf_op jit(solution)/shard_map/ppermute | solution.py:31
  109.2 70.1 %collective-permute-start.17 = (f32[1024,1152]{1,0:T(8,128)}, f32[1024,1152]{1,0:T(8,128)}, u32[]{:S(2)}, u32[]{:S(2)}) collective-permute-start(f32[1024,1152]{1,0:T(8,128)} %get-tuple-element.15), channel_id=1, source_target_pairs={{0,1},{1,0},{2,3},{3,2},{4,5},{5,4},{6,7},{7,6},{16,17},{17,16},{1... | collective-permute-start | bytes 14155784 | tf_op jit(solution)/shard_map/ppermute | solution.py:31
  111.3 6.0 %collective-permute-start.7 = (f32[5,128]{0,1:T(8,128)S(1)}, f32[5,128]{0,1:T(8,128)S(1)}, u32[]{:S(2)}, u32[]{:S(2)}) collective-permute-start(f32[5,128]{0,1:T(8,128)S(1)} %broadcast_in_dim.8), channel_id=1, source_target_pairs={{0,1},{1,0},{2,3},{3,2},{4,5},{5,4},{6,7},{7,6},{16,17},{17,16},{1... | collective-permute-start | bytes 7688 | tf_op jit(solution)/shard_map/ppermute | solution.py:31
  117.4 5.4 %collective-permute-start.9 = (f32[4,128]{0,1:T(8,128)S(1)}, f32[4,128]{0,1:T(8,128)S(1)}, u32[]{:S(2)}, u32[]{:S(2)}) collective-permute-start(f32[4,128]{0,1:T(8,128)S(1)} %broadcast_in_dim.9), channel_id=1, source_target_pairs={{2,0},{3,1},{4,2},{5,3},{6,4},{7,5},{0,6},{1,7},{18,16},{19,17},{2... | collective-permute-start | bytes 6152 | tf_op jit(solution)/shard_map/ppermute | solution.py:31
  119.4 6.5 %collective-permute-start.10 = (f32[4,128]{0,1:T(8,128)S(1)}, f32[4,128]{0,1:T(8,128)S(1)}, u32[]{:S(2)}, u32[]{:S(2)}) collective-permute-start(f32[4,128]{0,1:T(8,128)S(1)} %broadcast_in_dim.9), channel_id=1, source_target_pairs={{6,0},{7,1},{0,2},{1,3},{2,4},{3,5},{4,6},{5,7},{22,16},{23,17},{1... | collective-permute-start | bytes 6152 | tf_op jit(solution)/shard_map/ppermute | solution.py:31
  119.4 6.4 %collective-permute-start.8 = (f32[4,128]{0,1:T(8,128)S(1)}, f32[4,128]{0,1:T(8,128)S(1)}, u32[]{:S(2)}, u32[]{:S(2)}) collective-permute-start(f32[4,128]{0,1:T(8,128)S(1)} %broadcast_in_dim.9), channel_id=1, source_target_pairs={{4,0},{5,1},{6,2},{7,3},{0,4},{1,5},{2,6},{3,7},{20,16},{21,17},{2... | collective-permute-start | bytes 6152 | tf_op jit(solution)/shard_map/ppermute | solution.py:31
  125.9 7.5 %collective-permute-start.13 = (f32[4,128]{0,1:T(8,128)S(1)}, f32[4,128]{0,1:T(8,128)S(1)}, u32[]{:S(2)}, u32[]{:S(2)}) collective-permute-start(f32[4,128]{0,1:T(8,128)S(1)} %broadcast_in_dim.10), channel_id=1, source_target_pairs={{8,0},{9,1},{10,2},{11,3},{12,4},{13,5},{14,6},{15,7},{24,16},{25,... | collective-permute-start | bytes 6152 | tf_op jit(solution)/shard_map/ppermute | solution.py:31
  128.2 7.0 %collective-permute-start.11 = (f32[4,128]{0,1:T(8,128)S(1)}, f32[4,128]{0,1:T(8,128)S(1)}, u32[]{:S(2)}, u32[]{:S(2)}) collective-permute-start(f32[4,128]{0,1:T(8,128)S(1)} %broadcast_in_dim.10), channel_id=1, source_target_pairs={{112,0},{113,1},{114,2},{115,3},{116,4},{117,5},{118,6},{119,7},{8... | collective-permute-start | bytes 6152 | tf_op jit(solution)/shard_map/ppermute | solution.py:31
  133.2 7.6 %collective-permute-start.12 = (f32[4,128]{0,1:T(8,128)S(1)}, f32[4,128]{0,1:T(8,128)S(1)}, u32[]{:S(2)}, u32[]{:S(2)}) collective-permute-start(f32[4,128]{0,1:T(8,128)S(1)} %broadcast_in_dim.10), channel_id=1, source_target_pairs={{120,0},{121,1},{122,2},{123,3},{124,4},{125,5},{126,6},{127,7},{0... | collective-permute-start | bytes 6152 | tf_op jit(solution)/shard_map/ppermute | solution.py:31
  141.5 8.3 %collective-permute-start.14 = (f32[6,128]{0,1:T(8,128)}, f32[6,128]{0,1:T(8,128)S(1)}, u32[]{:S(2)}, u32[]{:S(2)}) collective-permute-start(f32[6,128]{0,1:T(8,128)} %broadcast_in_dim.11), channel_id=1, source_target_pairs={{0,64},{1,65},{2,66},{3,67},{4,68},{5,69},{6,70},{7,71},{16,80},{1... | collective-permute-start | bytes 9224 | tf_op jit(solution)/shard_map/ppermute | solution.py:31
  143.9 7.5 %collective-permute-start.15 = (f32[6,128]{0,1:T(8,128)}, f32[6,128]{0,1:T(8,128)S(1)}, u32[]{:S(2)}, u32[]{:S(2)}) collective-permute-start(f32[6,128]{0,1:T(8,128)} %broadcast_in_dim.11), channel_id=1, source_target_pairs={{0,32},{1,33},{2,34},{3,35},{4,36},{5,37},{6,38},{7,39},{16,48},{1... | collective-permute-start | bytes 9224 | tf_op jit(solution)/shard_map/ppermute | solution.py:31
  147.2 18.7 %collective-permute-start.21 = (f16[256,1152]{1,0:T(8,128)(2,1)}, f16[256,1152]{1,0:T(8,128)(2,1)S(1)}, u32[]{:S(2)}, u32[]{:S(2)}) collective-permute-start(f16[256,1152]{1,0:T(8,128)(2,1)} %get-tuple-element.17), channel_id=1, source_target_pairs={{2,0},{3,1},{4,2},{5,3},{6,4},{7,5},{0,6},{1,7},{18,16},{19,17},{2... | collective-permute-start | bytes 1769480 | tf_op jit(solution)/shard_map/ppermute | solution.py:31
  149.8 25.5 %collective-permute-start.22 = (f16[256,1152]{1,0:T(8,128)(2,1)}, f16[256,1152]{1,0:T(8,128)(2,1)S(1)}, u32[]{:S(2)}, u32[]{:S(2)}) collective-permute-start(f16[256,1152]{1,0:T(8,128)(2,1)} %get-tuple-element.19), channel_id=1, source_target_pairs={{6,0},{7,1},{0,2},{1,3},{2,4},{3,5},{4,6},{5,7},{22,16},{23,17},{1... | collective-permute-start | bytes 1769480 | tf_op jit(solution)/shard_map/ppermute | solution.py:31
  149.8 25.4 %collective-permute-start.23 = (f16[256,1152]{1,0:T(8,128)(2,1)}, f16[256,1152]{1,0:T(8,128)(2,1)}, u32[]{:S(2)}, u32[]{:S(2)}) collective-permute-start(f16[256,1152]{1,0:T(8,128)(2,1)} %get-tuple-element.18), channel_id=1, source_target_pairs={{4,0},{5,1},{6,2},{7,3},{0,4},{1,5},{2,6},{3,7},{20,16},{21,17},{2... | collective-permute-start | bytes 1769480 | tf_op jit(solution)/shard_map/ppermute | solution.py:31
  151.4 11.1 %collective-permute-start.16 = (f32[6,128]{0,1:T(8,128)}, f32[6,128]{0,1:T(8,128)}, u32[]{:S(2)}, u32[]{:S(2)}) collective-permute-start(f32[6,128]{0,1:T(8,128)} %broadcast_in_dim.11), channel_id=1, source_target_pairs={{0,96},{1,97},{2,98},{3,99},{4,100},{5,101},{6,102},{7,103},{16,11... | collective-permute-start | bytes 9224 | tf_op jit(solution)/shard_map/ppermute | solution.py:31
  183.9 17.4 %collective-permute-start.18 = (f16[256,1152]{1,0:T(8,128)(2,1)S(1)}, f16[256,1152]{1,0:T(8,128)(2,1)S(1)}, u32[]{:S(2)}, u32[]{:S(2)}) collective-permute-start(f16[256,1152]{1,0:T(8,128)(2,1)S(1)} %get-tuple-element.20), channel_id=1, source_target_pairs={{8,0},{9,1},{10,2},{11,3},{12,4},{13,5},{14,6},{15,7},{24,16},{25,... | collective-permute-start | bytes 1769480 | tf_op jit(solution)/shard_map/ppermute | solution.py:31
  184.0 31.4 %collective-permute-start.19 = (f16[256,1152]{1,0:T(8,128)(2,1)S(1)}, f16[256,1152]{1,0:T(8,128)(2,1)S(1)}, u32[]{:S(2)}, u32[]{:S(2)}) collective-permute-start(f16[256,1152]{1,0:T(8,128)(2,1)S(1)} %get-tuple-element.22), channel_id=1, source_target_pairs={{112,0},{113,1},{114,2},{115,3},{116,4},{117,5},{118,6},{119,7},{8... | collective-permute-start | bytes 1769480 | tf_op jit(solution)/shard_map/ppermute | solution.py:31
  184.8 30.6 %collective-permute-start.20 = (f16[256,1152]{1,0:T(8,128)(2,1)S(1)}, f16[256,1152]{1,0:T(8,128)(2,1)S(1)}, u32[]{:S(2)}, u32[]{:S(2)}) collective-permute-start(f16[256,1152]{1,0:T(8,128)(2,1)S(1)} %get-tuple-element.21), channel_id=1, source_target_pairs={{120,0},{121,1},{122,2},{123,3},{124,4},{125,5},{126,6},{127,7},{0... | collective-permute-start | bytes 1769480 | tf_op jit(solution)/shard_map/ppermute | solution.py:31
  (12 other events, 189.4 us)

commit v2 on v0

v2 whole, which is shorter than its diff:
```python
import functools

import jax
import jax.numpy as jnp
from jax import lax
from jax.experimental import pallas as pl
from jax.experimental.pallas import tpu as pltpu
from jax.sharding import PartitionSpec as P

AXES = ("blk", "group")
EPS = 1e-06
LOG2E = 1.4426950408889634
LN2 = 0.6931471805599453
ROWS = 256
BLOCK = 272
CHUNK = 16
LANES = 128
VMEM_LIMIT = 44 * 1024 * 1024


def place_index(z, y, x, core):
    z, y, x, core = z % 4, y % 4, x % 4, core % 2
    return (z * 2 + y % 2) * 16 + (y // 2) * 8 + x * 2 + core


def places():
    return [(z, y, x, c) for z in range(4) for y in range(4) for x in range(4) for c in range(2)]


def send(value, moved, back=False):
    pairs = [(place_index(*place), place_index(*moved(*place))) for place in places()]
    if back:
        pairs = [(target, source) for source, target in pairs]
    return lax.ppermute(value, AXES, pairs)


def other_core(z, y, x, c):
    return z, y, x, 1 - c


def x_up(z, y, x, c):
    return z, y, x + 1, c


def x_down(z, y, x, c):
    return z, y, x - 1, c


def x_far(z, y, x, c):
    return z, y, x + 2, c


def y_far(z, y, x, c):
    return z, y + 2, x, c


def before_up(z, y, x, c):
    return (z, y + 1, x, c) if y % 2 else (z - 1, y + 1, x, c)


def before_down(z, y, x, c):
    return (z, y - 1, x, c) if y % 2 else (z - 1, y - 1, x, c)


TEXT_MOVES = (x_up, x_down, x_far)
IMAGE_MOVES = (y_far, before_up, before_down)
FAR_MOVES = (
    lambda z, y, x, c: (z, y ^ 1, x, c),
    lambda z, y, x, c: (z, y ^ 2, x, c),
    lambda z, y, x, c: (z ^ 1, y, x, c),
    lambda z, y, x, c: (z ^ 2, y, x, c),
)
NEAR_MOVES = (
    lambda z, y, x, c: (z, y, x ^ 1, c),
    lambda z, y, x, c: (z, y, x ^ 2, c),
    other_core,
)


def halves_kernel(image_ref, text_ref, image_half_ref, text_half_ref):
    for ref, half_ref in ((image_ref, image_half_ref), (text_ref, text_half_ref)):
        rows = ref[...]
        length = jnp.sqrt(jnp.sum(rows * rows, axis=1, keepdims=True) + EPS)
        half_ref[...] = (rows / length).astype(jnp.bfloat16)


def halves(image_embeds, text_embeds):
    shape = jax.ShapeDtypeStruct(image_embeds.shape, jnp.bfloat16)
    return pl.pallas_call(
        halves_kernel,
        out_shape=(shape, shape),
        name="halves",
    )(image_embeds, text_embeds)


def log1p(value):
    small = value * (1.0 - value * (0.5 - value * (1.0 / 3.0)))
    return jnp.where(value < 1e-3, small, jnp.log(1.0 + value))


def pair_terms(dots_ref, weights_ref, scale, shift, sums_ref, first_step):
    rows, cols = dots_ref.shape
    offset = jnp.where(first_step, 0, -2 * rows)
    for first_col in range(0, cols, LANES):
        relu = weight_sum = dot_sum = product = jnp.zeros((8, LANES), jnp.float32)
        for first_row in range(0, rows, CHUNK):
            place = (slice(first_row, first_row + CHUNK), slice(first_col, first_col + LANES))
            dots = dots_ref[place]
            logits = dots * scale + shift
            decay = jnp.exp2(jnp.minimum(logits, -logits))
            above = 1.0 + decay
            share = pl.reciprocal(above, approx=True)
            share = share * (2.0 - above * share)
            marked = first_row < ROWS and first_col <= first_row < first_col + LANES
            if marked:
                row = lax.broadcasted_iota(jnp.int32, (CHUNK, LANES), 0) + first_row
                col = lax.broadcasted_iota(jnp.int32, (CHUNK, LANES), 1) + first_col
                same = row - col == offset
                logits = jnp.where(same, -logits, logits)
            weights = jnp.where(logits >= 0, share, decay * share)
            if marked:
                weights = jnp.where(same, -weights, weights)
            weights_ref[place] = weights.astype(jnp.bfloat16)
            positive = jnp.maximum(logits, 0.0)
            weighted = weights * dots
            for first in range(0, CHUNK, 8):
                part = slice(first, first + 8)
                relu = relu + positive[part]
                weight_sum = weight_sum + weights[part]
                dot_sum = dot_sum + weighted[part]
                product = product * above[part] + decay[part]
        sums_ref[0] += relu * LN2 + log1p(product)
        sums_ref[1] += weight_sum
        sums_ref[2] += dot_sum


def largest(value):
    return fold_max(jnp.max(jnp.abs(value).reshape(value.shape[0] // 8, 8, value.shape[1]), axis=0))


def fold_max(value):
    total = value[:, 0:128]
    for first in range(128, value.shape[1], 128):
        total = jnp.maximum(total, value[:, first : first + 128])
    return total


def power_of(limit):
    return jnp.floor(jnp.log2(jnp.maximum(limit, 1e-30))) + 1.0


def pairs_kernel(count, earlier, last, *refs):
    refs = list(refs)
    take = lambda number: [refs.pop(0) for _ in range(number)]
    (scalars_ref,) = take(1)
    text_refs, mine_refs, other_refs = take(4), take(count), take(count)
    prior_text_ref, prior_sums_ref = take(2) if earlier else (None, None)
    mine_acc_ref, other_acc_ref = take(2)
    back_refs = take(4) if last else None
    text_acc_ref, sums_ref = take(2)
    text_ref, images_ref, dots_ref, weights_ref, limit_ref = refs
    step = pl.program_id(0)
    scale, shift = scalars_ref[0], scalars_ref[1]
    width = text_ref.shape[1]

    @pl.when(step == 0)
    def _():
        sums_ref[...] = prior_sums_ref[...] if earlier else jnp.zeros_like(sums_ref)
        limit_ref[...] = jnp.zeros_like(limit_ref)
        for place, ref in enumerate(text_refs):
            text_ref[place * ROWS : (place + 1) * ROWS, :] = ref[...]

    for place in range(count):

        @pl.when(step == place)
        def _():
            images_ref[:ROWS, :] = mine_refs[place][...]
            images_ref[ROWS:, :] = other_refs[place][...]

    dots_ref[...] = lax.dot_general(
        images_ref[...], text_ref[...], (((1,), (1,)), ((), ())), preferred_element_type=jnp.float32
    )
    pair_terms(dots_ref, weights_ref, scale, shift, sums_ref, step == 0 if not earlier else step < 0)
    acc = jnp.dot(weights_ref[...], text_ref[...], preferred_element_type=jnp.float32)
    limit_ref[...] = jnp.maximum(limit_ref[...], largest(acc))
    mine_acc_ref[:ROWS, :] = acc[:ROWS]
    other_acc_ref[:ROWS, :] = acc[ROWS:]
    row = lax.broadcasted_iota(jnp.int32, (8, width), 0)
    sums = jnp.zeros((8, width), jnp.float32)
    for place in range(3):
        sums = jnp.where(row == place, jnp.sum(sums_ref[place]), sums)
    power = power_of(jnp.full((8, width), jnp.max(limit_ref[...])))
    for ref in (mine_acc_ref, other_acc_ref):
        ref[ROWS : ROWS + 8, :] = sums
        ref[ROWS + 8 :, :] = power
    back = lax.dot_general(
        weights_ref[...], images_ref[...], (((0,), (0,)), ((), ())), preferred_element_type=jnp.float32
    )
    if earlier:
        text_acc_ref[...] = prior_text_ref[...] + back
    else:

        @pl.when(step == 0)
        def _():
            text_acc_ref[...] = back

        @pl.when(step != 0)
        def _():
            text_acc_ref[...] += back

    if last:
        back_refs[0][...] = text_acc_ref[:ROWS, :]
        power = power_of(jnp.full((8, width), jnp.max(largest(text_acc_ref[ROWS:, :])))) - 10.0
        factor = jnp.exp2(-power)[:1]
        for place, ref in enumerate(back_refs[1:]):
            ref[:ROWS, :] = text_acc_ref[(place + 1) * ROWS : (place + 2) * ROWS, :] * factor
            ref[ROWS:, :] = jnp.concatenate([power, power], axis=0)


def pairs(scalars, texts, mine, other, prior=None):
    width = mine[0].shape[1]
    count = len(mine)
    last = prior is not None
    rows = 4 * ROWS
    unit = pl.BlockSpec((ROWS, width), lambda k: (0, 0))
    block = pl.BlockSpec((BLOCK, width), lambda k: (0, 0))
    each = pl.BlockSpec((BLOCK, width), lambda k: (k, 0))
    whole = pl.BlockSpec((rows, width), lambda k: (0, 0))
    sums = pl.BlockSpec((3, 8, 128), lambda k: (0, 0, 0))

    def shape(*dims):
        return jax.ShapeDtypeStruct(dims, jnp.float32)

    in_specs = [pl.BlockSpec(memory_space=pltpu.SMEM)] + [unit] * (4 + 2 * count)
    operands = [scalars, *texts, *mine, *other]
    out_specs = [each, each]
    out_shape = [shape(count * BLOCK, width)] * 2
    scratch = []
    if last:
        in_specs += [whole, sums]
        operands += prior
        out_specs += [unit, block, block, block]
        out_shape += [shape(ROWS, width)] + [shape(BLOCK, width)] * 3
        scratch += [pltpu.VMEM((rows, width), jnp.float32), pltpu.VMEM((3, 8, 128), jnp.float32)]
    else:
        out_specs += [whole, sums]
        out_shape += [shape(rows, width), shape(3, 8, 128)]
    return pl.pallas_call(
        functools.partial(pairs_kernel, count, last, last),
        grid=(count,),
        in_specs=in_specs,
        out_specs=out_specs,
        out_shape=out_shape,
        scratch_shapes=scratch
        + [
            pltpu.VMEM((rows, width), jnp.bfloat16),
            pltpu.VMEM((2 * ROWS, width), jnp.bfloat16),
            pltpu.VMEM((2 * ROWS, rows), jnp.float32),
            pltpu.VMEM((2 * ROWS, rows), jnp.bfloat16),
            pltpu.VMEM((8, 128), jnp.float32),
        ],
        compiler_params=pltpu.CompilerParams(vmem_limit_bytes=VMEM_LIMIT),
        cost_estimate=pl.CostEstimate(
            flops=(20 if last else 6) * rows * 2 * count * ROWS * width, bytes_accessed=1 << 20, transcendentals=3 * rows * 2 * count * ROWS
        ),
        name="pairs",
    )(*operands)


def tangent_kernel(scalars_ref, embeds_ref, accum_ref, out_ref):
    embeds = embeds_ref[...]
    accum = accum_ref[...]
    length = jnp.sqrt(jnp.sum(embeds * embeds, axis=1, keepdims=True) + EPS)
    inverse = 1.0 / length
    unit = embeds * inverse
    along = jnp.sum(unit * accum, axis=1, keepdims=True)
    out_ref[...] = (accum - unit * along) * (scalars_ref[2] * inverse)


def tangent_part(scalars, embeds, accum):
    return pl.pallas_call(
        tangent_kernel,
        in_specs=[pl.BlockSpec(memory_space=pltpu.SMEM)] + [pl.BlockSpec(memory_space=pltpu.VMEM)] * 2,
        out_shape=jax.ShapeDtypeStruct(embeds.shape, jnp.float32),
        name="tangent",
    )(scalars, embeds, accum)


def groups(rows):
    return rows.reshape(rows.shape[0] // 8, 8, rows.shape[1])


def packed(mine, other):
    mine, other = groups(mine), groups(other)
    power = jnp.maximum(mine[-1:], other[-1:]) - 9.0
    group = lax.broadcasted_iota(jnp.int32, mine.shape, 0)
    rows = jnp.where(group < ROWS // 8, (mine + other) * jnp.exp2(-power), power)
    return rows.astype(jnp.float16).reshape(BLOCK, -1)


def unpacked(rows):
    rows = groups(rows).astype(jnp.float32)
    return (rows[: ROWS // 8] * jnp.exp2(rows[-1:])).reshape(ROWS, -1)


def after(value, *others):
    return lax.optimization_barrier((value, *others))[0]


def on_device(image_embeds, text_embeds, log_scale, bias):
    image_half, text_half = halves(image_embeds, text_embeds)
    scale_value = jnp.exp(log_scale[0])
    scalars = jnp.stack([scale_value * LOG2E, bias[0] * LOG2E, scale_value])
    above = send(image_half, before_up)
    below = send(image_half, before_down)
    texts = [text_half] + [send(text_half, move) for move in TEXT_MOVES]
    beside = send(image_half, other_core)
    opposite = send(image_half, y_far)
    first = [image_half, above, below]
    first_other = [beside, send(above, other_core), send(below, other_core)]
    second_other = send(opposite, other_core)

    mine, other, text_acc, sums = pairs(scalars, texts, first, first_other)
    from_core = send(other, other_core)
    second, other, back0, back1, back2, back3 = pairs(
        scalars, texts, [opposite], [second_other], [text_acc, sums]
    )
    second_from_core = send(other, other_core)

    blocks = [slice(place * BLOCK, (place + 1) * BLOCK) for place in range(3)]
    packs = [
        packed(second, second_from_core),
        packed(mine[blocks[1]], from_core[blocks[1]]),
        packed(mine[blocks[2]], from_core[blocks[2]]),
    ]
    totals, *packs = lax.optimization_barrier((second[ROWS : ROWS + 8, :128], *packs))
    opposite, above, below = [send(rows, move, back=True) for rows, move in zip(packs, IMAGE_MOVES)]
    for move in NEAR_MOVES:
        totals = totals + send(totals, move)
    back1, back2, back3 = after((back1, back2, back3), totals)
    up = send(back1.astype(jnp.float16), x_up, back=True)
    down = send(back2.astype(jnp.float16), x_down, back=True)
    far = send(back3.astype(jnp.float16), x_far, back=True)
    totals = after(totals, above, below, opposite)
    for move in FAR_MOVES:
        totals = totals + send(totals, move)
    totals = totals[:3, 0] / (ROWS * lax.axis_size("blk") * lax.axis_size("group"))

    text_sum = back0
    for rows in (up, down, far):
        text_sum = text_sum + unpacked(rows)
    image_sum = mine[:ROWS] + from_core[:ROWS]
    for rows in (opposite, above, below):
        image_sum = image_sum + unpacked(rows)
    grad_text = tangent_part(scalars, text_embeds, text_sum)
    grad_image = tangent_part(scalars, image_embeds, image_sum)
    return (totals[0:1], grad_image, grad_text, scale_value * totals[2:3], totals[1:2])


def solution(mesh):
    return jax.shard_map(
        on_device,
        mesh=mesh,
        in_specs=(P(AXES, None), P(AXES, None), P(), P()),
        out_specs=(P(), P(AXES, None), P(AXES, None), P(), P()),
        check_vma=False,
    )
```

time: 320 us -> 157 us (0.49)
  blocking collectives: 100 us -> 0 us
  waiting for transfers between devices: 120 us -> 61.2 us
  matrix products: 53.6 us -> 0 us
  Pallas kernels: 0 us -> 40 us
  starting transfers between devices: 9.34 us -> 32 us
  between operations: 24.7 us -> 3.98 us
  local copies, waits for them, and re-layouts: 1.99 us -> 6.77 us
    psum x1 -> x0, blocking collectives: 100 us -> none  [on_device(): totals = lax.psum((loss_sum, weight_sum, dot_sum), ('blk', 'group'))]
    all_gather x1 -> x0, waiting for transfers between devices: 73.6 us -> none  [on_device(): text_group = lax.all_gather(text_half, 'group', axis=0, tiled=True)]
    dot_general x6 -> x0, matrix products: 53.6 us -> none  [the longest x2 20.9 us: back_rows(): lax.dot_general(weights_half, rows_half, (((0,), (0,)), ((), ())), prefer...]
    pallas_call x0 -> x5, Pallas kernels: none -> 40 us  [the longest x2 31 us: pairs(): pl.pallas_call(functools.partial(pairs_kernel, count, last, last), grid=(...]
    ppermute x3 -> x25, waiting for transfers between devices: 25.6 us -> 61.2 us  [send(): return lax.ppermute(value, AXES, pairs)]
    ppermute x3 -> x25, starting transfers between devices: 9.26 us -> 32 us  [send(): return lax.ppermute(value, AXES, pairs)]
    reduce_scatter x1 -> x0, waiting for transfers between devices: 20.3 us -> none  [on_device(): lax.psum_scatter(text_acc, 'group', scatter_dimension=0, tiled=True)]
    add x1 -> x9, other arithmetic: 0.01 us -> 4.47 us  [the longest x1 3.07 us: on_device(): image_sum = image_sum + unpacked(rows)]
  transfers between devices with their start and end apart: 5 -> 25, of which waited for: 3 -> 11; matrix products, arithmetic and copies ran while one was open for 12% -> 5% of each run, Pallas kernels for 0% -> 24%
where the time goes in v2:
time: 157 us; the launch traced here: 156 us
  waiting for transfers between devices  61.2 us (39%)
  Pallas kernels  40 us (25%)
  starting transfers between devices  32 us (20%)
  other arithmetic  12.4 us (8%)
  local copies, waits for them, and re-layouts  6.77 us (4%)
  between operations  3.98 us (3%)
    ppermute x25, waiting for transfers between devices, send(): return lax.ppermute(value, AXES, pairs)  61.2 us
    ppermute x25, starting transfers between devices, send(): return lax.ppermute(value, AXES, pairs)  32 us
    pallas_call x2, Pallas kernels, pairs(): pl.pallas_call(functools.partial(pairs_kernel, count, last, last), grid=(...  31 us
    pallas_call x2, Pallas kernels, tangent_part(): pl.pallas_call(tangent_kernel, in_specs=[pl.BlockSpec(memory_space=pltpu....  6.1 us
    unnamed x18, local copies, waits for them, and re-layouts  6.07 us
    convert_element_type x1, other arithmetic, packed(): return rows.astype(jnp.float16).reshape(BLOCK, -1)  3.56 us
  transfers between devices with their start and end apart: 25, of which 11 were waited for; matrix products, arithmetic and copies ran while one was open for 5% of the time, Pallas kernels for 24%

profile of v2, /device:TPU:0, one launch (start us, length us, event | category | flops | bytes accessed | tf_op | source)
XLA Modules:
  0.0 156.4 jit_solution(7713662484610294073)
XLA Ops:
  0.6 2.9 %halves.1 = (bf16[256,1152]{1,0:T(8,128)(2,1)}, bf16[256,1152]{1,0:T(8,128)(2,1)}) custom-call(f32[256,1152]{1,0:T(8,128)} %embeds_ref.2, f32[256,1152]{1,0:T(8,128)} %embeds_ref.3), custom_call_target="tpu_custom_call" | custom-call | tf_op jit(solution)/shard_map/halves/pallas_call | solution.py:89
  3.5 5.1 %collective-permute-start.5 = (bf16[256,1152]{1,0:T(8,128)(2,1)}, bf16[256,1152]{1,0:T(8,128)(2,1)S(1)}, u32[]{:S(2)}, u32[]{:S(2)}) collective-permute-start(bf16[256,1152]{1,0:T(8,128)(2,1)} %get-tuple-element.26.refs_5_), channel_id=1, source_target_pairs={{0,112},{1,113},{2,114},{3,115},{4,116},{5,117},{6,118},{7,119},{1... | collective-permute-start | bytes 1769480 | tf_op jit(solution)/shard_map/ppermute | solution.py:34
  11.8 1.7 %collective-permute-start.1 = (bf16[256,1152]{1,0:T(8,128)(2,1)}, bf16[256,1152]{1,0:T(8,128)(2,1)S(1)}, u32[]{:S(2)}, u32[]{:S(2)}) collective-permute-start(bf16[256,1152]{1,0:T(8,128)(2,1)} %get-tuple-element.25.refs_1_), channel_id=1, source_target_pairs={{0,6},{1,7},{2,0},{3,1},{4,2},{5,3},{6,4},{7,5},{16,22},{17,23},{1... | collective-permute-start | bytes 1769480 | tf_op jit(solution)/shard_map/ppermute | solution.py:34
  13.6 1.8 %collective-permute-start.2 = (bf16[256,1152]{1,0:T(8,128)(2,1)}, bf16[256,1152]{1,0:T(8,128)(2,1)S(1)}, u32[]{:S(2)}, u32[]{:S(2)}) collective-permute-start(bf16[256,1152]{1,0:T(8,128)(2,1)} %get-tuple-element.25.refs_1_), channel_id=1, source_target_pairs={{0,4},{1,5},{2,6},{3,7},{4,0},{5,1},{6,2},{7,3},{16,20},{17,21},{1... | collective-permute-start | bytes 1769480 | tf_op jit(solution)/shard_map/ppermute | solution.py:34
  15.4 16.5 %collective-permute-done.5.refs_6_ = bf16[256,1152]{1,0:T(8,128)(2,1)S(1)} collective-permute-done((bf16[256,1152]{1,0:T(8,128)(2,1)}, bf16[256,1152]{1,0:T(8,128)(2,1)S(1)}, u32[]{:S(2)}, u32[]{:S(2)}) %collective-permute-start.5) | collective-permute-done | bytes 589856 | tf_op jit(solution)/shard_map/ppermute | solution.py:34
  33.9 4.4 %collective-permute-done.1.refs_3_ = bf16[256,1152]{1,0:T(8,128)(2,1)S(1)} collective-permute-done((bf16[256,1152]{1,0:T(8,128)(2,1)}, bf16[256,1152]{1,0:T(8,128)(2,1)S(1)}, u32[]{:S(2)}, u32[]{:S(2)}) %collective-permute-start.1) | collective-permute-done | bytes 589856 | tf_op jit(solution)/shard_map/ppermute | solution.py:34
  38.3 1.9 %collective-permute-start.3 = (bf16[256,1152]{1,0:T(8,128)(2,1)}, bf16[256,1152]{1,0:T(8,128)(2,1)S(1)}, u32[]{:S(2)}, u32[]{:S(2)}) collective-permute-start(bf16[256,1152]{1,0:T(8,128)(2,1)} %get-tuple-element.26.refs_5_), channel_id=1, source_target_pairs={{0,8},{1,9},{2,10},{3,11},{4,12},{5,13},{6,14},{7,15},{16,24},{17,... | collective-permute-start | bytes 1769480 | tf_op jit(solution)/shard_map/ppermute | solution.py:34
  42.4 21.4 %pairs.2 = (f32[816,1152]{1,0:T(8,128)S(1)}, f32[816,1152]{1,0:T(8,128)}, f32[1024,1152]{1,0:T(8,128)}, f32[3,8,128]{2,1,0:T(8,128)S(1)}) custom-call(f32[3]{0:T(128)S(1)} %pad_maximum_fusion.refs_0_.scalars_ref, bf16[256,1152]{1,0:T(8,128)(2,1)S(1)} %copy-done.6, bf16[256,1152]{1,0:T(8,128)(2,1)S(1)} %collective-permute-done.refs_2_, ...), custom_call_target="tpu_custom_call" | custom-call | flops 10871635968 | bytes 1048576 | tf_op jit(solution)/shard_map/pairs/pallas_call | solution.py:248
  63.9 1.8 %copy-done = f32[816,1152]{1,0:T(8,128)} copy-done((f32[816,1152]{1,0:T(8,128)}, f32[816,1152]{1,0:T(8,128)S(1)}, u32[]{:S(2)}) %copy-start) | copy-done | bytes 3760152
  66.2 6.5 %collective-permute-done.4.refs_6_ = bf16[256,1152]{1,0:T(8,128)(2,1)S(1)} collective-permute-done((bf16[256,1152]{1,0:T(8,128)(2,1)S(1)}, bf16[256,1152]{1,0:T(8,128)(2,1)S(1)}, u32[]{:S(2)}, u32[]{:S(2)}) %collective-permute-start.4) | collective-permute-done | bytes 589856 | tf_op jit(solution)/shard_map/ppermute | solution.py:34
  72.7 9.6 %pairs.3 = (f32[272,1152]{1,0:T(8,128)S(1)}, f32[272,1152]{1,0:T(8,128)}, f32[256,1152]{1,0:T(8,128)S(1)}, f32[272,1152]{1,0:T(8,128)S(1)}, f32[272,1152]{1,0:T(8,128)S(1)}, /*index=5*/f32[272,1152]{1,0:T(8,128)}) custom-call(f32[3]{0:T(128)S(1)} %pad_maximum_fusion.refs_0_.scalars_ref, bf16[256,1152]{1,0:T(8,128)(2,1)S(1)} %copy-done.6, ...), custom_call_target="tpu_custom_call" | custom-call | flops 12079595520 | bytes 1048576 | tf_op jit(solution)/shard_map/pairs/pallas_call | solution.py:248
  85.0 2.7 %collective-permute-done.10 = f32[272,1152]{1,0:T(8,128)} collective-permute-done((f32[272,1152]{1,0:T(8,128)}, f32[272,1152]{1,0:T(8,128)}, u32[]{:S(2)}, u32[]{:S(2)}) %collective-permute-start.10) | collective-permute-done | bytes 1253408 | tf_op jit(solution)/shard_map/ppermute | solution.py:34
  89.4 3.6 %fusion.2 = (f16[272,1152]{1,0:T(8,128)(2,1)S(1)}, f16[272,1152]{1,0:T(8,128)(2,1)S(1)}, f16[272,1152]{1,0:T(8,128)(2,1)S(1)}) fusion(f32[816,1152]{1,0:T(8,128)} %collective-permute-done.11, f32[816,1152]{1,0:T(8,128)} %copy-done, f32[8,1152]{1,0:T(8,128)S(1)} %get-tuple-element.46, f32[8,1152]{1,0:T(8,128)S(1)} %get-tuple-element.45, ...), kind=kLoop, calls=%fused_computation.3 | loop fusion | flops 3760128 | bytes 9621776 | tf_op jit(solution)/shard_map/convert_element_type | solution.py:298
  95.6 2.5 %collective-permute-done.12 = f32[8,128]{1,0:T(8,128)S(1)} collective-permute-done((f32[8,128]{1,0:T(8,128)S(1)}, f32[8,128]{1,0:T(8,128)S(1)}, u32[]{:S(2)}, u32[]{:S(2)}) %collective-permute-start.12) | collective-permute-done | bytes 4128 | tf_op jit(solution)/shard_map/ppermute | solution.py:34
  98.1 2.7 %collective-permute-start.13 = (f32[8,128]{1,0:T(8,128)S(1)}, f32[8,128]{1,0:T(8,128)S(1)}, u32[]{:S(2)}, u32[]{:S(2)}) collective-permute-start(f32[8,128]{1,0:T(8,128)S(1)} %add.63), channel_id=1, source_target_pairs={{0,4},{1,5},{2,6},{3,7},{4,0},{5,1},{6,2},{7,3},{16,20},{17,21},{1... | collective-permute-start | bytes 12296 | tf_op jit(solution)/shard_map/ppermute | solution.py:34
  100.8 2.4 %collective-permute-done.13 = f32[8,128]{1,0:T(8,128)S(1)} collective-permute-done((f32[8,128]{1,0:T(8,128)S(1)}, f32[8,128]{1,0:T(8,128)S(1)}, u32[]{:S(2)}, u32[]{:S(2)}) %collective-permute-start.13) | collective-permute-done | bytes 4128 | tf_op jit(solution)/shard_map/ppermute | solution.py:34
  105.5 3.0 %collective-permute-start.24 = (f16[272,1152]{1,0:T(8,128)(2,1)}, f16[272,1152]{1,0:T(8,128)(2,1)}, u32[]{:S(2)}, u32[]{:S(2)}) collective-permute-start(f16[272,1152]{1,0:T(8,128)(2,1)} %convert_element_type.55), channel_id=1, source_target_pairs={{4,0},{5,1},{6,2},{7,3},{0,4},{1,5},{2,6},{3,7},{20,16},{21,17},{2... | collective-permute-start | bytes 1880072 | tf_op jit(solution)/shard_map/ppermute | solution.py:34
  110.1 20.2 %collective-permute-done.16 = f16[272,1152]{1,0:T(8,128)(2,1)S(1)} collective-permute-done((f16[272,1152]{1,0:T(8,128)(2,1)S(1)}, f16[272,1152]{1,0:T(8,128)(2,1)S(1)}, u32[]{:S(2)}, u32[]{:S(2)}) %collective-permute-start.16) | collective-permute-done | bytes 626720 | tf_op jit(solution)/shard_map/ppermute | solution.py:34
  130.3 3.6 %collective-permute-start.22 = (f16[272,1152]{1,0:T(8,128)(2,1)S(1)}, f16[272,1152]{1,0:T(8,128)(2,1)S(1)}, u32[]{:S(2)}, u32[]{:S(2)}) collective-permute-start(f16[272,1152]{1,0:T(8,128)(2,1)S(1)} %convert_element_type.51), channel_id=1, source_target_pairs={{2,0},{3,1},{4,2},{5,3},{6,4},{7,5},{0,6},{1,7},{18,16},{19,17},{2... | collective-permute-start | bytes 1880072 | tf_op jit(solution)/shard_map/ppermute | solution.py:34
  134.3 3.5 %collective-permute-done.18 = f32[8,128]{1,0:T(8,128)S(1)} collective-permute-done((f32[8,128]{1,0:T(8,128)S(1)}, f32[8,128]{1,0:T(8,128)S(1)}, u32[]{:S(2)}, u32[]{:S(2)}) %collective-permute-start.18) | collective-permute-done | bytes 4128 | tf_op jit(solution)/shard_map/ppermute | solution.py:34
  139.2 3.1 %fusion.18.accum_ref = f32[256,1152]{1,0:T(8,128)} fusion(f32[272,1152]{1,0:T(8,128)S(1)} %convert_element_type.50, f32[272,1152]{1,0:T(8,128)S(1)} %convert_element_type.49, f32[272,1152]{1,0:T(8,128)S(1)} %convert_element_type.48, f32[816,1152]{1,0:T(8,128)} %collective-permute-done.11, f32[816,1152]{1,0:T(8,128)} %copy-done, f32[8,1152]{1,0:T(8,128)S(1)} %fusion.28, ...), kind=kLoop, calls=%fused_computation.26 | loop fusion | flops 2064384 | bytes 7188480 | tf_op jit(solution)/shard_map/add | solution.py:354
  142.3 3.0 %tangent.2 = f32[256,1152]{1,0:T(8,128)} custom-call(f32[3]{0:T(128)} %copy-done.5, f32[256,1152]{1,0:T(8,128)} %embeds_ref.2, f32[256,1152]{1,0:T(8,128)} %fusion.18.accum_ref), custom_call_target="tpu_custom_call" | custom-call | tf_op jit(solution)/shard_map/tangent/pallas_call | solution.py:281
  147.1 1.9 %collective-permute-done.20 = f32[8,128]{1,0:T(8,128)S(1)} collective-permute-done((f32[8,128]{1,0:T(8,128)S(1)}, f32[8,128]{1,0:T(8,128)S(1)}, u32[]{:S(2)}, u32[]{:S(2)}) %collective-permute-start.20) | collective-permute-done | bytes 4128 | tf_op jit(solution)/shard_map/ppermute | solution.py:34
  150.8 3.0 %tangent.3 = f32[256,1152]{1,0:T(8,128)} custom-call(f32[3]{0:T(128)} %copy-done.5, f32[256,1152]{1,0:T(8,128)} %embeds_ref.3, f32[256,1152]{1,0:T(8,128)} %fusion.9.accum_ref), custom_call_target="tpu_custom_call" | custom-call | tf_op jit(solution)/shard_map/tangent/pallas_call | solution.py:281
  (83 shorter events, 23.5 us)
Async XLA Ops:
  3.5 28.4 %collective-permute-start.5 = (bf16[256,1152]{1,0:T(8,128)(2,1)}, bf16[256,1152]{1,0:T(8,128)(2,1)S(1)}, u32[]{:S(2)}, u32[]{:S(2)}) collective-permute-start(bf16[256,1152]{1,0:T(8,128)(2,1)} %get-tuple-element.26.refs_5_), channel_id=1, source_target_pairs={{0,112},{1,113},{2,114},{3,115},{4,116},{5,117},{6,118},{7,119},{1... | collective-permute-start | bytes 1769480 | tf_op jit(solution)/shard_map/ppermute | solution.py:34
  8.7 23.2 %collective-permute-start.6 = (bf16[256,1152]{1,0:T(8,128)(2,1)}, bf16[256,1152]{1,0:T(8,128)(2,1)S(1)}, u32[]{:S(2)}, u32[]{:S(2)}) collective-permute-start(bf16[256,1152]{1,0:T(8,128)(2,1)} %get-tuple-element.26.refs_5_), channel_id=1, source_target_pairs={{0,120},{1,121},{2,122},{3,123},{4,124},{5,125},{6,126},{7,127},{1... | collective-permute-start | bytes 1769480 | tf_op jit(solution)/shard_map/ppermute | solution.py:34
  10.3 22.1 %collective-permute-start = (bf16[256,1152]{1,0:T(8,128)(2,1)}, bf16[256,1152]{1,0:T(8,128)(2,1)S(1)}, u32[]{:S(2)}, u32[]{:S(2)}) collective-permute-start(bf16[256,1152]{1,0:T(8,128)(2,1)} %get-tuple-element.25.refs_1_), channel_id=1, source_target_pairs={{0,2},{1,3},{2,4},{3,5},{4,6},{5,7},{6,0},{7,1},{16,18},{17,19},{1... | collective-permute-start | bytes 1769480 | tf_op jit(solution)/shard_map/ppermute | solution.py:34
  11.8 26.5 %collective-permute-start.1 = (bf16[256,1152]{1,0:T(8,128)(2,1)}, bf16[256,1152]{1,0:T(8,128)(2,1)S(1)}, u32[]{:S(2)}, u32[]{:S(2)}) collective-permute-start(bf16[256,1152]{1,0:T(8,128)(2,1)} %get-tuple-element.25.refs_1_), channel_id=1, source_target_pairs={{0,6},{1,7},{2,0},{3,1},{4,2},{5,3},{6,4},{7,5},{16,22},{17,23},{1... | collective-permute-start | bytes 1769480 | tf_op jit(solution)/shard_map/ppermute | solution.py:34
  13.6 26.7 %collective-permute-start.2 = (bf16[256,1152]{1,0:T(8,128)(2,1)}, bf16[256,1152]{1,0:T(8,128)(2,1)S(1)}, u32[]{:S(2)}, u32[]{:S(2)}) collective-permute-start(bf16[256,1152]{1,0:T(8,128)(2,1)} %get-tuple-element.25.refs_1_), channel_id=1, source_target_pairs={{0,4},{1,5},{2,6},{3,7},{4,0},{5,1},{6,2},{7,3},{16,20},{17,21},{1... | collective-permute-start | bytes 1769480 | tf_op jit(solution)/shard_map/ppermute | solution.py:34
  31.9 8.4 %collective-permute-start.7 = (bf16[256,1152]{1,0:T(8,128)(2,1)}, bf16[256,1152]{1,0:T(8,128)(2,1)S(1)}, u32[]{:S(2)}, u32[]{:S(2)}) collective-permute-start(bf16[256,1152]{1,0:T(8,128)(2,1)} %get-tuple-element.26.refs_5_), channel_id=1, source_target_pairs={{0,1},{1,0},{2,3},{3,2},{4,5},{5,4},{6,7},{7,6},{16,17},{17,16},{1... | collective-permute-start | bytes 1769480 | tf_op jit(solution)/shard_map/ppermute | solution.py:34
  31.9 8.4 %collective-permute-start.8 = (bf16[256,1152]{1,0:T(8,128)(2,1)S(1)}, bf16[256,1152]{1,0:T(8,128)(2,1)S(1)}, u32[]{:S(2)}, u32[]{:S(2)}) collective-permute-start(bf16[256,1152]{1,0:T(8,128)(2,1)S(1)} %collective-permute-done.5.refs_6_), channel_id=1, source_target_pairs={{0,1},{1,0},{2,3},{3,2},{4,5},{5,4},{6,7},{7,6},{16,17},{17,16},{1... | collective-permute-start | bytes 1769480 | tf_op jit(solution)/shard_map/ppermute | solution.py:34
  32.4 7.9 %collective-permute-start.9 = (bf16[256,1152]{1,0:T(8,128)(2,1)S(1)}, bf16[256,1152]{1,0:T(8,128)(2,1)S(1)}, u32[]{:S(2)}, u32[]{:S(2)}) collective-permute-start(bf16[256,1152]{1,0:T(8,128)(2,1)S(1)} %collective-permute-done.6.refs_7_), channel_id=1, source_target_pairs={{0,1},{1,0},{2,3},{3,2},{4,5},{5,4},{6,7},{7,6},{16,17},{17,16},{1... | collective-permute-start | bytes 1769480 | tf_op jit(solution)/shard_map/ppermute | solution.py:34
  38.3 27.4 %collective-permute-start.3 = (bf16[256,1152]{1,0:T(8,128)(2,1)}, bf16[256,1152]{1,0:T(8,128)(2,1)S(1)}, u32[]{:S(2)}, u32[]{:S(2)}) collective-permute-start(bf16[256,1152]{1,0:T(8,128)(2,1)} %get-tuple-element.26.refs_5_), channel_id=1, source_target_pairs={{0,8},{1,9},{2,10},{3,11},{4,12},{5,13},{6,14},{7,15},{16,24},{17,... | collective-permute-start | bytes 1769480 | tf_op jit(solution)/shard_map/ppermute | solution.py:34
  65.7 22.8 %collective-permute-start.11 = (f32[816,1152]{1,0:T(8,128)}, f32[816,1152]{1,0:T(8,128)}, u32[]{:S(2)}, u32[]{:S(2)}) collective-permute-start(f32[816,1152]{1,0:T(8,128)} %get-tuple-element.32), channel_id=1, source_target_pairs={{0,1},{1,0},{2,3},{3,2},{4,5},{5,4},{6,7},{7,6},{16,17},{17,16},{1... | collective-permute-start | bytes 11280392 | tf_op jit(solution)/shard_map/ppermute | solution.py:34
  65.7 7.0 %collective-permute-start.4 = (bf16[256,1152]{1,0:T(8,128)(2,1)S(1)}, bf16[256,1152]{1,0:T(8,128)(2,1)S(1)}, u32[]{:S(2)}, u32[]{:S(2)}) collective-permute-start(bf16[256,1152]{1,0:T(8,128)(2,1)S(1)} %collective-permute-done.3.refs_5_), channel_id=1, source_target_pairs={{0,1},{1,0},{2,3},{3,2},{4,5},{5,4},{6,7},{7,6},{16,17},{17,16},{1... | collective-permute-start | bytes 1769480 | tf_op jit(solution)/shard_map/ppermute | solution.py:34
  84.4 3.3 %collective-permute-start.10 = (f32[272,1152]{1,0:T(8,128)}, f32[272,1152]{1,0:T(8,128)}, u32[]{:S(2)}, u32[]{:S(2)}) collective-permute-start(f32[272,1152]{1,0:T(8,128)} %get-tuple-element.30), channel_id=1, source_target_pairs={{0,1},{1,0},{2,3},{3,2},{4,5},{5,4},{6,7},{7,6},{16,17},{17,16},{1... | collective-permute-start | bytes 3760136 | tf_op jit(solution)/shard_map/ppermute | solution.py:34
  92.9 37.4 %collective-permute-start.16 = (f16[272,1152]{1,0:T(8,128)(2,1)S(1)}, f16[272,1152]{1,0:T(8,128)(2,1)S(1)}, u32[]{:S(2)}, u32[]{:S(2)}) collective-permute-start(f16[272,1152]{1,0:T(8,128)(2,1)S(1)} %get-tuple-element.35), channel_id=1, source_target_pairs={{120,0},{121,1},{122,2},{123,3},{124,4},{125,5},{126,6},{127,7},{0... | collective-permute-start | bytes 1880072 | tf_op jit(solution)/shard_map/ppermute | solution.py:34
  93.7 40.3 %collective-permute-start.15 = (f16[272,1152]{1,0:T(8,128)(2,1)S(1)}, f16[272,1152]{1,0:T(8,128)(2,1)S(1)}, u32[]{:S(2)}, u32[]{:S(2)}) collective-permute-start(f16[272,1152]{1,0:T(8,128)(2,1)S(1)} %get-tuple-element.34), channel_id=1, source_target_pairs={{112,0},{113,1},{114,2},{115,3},{116,4},{117,5},{118,6},{119,7},{8... | collective-permute-start | bytes 1880072 | tf_op jit(solution)/shard_map/ppermute | solution.py:34
  94.5 3.6 %collective-permute-start.12 = (f32[8,128]{1,0:T(8,128)S(1)}, f32[8,128]{1,0:T(8,128)S(1)}, u32[]{:S(2)}, u32[]{:S(2)}) collective-permute-start(f32[8,128]{1,0:T(8,128)S(1)} %slice.130), channel_id=1, source_target_pairs={{0,2},{1,3},{2,0},{3,1},{4,6},{5,7},{6,4},{7,5},{16,18},{17,19},{1... | collective-permute-start | bytes 12296 | tf_op jit(solution)/shard_map/ppermute | solution.py:34
  98.1 5.1 %collective-permute-start.13 = (f32[8,128]{1,0:T(8,128)S(1)}, f32[8,128]{1,0:T(8,128)S(1)}, u32[]{:S(2)}, u32[]{:S(2)}) collective-permute-start(f32[8,128]{1,0:T(8,128)S(1)} %add.63), channel_id=1, source_target_pairs={{0,4},{1,5},{2,6},{3,7},{4,0},{5,1},{6,2},{7,3},{16,20},{17,21},{1... | collective-permute-start | bytes 12296 | tf_op jit(solution)/shard_map/ppermute | solution.py:34
  103.2 30.9 %collective-permute-start.17 = (f16[272,1152]{1,0:T(8,128)(2,1)S(1)}, f16[272,1152]{1,0:T(8,128)(2,1)S(1)}, u32[]{:S(2)}, u32[]{:S(2)}) collective-permute-start(f16[272,1152]{1,0:T(8,128)(2,1)S(1)} %get-tuple-element.36), channel_id=1, source_target_pairs={{8,0},{9,1},{10,2},{11,3},{12,4},{13,5},{14,6},{15,7},{24,16},{25,... | collective-permute-start | bytes 1880072 | tf_op jit(solution)/shard_map/ppermute | solution.py:34
  105.5 40.0 %collective-permute-start.24 = (f16[272,1152]{1,0:T(8,128)(2,1)}, f16[272,1152]{1,0:T(8,128)(2,1)}, u32[]{:S(2)}, u32[]{:S(2)}) collective-permute-start(f16[272,1152]{1,0:T(8,128)(2,1)} %convert_element_type.55), channel_id=1, source_target_pairs={{4,0},{5,1},{6,2},{7,3},{0,4},{1,5},{2,6},{3,7},{20,16},{21,17},{2... | collective-permute-start | bytes 1880072 | tf_op jit(solution)/shard_map/ppermute | solution.py:34
  108.6 38.1 %collective-permute-start.23 = (f16[272,1152]{1,0:T(8,128)(2,1)S(1)}, f16[272,1152]{1,0:T(8,128)(2,1)S(1)}, u32[]{:S(2)}, u32[]{:S(2)}) collective-permute-start(f16[272,1152]{1,0:T(8,128)(2,1)S(1)} %convert_element_type.53), channel_id=1, source_target_pairs={{6,0},{7,1},{0,2},{1,3},{2,4},{3,5},{4,6},{5,7},{22,16},{23,17},{1... | collective-permute-start | bytes 1880072 | tf_op jit(solution)/shard_map/ppermute | solution.py:34
  130.3 16.7 %collective-permute-start.22 = (f16[272,1152]{1,0:T(8,128)(2,1)S(1)}, f16[272,1152]{1,0:T(8,128)(2,1)S(1)}, u32[]{:S(2)}, u32[]{:S(2)}) collective-permute-start(f16[272,1152]{1,0:T(8,128)(2,1)S(1)} %convert_element_type.51), channel_id=1, source_target_pairs={{2,0},{3,1},{4,2},{5,3},{6,4},{7,5},{0,6},{1,7},{18,16},{19,17},{2... | collective-permute-start | bytes 1880072 | tf_op jit(solution)/shard_map/ppermute | solution.py:34
  134.1 3.7 %collective-permute-start.18 = (f32[8,128]{1,0:T(8,128)S(1)}, f32[8,128]{1,0:T(8,128)S(1)}, u32[]{:S(2)}, u32[]{:S(2)}) collective-permute-start(f32[8,128]{1,0:T(8,128)S(1)} %add.65), channel_id=1, source_target_pairs={{0,16},{1,17},{2,18},{3,19},{4,20},{5,21},{6,22},{7,23},{16,0},{17... | collective-permute-start | bytes 12296 | tf_op jit(solution)/shard_map/ppermute | solution.py:34
  137.8 7.5 %collective-permute-start.19 = (f32[8,128]{1,0:T(8,128)S(1)}, f32[8,128]{1,0:T(8,128)S(1)}, u32[]{:S(2)}, u32[]{:S(2)}) collective-permute-start(f32[8,128]{1,0:T(8,128)S(1)} %add.66), channel_id=1, source_target_pairs={{0,8},{1,9},{2,10},{3,11},{4,12},{5,13},{6,14},{7,15},{16,24},{17,... | collective-permute-start | bytes 12296 | tf_op jit(solution)/shard_map/ppermute | solution.py:34
  145.3 3.7 %collective-permute-start.20 = (f32[8,128]{1,0:T(8,128)S(1)}, f32[8,128]{1,0:T(8,128)S(1)}, u32[]{:S(2)}, u32[]{:S(2)}) collective-permute-start(f32[8,128]{1,0:T(8,128)S(1)} %add.67), channel_id=1, source_target_pairs={{0,32},{1,33},{2,34},{3,35},{4,36},{5,37},{6,38},{7,39},{16,48},{1... | collective-permute-start | bytes 12296 | tf_op jit(solution)/shard_map/ppermute | solution.py:34
  149.0 5.1 %collective-permute-start.21 = (f32[8,128]{1,0:T(8,128)S(1)}, f32[8,128]{1,0:T(8,128)S(1)}, u32[]{:S(2)}, u32[]{:S(2)}) collective-permute-start(f32[8,128]{1,0:T(8,128)S(1)} %add.68), channel_id=1, source_target_pairs={{0,64},{1,65},{2,66},{3,67},{4,68},{5,69},{6,70},{7,71},{16,80},{1... | collective-permute-start | bytes 12296 | tf_op jit(solution)/shard_map/ppermute | solution.py:34
  (10 other events, 79.7 us)

commit v3 on v2

--- a/solution.py
+++ b/solution.py
@@ -64,16 +64,16 @@
 
 TEXT_MOVES = (x_up, x_down, x_far)
 IMAGE_MOVES = (y_far, before_up, before_down)
-FAR_MOVES = (
-    lambda z, y, x, c: (z, y ^ 1, x, c),
-    lambda z, y, x, c: (z, y ^ 2, x, c),
-    lambda z, y, x, c: (z ^ 1, y, x, c),
-    lambda z, y, x, c: (z ^ 2, y, x, c),
-)
 NEAR_MOVES = (
     lambda z, y, x, c: (z, y, x ^ 1, c),
     lambda z, y, x, c: (z, y, x ^ 2, c),
     other_core,
+)
+FAR_MOVES = (
+    lambda z, y, x, c: (z ^ 1, y, x, c),
+    lambda z, y, x, c: (z ^ 2, y, x, c),
+    lambda z, y, x, c: (z, y ^ 1, x, c),
+    lambda z, y, x, c: (z, y ^ 2, x, c),
 )
 
 
@@ -315,32 +315,34 @@
     below = send(image_half, before_down)
     texts = [text_half] + [send(text_half, move) for move in TEXT_MOVES]
     beside = send(image_half, other_core)
-    opposite = send(image_half, y_far)
+    opposite = send(after(image_half, above), y_far)
     first = [image_half, above, below]
     first_other = [beside, send(above, other_core), send(below, other_core)]
-    second_other = send(opposite, other_core)
 
     mine, other, text_acc, sums = pairs(scalars, texts, first, first_other)
-    from_core = send(other, other_core)
+    second_other = send(after(opposite, sums), other_core)
+    from_core = send(after(other, second_other), other_core)
     second, other, back0, back1, back2, back3 = pairs(
         scalars, texts, [opposite], [second_other], [text_acc, sums]
     )
     second_from_core = send(other, other_core)
 
     blocks = [slice(place * BLOCK, (place + 1) * BLOCK) for place in range(3)]
-    packs = [
-        packed(second, second_from_core),
-        packed(mine[blocks[1]], from_core[blocks[1]]),
-        packed(mine[blocks[2]], from_core[blocks[2]]),
-    ]
-    totals, *packs = lax.optimization_barrier((second[ROWS : ROWS + 8, :128], *packs))
-    opposite, above, below = [send(rows, move, back=True) for rows, move in zip(packs, IMAGE_MOVES)]
+    above = packed(mine[blocks[1]], from_core[blocks[1]])
+    below = packed(mine[blocks[2]], from_core[blocks[2]])
+    totals, above, below, second_from_core = lax.optimization_barrier(
+        (second[ROWS : ROWS + 8, :128], above, below, second_from_core)
+    )
+    opposite = packed(second, second_from_core)
+    above = send(above, before_up, back=True)
+    below = send(below, before_down, back=True)
     for move in NEAR_MOVES:
         totals = totals + send(totals, move)
-    back1, back2, back3 = after((back1, back2, back3), totals)
+    back1, back2, back3, opposite = after((back1, back2, back3, opposite), totals)
     up = send(back1.astype(jnp.float16), x_up, back=True)
     down = send(back2.astype(jnp.float16), x_down, back=True)
-    far = send(back3.astype(jnp.float16), x_far, back=True)
+    far = send(after(back3, up, down).astype(jnp.float16), x_far, back=True)
+    opposite = send(opposite, y_far, back=True)
     totals = after(totals, above, below, opposite)
     for move in FAR_MOVES:
         totals = totals + send(totals, move)

time: 157 us -> 152 us (0.968)
  waiting for transfers between devices: 61.2 us -> 51.6 us
  starting transfers between devices: 32 us -> 35.8 us
    ppermute x25, waiting for transfers between devices: 61.2 us -> 51.6 us  [send(): return lax.ppermute(value, AXES, pairs)]
    ppermute x25, starting transfers between devices: 32 us -> 35.8 us  [send(): return lax.ppermute(value, AXES, pairs)]
    convert_element_type x1 -> x2, other arithmetic: 3.56 us -> 4.5 us  [packed(): return rows.astype(jnp.float16).reshape(BLOCK, -1)]
  transfers between devices with their start and end apart: 25 -> 25, of which waited for: 11 -> 9; matrix products, arithmetic and copies ran while one was open for 5% -> 7% of each run, Pallas kernels for 24% -> 22%
where the time goes in v3:
time: 152 us
  waiting for transfers between devices  51.6 us (34%)
  Pallas kernels  40 us (26%)
  starting transfers between devices  35.8 us (24%)
  other arithmetic  12.6 us (8%)
  local copies, waits for them, and re-layouts  7.79 us (5%)
  between operations  4.03 us (3%)
    ppermute x25, waiting for transfers between devices, send(): return lax.ppermute(value, AXES, pairs)  51.6 us
    ppermute x25, starting transfers between devices, send(): return lax.ppermute(value, AXES, pairs)  35.8 us
    pallas_call x2, Pallas kernels, pairs(): pl.pallas_call(functools.partial(pairs_kernel, count, last, last), grid=(...  31 us
    unnamed x18, local copies, waits for them, and re-layouts  7.09 us
    pallas_call x2, Pallas kernels, tangent_part(): pl.pallas_call(tangent_kernel, in_specs=[pl.BlockSpec(memory_space=pltpu....  6.1 us
    convert_element_type x2, other arithmetic, packed(): return rows.astype(jnp.float16).reshape(BLOCK, -1)  4.5 us
    add x1, other arithmetic, on_device(): image_sum = image_sum + unpacked(rows)  3.07 us
  transfers between devices with their start and end apart: 25, of which 9 were waited for; matrix products, arithmetic and copies ran while one was open for 7% of the time, Pallas kernels for 22%

profile of v3, /device:TPU:0, one launch (start us, length us, event | category | flops | bytes accessed | tf_op | source)
XLA Modules:
  0.0 151.8 jit_solution(14356323039138190936)
XLA Ops:
  0.6 2.9 %halves.1 = (bf16[256,1152]{1,0:T(8,128)(2,1)}, bf16[256,1152]{1,0:T(8,128)(2,1)}) custom-call(f32[256,1152]{1,0:T(8,128)} %embeds_ref.2, f32[256,1152]{1,0:T(8,128)} %embeds_ref.3), custom_call_target="tpu_custom_call" | custom-call | tf_op jit(solution)/shard_map/halves/pallas_call | solution.py:89
  5.1 5.0 %collective-permute-start.3 = (bf16[256,1152]{1,0:T(8,128)(2,1)}, bf16[256,1152]{1,0:T(8,128)(2,1)S(1)}, u32[]{:S(2)}, u32[]{:S(2)}) collective-permute-start(bf16[256,1152]{1,0:T(8,128)(2,1)} %get-tuple-element.32.refs_5_), channel_id=1, source_target_pairs={{0,112},{1,113},{2,114},{3,115},{4,116},{5,117},{6,118},{7,119},{1... | collective-permute-start | bytes 1769480 | tf_op jit(solution)/shard_map/ppermute | solution.py:34
  10.1 1.7 %collective-permute-start.5 = (bf16[256,1152]{1,0:T(8,128)(2,1)}, bf16[256,1152]{1,0:T(8,128)(2,1)S(1)}, u32[]{:S(2)}, u32[]{:S(2)}) collective-permute-start(bf16[256,1152]{1,0:T(8,128)(2,1)} %get-tuple-element.32.refs_5_), channel_id=1, source_target_pairs={{0,120},{1,121},{2,122},{3,123},{4,124},{5,125},{6,126},{7,127},{1... | collective-permute-start | bytes 1769480 | tf_op jit(solution)/shard_map/ppermute | solution.py:34
  11.8 1.7 %collective-permute-start.1 = (bf16[256,1152]{1,0:T(8,128)(2,1)}, bf16[256,1152]{1,0:T(8,128)(2,1)S(1)}, u32[]{:S(2)}, u32[]{:S(2)}) collective-permute-start(bf16[256,1152]{1,0:T(8,128)(2,1)} %get-tuple-element.30.refs_1_), channel_id=1, source_target_pairs={{0,6},{1,7},{2,0},{3,1},{4,2},{5,3},{6,4},{7,5},{16,22},{17,23},{1... | collective-permute-start | bytes 1769480 | tf_op jit(solution)/shard_map/ppermute | solution.py:34
  13.6 1.8 %collective-permute-start.2 = (bf16[256,1152]{1,0:T(8,128)(2,1)}, bf16[256,1152]{1,0:T(8,128)(2,1)S(1)}, u32[]{:S(2)}, u32[]{:S(2)}) collective-permute-start(bf16[256,1152]{1,0:T(8,128)(2,1)} %get-tuple-element.30.refs_1_), channel_id=1, source_target_pairs={{0,4},{1,5},{2,6},{3,7},{4,0},{5,1},{6,2},{7,3},{16,20},{17,21},{1... | collective-permute-start | bytes 1769480 | tf_op jit(solution)/shard_map/ppermute | solution.py:34
  15.4 4.5 %collective-permute-done.refs_2_ = bf16[256,1152]{1,0:T(8,128)(2,1)S(1)} collective-permute-done((bf16[256,1152]{1,0:T(8,128)(2,1)}, bf16[256,1152]{1,0:T(8,128)(2,1)S(1)}, u32[]{:S(2)}, u32[]{:S(2)}) %collective-permute-start) | collective-permute-done | bytes 589856 | tf_op jit(solution)/shard_map/ppermute | solution.py:34
  19.9 13.2 %collective-permute-done.3.refs_6_ = bf16[256,1152]{1,0:T(8,128)(2,1)S(1)} collective-permute-done((bf16[256,1152]{1,0:T(8,128)(2,1)}, bf16[256,1152]{1,0:T(8,128)(2,1)S(1)}, u32[]{:S(2)}, u32[]{:S(2)}) %collective-permute-start.3) | collective-permute-done | bytes 589856 | tf_op jit(solution)/shard_map/ppermute | solution.py:34
  35.0 3.3 %collective-permute-done.1.refs_3_ = bf16[256,1152]{1,0:T(8,128)(2,1)S(1)} collective-permute-done((bf16[256,1152]{1,0:T(8,128)(2,1)}, bf16[256,1152]{1,0:T(8,128)(2,1)S(1)}, u32[]{:S(2)}, u32[]{:S(2)}) %collective-permute-start.1) | collective-permute-done | bytes 589856 | tf_op jit(solution)/shard_map/ppermute | solution.py:34
  38.3 1.9 %collective-permute-start.4 = (bf16[256,1152]{1,0:T(8,128)(2,1)}, bf16[256,1152]{1,0:T(8,128)(2,1)S(1)}, u32[]{:S(2)}, u32[]{:S(2)}) collective-permute-start(bf16[256,1152]{1,0:T(8,128)(2,1)} %get-tuple-element.32.refs_5_), channel_id=1, source_target_pairs={{0,8},{1,9},{2,10},{3,11},{4,12},{5,13},{6,14},{7,15},{16,24},{17,... | collective-permute-start | bytes 1769480 | tf_op jit(solution)/shard_map/ppermute | solution.py:34
  42.4 21.4 %pairs.2 = (f32[816,1152]{1,0:T(8,128)S(1)}, f32[816,1152]{1,0:T(8,128)}, f32[1024,1152]{1,0:T(8,128)}, f32[3,8,128]{2,1,0:T(8,128)S(1)}) custom-call(f32[3]{0:T(128)S(1)} %pad_maximum_fusion.refs_0_.scalars_ref, bf16[256,1152]{1,0:T(8,128)(2,1)S(1)} %copy-done.6, bf16[256,1152]{1,0:T(8,128)(2,1)S(1)} %collective-permute-done.refs_2_, ...), custom_call_target="tpu_custom_call" | custom-call | flops 10871635968 | bytes 1048576 | tf_op jit(solution)/shard_map/pairs/pallas_call | solution.py:248
  63.9 1.8 %copy-done = f32[816,1152]{1,0:T(8,128)} copy-done((f32[816,1152]{1,0:T(8,128)}, f32[816,1152]{1,0:T(8,128)S(1)}, u32[]{:S(2)}) %copy-start) | copy-done | bytes 3760152
  65.7 2.0 %collective-permute-done.9.refs_6_ = bf16[256,1152]{1,0:T(8,128)(2,1)S(1)} collective-permute-done((bf16[256,1152]{1,0:T(8,128)(2,1)S(1)}, bf16[256,1152]{1,0:T(8,128)(2,1)S(1)}, u32[]{:S(2)}, u32[]{:S(2)}) %collective-permute-start.9) | collective-permute-done | bytes 589856 | tf_op jit(solution)/shard_map/ppermute | solution.py:34
  67.8 9.6 %pairs.3 = (f32[272,1152]{1,0:T(8,128)S(1)}, f32[272,1152]{1,0:T(8,128)}, f32[256,1152]{1,0:T(8,128)S(1)}, f32[272,1152]{1,0:T(8,128)S(1)}, f32[272,1152]{1,0:T(8,128)S(1)}, /*index=5*/f32[272,1152]{1,0:T(8,128)}) custom-call(f32[3]{0:T(128)S(1)} %pad_maximum_fusion.refs_0_.scalars_ref, bf16[256,1152]{1,0:T(8,128)(2,1)S(1)} %copy-done.6, ...), custom_call_target="tpu_custom_call" | custom-call | flops 12079595520 | bytes 1048576 | tf_op jit(solution)/shard_map/pairs/pallas_call | solution.py:248
  81.0 2.9 %fusion.2 = (f16[272,1152]{1,0:T(8,128)(2,1)S(1)}, f16[272,1152]{1,0:T(8,128)(2,1)S(1)}) fusion(f32[816,1152]{1,0:T(8,128)} %collective-permute-done.10, f32[816,1152]{1,0:T(8,128)} %copy-done, f32[8,1152]{1,0:T(8,128)S(1)} %get-tuple-element.58, f32[8,1152]{1,0:T(8,128)S(1)} %get-tuple-element.57, pred[272]{0:T(512)(128)(4,1)S(1)} %iota.32, ...), kind=kLoop, calls=%fused_computation.3 | loop fusion | flops 2506752 | bytes 6414608 | tf_op jit(solution)/shard_map/convert_element_type | solution.py:298
  87.5 3.0 %collective-permute-start.13 = (f32[8,128]{1,0:T(8,128)S(1)}, f32[8,128]{1,0:T(8,128)S(1)}, u32[]{:S(2)}, u32[]{:S(2)}) collective-permute-start(f32[8,128]{1,0:T(8,128)S(1)} %add.62), channel_id=1, source_target_pairs={{0,4},{1,5},{2,6},{3,7},{4,0},{5,1},{6,2},{7,3},{16,20},{17,21},{1... | collective-permute-start | bytes 12296 | tf_op jit(solution)/shard_map/ppermute | solution.py:34
  94.3 1.7 %collective-permute-start.17 = (f16[272,1152]{1,0:T(8,128)(2,1)S(1)}, f16[272,1152]{1,0:T(8,128)(2,1)S(1)}, u32[]{:S(2)}, u32[]{:S(2)}) collective-permute-start(f16[272,1152]{1,0:T(8,128)(2,1)S(1)} %fusion.6), channel_id=1, source_target_pairs={{8,0},{9,1},{10,2},{11,3},{12,4},{13,5},{14,6},{15,7},{24,16},{25,... | collective-permute-start | bytes 1880072 | tf_op jit(solution)/shard_map/ppermute | solution.py:34
  96.1 3.6 %collective-permute-start.22 = (f16[272,1152]{1,0:T(8,128)(2,1)S(1)}, f16[272,1152]{1,0:T(8,128)(2,1)S(1)}, u32[]{:S(2)}, u32[]{:S(2)}) collective-permute-start(f16[272,1152]{1,0:T(8,128)(2,1)S(1)} %convert_element_type.51), channel_id=1, source_target_pairs={{2,0},{3,1},{4,2},{5,3},{6,4},{7,5},{0,6},{1,7},{18,16},{19,17},{2... | collective-permute-start | bytes 1880072 | tf_op jit(solution)/shard_map/ppermute | solution.py:34
  99.9 23.0 %collective-permute-done.16 = f16[272,1152]{1,0:T(8,128)(2,1)S(1)} collective-permute-done((f16[272,1152]{1,0:T(8,128)(2,1)S(1)}, f16[272,1152]{1,0:T(8,128)(2,1)S(1)}, u32[]{:S(2)}, u32[]{:S(2)}) %collective-permute-start.16) | collective-permute-done | bytes 626720 | tf_op jit(solution)/shard_map/ppermute | solution.py:34
  124.5 3.3 %collective-permute-start.24 = (f16[272,1152]{1,0:T(8,128)(2,1)S(1)}, f16[272,1152]{1,0:T(8,128)(2,1)}, u32[]{:S(2)}, u32[]{:S(2)}) collective-permute-start(f16[272,1152]{1,0:T(8,128)(2,1)S(1)} %convert_element_type.55), channel_id=1, source_target_pairs={{4,0},{5,1},{6,2},{7,3},{0,4},{1,5},{2,6},{3,7},{20,16},{21,17},{2... | collective-permute-start | bytes 1880072 | tf_op jit(solution)/shard_map/ppermute | solution.py:34
  128.1 3.1 %fusion.18.accum_ref = f32[256,1152]{1,0:T(8,128)} fusion(f32[272,1152]{1,0:T(8,128)S(1)} %convert_element_type.50, f32[272,1152]{1,0:T(8,128)S(1)} %convert_element_type.49, f32[272,1152]{1,0:T(8,128)S(1)} %convert_element_type.48, f32[816,1152]{1,0:T(8,128)} %collective-permute-done.10, f32[816,1152]{1,0:T(8,128)} %copy-done, f32[8,1152]{1,0:T(8,128)S(1)} %fusion.28, ...), kind=kLoop, calls=%fused_computation.26 | loop fusion | flops 2064384 | bytes 7188480 | tf_op jit(solution)/shard_map/add | solution.py:356
  132.9 2.5 %collective-permute-start.20 = (f32[8,128]{1,0:T(8,128)S(1)}, f32[8,128]{1,0:T(8,128)S(1)}, u32[]{:S(2)}, u32[]{:S(2)}) collective-permute-start(f32[8,128]{1,0:T(8,128)S(1)} %add.67), channel_id=1, source_target_pairs={{0,16},{1,17},{2,18},{3,19},{4,20},{5,21},{6,22},{7,23},{16,0},{17... | collective-permute-start | bytes 12296 | tf_op jit(solution)/shard_map/ppermute | solution.py:34
  136.9 3.8 %collective-permute-start.21 = (f32[8,128]{1,0:T(8,128)S(1)}, f32[8,128]{1,0:T(8,128)S(1)}, u32[]{:S(2)}, u32[]{:S(2)}) collective-permute-start(f32[8,128]{1,0:T(8,128)S(1)} %add.68), channel_id=1, source_target_pairs={{0,8},{1,9},{2,10},{3,11},{4,12},{5,13},{6,14},{7,15},{16,24},{17,... | collective-permute-start | bytes 12296 | tf_op jit(solution)/shard_map/ppermute | solution.py:34
  140.8 3.1 %tangent.2 = f32[256,1152]{1,0:T(8,128)} custom-call(f32[3]{0:T(128)} %copy-done.5, f32[256,1152]{1,0:T(8,128)} %embeds_ref.2, f32[256,1152]{1,0:T(8,128)} %fusion.18.accum_ref), custom_call_target="tpu_custom_call" | custom-call | tf_op jit(solution)/shard_map/tangent/pallas_call | solution.py:281
  147.6 3.0 %tangent.3 = f32[256,1152]{1,0:T(8,128)} custom-call(f32[3]{0:T(128)} %copy-done.5, f32[256,1152]{1,0:T(8,128)} %embeds_ref.3, f32[256,1152]{1,0:T(8,128)} %fusion.9.accum_ref), custom_call_target="tpu_custom_call" | custom-call | tf_op jit(solution)/shard_map/tangent/pallas_call | solution.py:281
  (84 shorter events, 23.8 us)
Async XLA Ops:
  3.5 16.4 %collective-permute-start = (bf16[256,1152]{1,0:T(8,128)(2,1)}, bf16[256,1152]{1,0:T(8,128)(2,1)S(1)}, u32[]{:S(2)}, u32[]{:S(2)}) collective-permute-start(bf16[256,1152]{1,0:T(8,128)(2,1)} %get-tuple-element.30.refs_1_), channel_id=1, source_target_pairs={{0,2},{1,3},{2,4},{3,5},{4,6},{5,7},{6,0},{7,1},{16,18},{17,19},{1... | collective-permute-start | bytes 1769480 | tf_op jit(solution)/shard_map/ppermute | solution.py:34
  5.1 28.0 %collective-permute-start.3 = (bf16[256,1152]{1,0:T(8,128)(2,1)}, bf16[256,1152]{1,0:T(8,128)(2,1)S(1)}, u32[]{:S(2)}, u32[]{:S(2)}) collective-permute-start(bf16[256,1152]{1,0:T(8,128)(2,1)} %get-tuple-element.32.refs_5_), channel_id=1, source_target_pairs={{0,112},{1,113},{2,114},{3,115},{4,116},{5,117},{6,118},{7,119},{1... | collective-permute-start | bytes 1769480 | tf_op jit(solution)/shard_map/ppermute | solution.py:34
  10.1 23.0 %collective-permute-start.5 = (bf16[256,1152]{1,0:T(8,128)(2,1)}, bf16[256,1152]{1,0:T(8,128)(2,1)S(1)}, u32[]{:S(2)}, u32[]{:S(2)}) collective-permute-start(bf16[256,1152]{1,0:T(8,128)(2,1)} %get-tuple-element.32.refs_5_), channel_id=1, source_target_pairs={{0,120},{1,121},{2,122},{3,123},{4,124},{5,125},{6,126},{7,127},{1... | collective-permute-start | bytes 1769480 | tf_op jit(solution)/shard_map/ppermute | solution.py:34
  11.8 26.5 %collective-permute-start.1 = (bf16[256,1152]{1,0:T(8,128)(2,1)}, bf16[256,1152]{1,0:T(8,128)(2,1)S(1)}, u32[]{:S(2)}, u32[]{:S(2)}) collective-permute-start(bf16[256,1152]{1,0:T(8,128)(2,1)} %get-tuple-element.30.refs_1_), channel_id=1, source_target_pairs={{0,6},{1,7},{2,0},{3,1},{4,2},{5,3},{6,4},{7,5},{16,22},{17,23},{1... | collective-permute-start | bytes 1769480 | tf_op jit(solution)/shard_map/ppermute | solution.py:34
  13.6 26.7 %collective-permute-start.2 = (bf16[256,1152]{1,0:T(8,128)(2,1)}, bf16[256,1152]{1,0:T(8,128)(2,1)S(1)}, u32[]{:S(2)}, u32[]{:S(2)}) collective-permute-start(bf16[256,1152]{1,0:T(8,128)(2,1)} %get-tuple-element.30.refs_1_), channel_id=1, source_target_pairs={{0,4},{1,5},{2,6},{3,7},{4,0},{5,1},{6,2},{7,3},{16,20},{17,21},{1... | collective-permute-start | bytes 1769480 | tf_op jit(solution)/shard_map/ppermute | solution.py:34
  19.9 20.4 %collective-permute-start.6 = (bf16[256,1152]{1,0:T(8,128)(2,1)}, bf16[256,1152]{1,0:T(8,128)(2,1)S(1)}, u32[]{:S(2)}, u32[]{:S(2)}) collective-permute-start(bf16[256,1152]{1,0:T(8,128)(2,1)} %get-tuple-element.32.refs_5_), channel_id=1, source_target_pairs={{0,1},{1,0},{2,3},{3,2},{4,5},{5,4},{6,7},{7,6},{16,17},{17,16},{1... | collective-permute-start | bytes 1769480 | tf_op jit(solution)/shard_map/ppermute | solution.py:34
  33.1 7.2 %collective-permute-start.7 = (bf16[256,1152]{1,0:T(8,128)(2,1)S(1)}, bf16[256,1152]{1,0:T(8,128)(2,1)S(1)}, u32[]{:S(2)}, u32[]{:S(2)}) collective-permute-start(bf16[256,1152]{1,0:T(8,128)(2,1)S(1)} %collective-permute-done.3.refs_6_), channel_id=1, source_target_pairs={{0,1},{1,0},{2,3},{3,2},{4,5},{5,4},{6,7},{7,6},{16,17},{17,16},{1... | collective-permute-start | bytes 1769480 | tf_op jit(solution)/shard_map/ppermute | solution.py:34
  33.1 7.2 %collective-permute-start.8 = (bf16[256,1152]{1,0:T(8,128)(2,1)S(1)}, bf16[256,1152]{1,0:T(8,128)(2,1)S(1)}, u32[]{:S(2)}, u32[]{:S(2)}) collective-permute-start(bf16[256,1152]{1,0:T(8,128)(2,1)S(1)} %collective-permute-done.5.refs_7_), channel_id=1, source_target_pairs={{0,1},{1,0},{2,3},{3,2},{4,5},{5,4},{6,7},{7,6},{16,17},{17,16},{1... | collective-permute-start | bytes 1769480 | tf_op jit(solution)/shard_map/ppermute | solution.py:34
  38.3 27.4 %collective-permute-start.4 = (bf16[256,1152]{1,0:T(8,128)(2,1)}, bf16[256,1152]{1,0:T(8,128)(2,1)S(1)}, u32[]{:S(2)}, u32[]{:S(2)}) collective-permute-start(bf16[256,1152]{1,0:T(8,128)(2,1)} %get-tuple-element.32.refs_5_), channel_id=1, source_target_pairs={{0,8},{1,9},{2,10},{3,11},{4,12},{5,13},{6,14},{7,15},{16,24},{17,... | collective-permute-start | bytes 1769480 | tf_op jit(solution)/shard_map/ppermute | solution.py:34
  65.7 2.0 %collective-permute-start.9 = (bf16[256,1152]{1,0:T(8,128)(2,1)S(1)}, bf16[256,1152]{1,0:T(8,128)(2,1)S(1)}, u32[]{:S(2)}, u32[]{:S(2)}) collective-permute-start(bf16[256,1152]{1,0:T(8,128)(2,1)S(1)} %collective-permute-done.4.refs_5_), channel_id=1, source_target_pairs={{0,1},{1,0},{2,3},{3,2},{4,5},{5,4},{6,7},{7,6},{16,17},{17,16},{1... | collective-permute-start | bytes 1769480 | tf_op jit(solution)/shard_map/ppermute | solution.py:34
  67.7 12.4 %collective-permute-start.10 = (f32[816,1152]{1,0:T(8,128)}, f32[816,1152]{1,0:T(8,128)}, u32[]{:S(2)}, u32[]{:S(2)}) collective-permute-start(f32[816,1152]{1,0:T(8,128)} %get-tuple-element.39), channel_id=1, source_target_pairs={{0,1},{1,0},{2,3},{3,2},{4,5},{5,4},{6,7},{7,6},{16,17},{17,16},{1... | collective-permute-start | bytes 11280392 | tf_op jit(solution)/shard_map/ppermute | solution.py:34
  79.5 4.3 %collective-permute-start.11 = (f32[272,1152]{1,0:T(8,128)}, f32[272,1152]{1,0:T(8,128)}, u32[]{:S(2)}, u32[]{:S(2)}) collective-permute-start(f32[272,1152]{1,0:T(8,128)} %get-tuple-element.40), channel_id=1, source_target_pairs={{0,1},{1,0},{2,3},{3,2},{4,5},{5,4},{6,7},{7,6},{16,17},{17,16},{1... | collective-permute-start | bytes 3760136 | tf_op jit(solution)/shard_map/ppermute | solution.py:34
  83.8 3.7 %collective-permute-start.12 = (f32[8,128]{1,0:T(8,128)S(1)}, f32[8,128]{1,0:T(8,128)S(1)}, u32[]{:S(2)}, u32[]{:S(2)}) collective-permute-start(f32[8,128]{1,0:T(8,128)S(1)} %slice.130), channel_id=1, source_target_pairs={{0,2},{1,3},{2,0},{3,1},{4,6},{5,7},{6,4},{7,5},{16,18},{17,19},{1... | collective-permute-start | bytes 12296 | tf_op jit(solution)/shard_map/ppermute | solution.py:34
  85.4 37.6 %collective-permute-start.15 = (f16[272,1152]{1,0:T(8,128)(2,1)S(1)}, f16[272,1152]{1,0:T(8,128)(2,1)S(1)}, u32[]{:S(2)}, u32[]{:S(2)}) collective-permute-start(f16[272,1152]{1,0:T(8,128)(2,1)S(1)} %get-tuple-element.42), channel_id=1, source_target_pairs={{112,0},{113,1},{114,2},{115,3},{116,4},{117,5},{118,6},{119,7},{8... | collective-permute-start | bytes 1880072 | tf_op jit(solution)/shard_map/ppermute | solution.py:34
  86.5 36.4 %collective-permute-start.16 = (f16[272,1152]{1,0:T(8,128)(2,1)S(1)}, f16[272,1152]{1,0:T(8,128)(2,1)S(1)}, u32[]{:S(2)}, u32[]{:S(2)}) collective-permute-start(f16[272,1152]{1,0:T(8,128)(2,1)S(1)} %get-tuple-element.43), channel_id=1, source_target_pairs={{120,0},{121,1},{122,2},{123,3},{124,4},{125,5},{126,6},{127,7},{0... | collective-permute-start | bytes 1880072 | tf_op jit(solution)/shard_map/ppermute | solution.py:34
  87.5 5.1 %collective-permute-start.13 = (f32[8,128]{1,0:T(8,128)S(1)}, f32[8,128]{1,0:T(8,128)S(1)}, u32[]{:S(2)}, u32[]{:S(2)}) collective-permute-start(f32[8,128]{1,0:T(8,128)S(1)} %add.62), channel_id=1, source_target_pairs={{0,4},{1,5},{2,6},{3,7},{4,0},{5,1},{6,2},{7,3},{16,20},{17,21},{1... | collective-permute-start | bytes 12296 | tf_op jit(solution)/shard_map/ppermute | solution.py:34
  94.3 28.8 %collective-permute-start.17 = (f16[272,1152]{1,0:T(8,128)(2,1)S(1)}, f16[272,1152]{1,0:T(8,128)(2,1)S(1)}, u32[]{:S(2)}, u32[]{:S(2)}) collective-permute-start(f16[272,1152]{1,0:T(8,128)(2,1)S(1)} %fusion.6), channel_id=1, source_target_pairs={{8,0},{9,1},{10,2},{11,3},{12,4},{13,5},{14,6},{15,7},{24,16},{25,... | collective-permute-start | bytes 1880072 | tf_op jit(solution)/shard_map/ppermute | solution.py:34
  96.1 27.3 %collective-permute-start.22 = (f16[272,1152]{1,0:T(8,128)(2,1)S(1)}, f16[272,1152]{1,0:T(8,128)(2,1)S(1)}, u32[]{:S(2)}, u32[]{:S(2)}) collective-permute-start(f16[272,1152]{1,0:T(8,128)(2,1)S(1)} %convert_element_type.51), channel_id=1, source_target_pairs={{2,0},{3,1},{4,2},{5,3},{6,4},{7,5},{0,6},{1,7},{18,16},{19,17},{2... | collective-permute-start | bytes 1880072 | tf_op jit(solution)/shard_map/ppermute | solution.py:34
  99.8 23.6 %collective-permute-start.23 = (f16[272,1152]{1,0:T(8,128)(2,1)S(1)}, f16[272,1152]{1,0:T(8,128)(2,1)S(1)}, u32[]{:S(2)}, u32[]{:S(2)}) collective-permute-start(f16[272,1152]{1,0:T(8,128)(2,1)S(1)} %convert_element_type.53), channel_id=1, source_target_pairs={{6,0},{7,1},{0,2},{1,3},{2,4},{3,5},{4,6},{5,7},{22,16},{23,17},{1... | collective-permute-start | bytes 1880072 | tf_op jit(solution)/shard_map/ppermute | solution.py:34
  123.1 4.6 %collective-permute-start.18 = (f32[8,128]{1,0:T(8,128)S(1)}, f32[8,128]{1,0:T(8,128)S(1)}, u32[]{:S(2)}, u32[]{:S(2)}) collective-permute-start(f32[8,128]{1,0:T(8,128)S(1)} %add.64), channel_id=1, source_target_pairs={{0,32},{1,33},{2,34},{3,35},{4,36},{5,37},{6,38},{7,39},{16,48},{1... | collective-permute-start | bytes 12296 | tf_op jit(solution)/shard_map/ppermute | solution.py:34
  124.5 20.5 %collective-permute-start.24 = (f16[272,1152]{1,0:T(8,128)(2,1)S(1)}, f16[272,1152]{1,0:T(8,128)(2,1)}, u32[]{:S(2)}, u32[]{:S(2)}) collective-permute-start(f16[272,1152]{1,0:T(8,128)(2,1)S(1)} %convert_element_type.55), channel_id=1, source_target_pairs={{4,0},{5,1},{6,2},{7,3},{0,4},{1,5},{2,6},{3,7},{20,16},{21,17},{2... | collective-permute-start | bytes 1880072 | tf_op jit(solution)/shard_map/ppermute | solution.py:34
  127.8 5.1 %collective-permute-start.19 = (f32[8,128]{1,0:T(8,128)S(1)}, f32[8,128]{1,0:T(8,128)S(1)}, u32[]{:S(2)}, u32[]{:S(2)}) collective-permute-start(f32[8,128]{1,0:T(8,128)S(1)} %add.66), channel_id=1, source_target_pairs={{0,64},{1,65},{2,66},{3,67},{4,68},{5,69},{6,70},{7,71},{16,80},{1... | collective-permute-start | bytes 12296 | tf_op jit(solution)/shard_map/ppermute | solution.py:34
  132.9 4.0 %collective-permute-start.20 = (f32[8,128]{1,0:T(8,128)S(1)}, f32[8,128]{1,0:T(8,128)S(1)}, u32[]{:S(2)}, u32[]{:S(2)}) collective-permute-start(f32[8,128]{1,0:T(8,128)S(1)} %add.67), channel_id=1, source_target_pairs={{0,16},{1,17},{2,18},{3,19},{4,20},{5,21},{6,22},{7,23},{16,0},{17... | collective-permute-start | bytes 12296 | tf_op jit(solution)/shard_map/ppermute | solution.py:34
  136.9 6.9 %collective-permute-start.21 = (f32[8,128]{1,0:T(8,128)S(1)}, f32[8,128]{1,0:T(8,128)S(1)}, u32[]{:S(2)}, u32[]{:S(2)}) collective-permute-start(f32[8,128]{1,0:T(8,128)S(1)} %add.68), channel_id=1, source_target_pairs={{0,8},{1,9},{2,10},{3,11},{4,12},{5,13},{6,14},{7,15},{16,24},{17,... | collective-permute-start | bytes 12296 | tf_op jit(solution)/shard_map/ppermute | solution.py:34
  (10 other events, 47.6 us)

commit v4 on v3

--- a/solution.py
+++ b/solution.py
@@ -15,7 +15,7 @@
 BLOCK = 272
 CHUNK = 16
 LANES = 128
-VMEM_LIMIT = 44 * 1024 * 1024
+VMEM_LIMIT = 32 * 1024 * 1024
 
 
 def place_index(z, y, x, core):
@@ -77,18 +77,63 @@
 )
 
 
-def halves_kernel(image_ref, text_ref, image_half_ref, text_half_ref):
-    for ref, half_ref in ((image_ref, image_half_ref), (text_ref, text_half_ref)):
-        rows = ref[...]
-        length = jnp.sqrt(jnp.sum(rows * rows, axis=1, keepdims=True) + EPS)
-        half_ref[...] = (rows / length).astype(jnp.bfloat16)
+PARTS = 4
+
+
+def part_copies(sources, targets, sems):
+    rows = ROWS // PARTS
+    return [
+        [
+            pltpu.make_async_copy(
+                source.at[pl.ds(part * rows, rows)], target.at[pl.ds(part * rows, rows)], sems.at[part, place]
+            )
+            for place, (source, target) in enumerate(zip(sources, targets))
+        ]
+        for part in range(PARTS)
+    ]
+
+
+def by_parts(work, sources, held, results, targets, in_sems, out_sems):
+    inward = part_copies(sources, held, in_sems)
+    outward = part_copies(results, targets, out_sems)
+    for copies in inward:
+        for copy in copies:
+            copy.start()
+    for part in range(PARTS):
+        for copy in inward[part]:
+            copy.wait()
+        work(slice(part * (ROWS // PARTS), (part + 1) * (ROWS // PARTS)))
+        for copy in outward[part]:
+            copy.start()
+    for copies in outward:
+        for copy in copies:
+            copy.wait()
+
+
+def halves_kernel(image_ref, text_ref, image_half_ref, text_half_ref, *buffers):
+    held, results, sems = buffers[:2], buffers[2:4], buffers[4:]
+
+    def work(part):
+        for ref, half_ref in zip(held, results):
+            rows = ref[part, :]
+            length = jnp.sqrt(jnp.sum(rows * rows, axis=1, keepdims=True) + EPS)
+            half_ref[part, :] = (rows * (1.0 / length)).astype(jnp.bfloat16)
+
+    by_parts(work, (image_ref, text_ref), held, results, (image_half_ref, text_half_ref), *sems)
 
 
 def halves(image_embeds, text_embeds):
-    shape = jax.ShapeDtypeStruct(image_embeds.shape, jnp.bfloat16)
+    shape = image_embeds.shape
+    half = jax.ShapeDtypeStruct(shape, jnp.bfloat16)
+    anywhere = pl.BlockSpec(memory_space=pl.ANY)
     return pl.pallas_call(
         halves_kernel,
-        out_shape=(shape, shape),
+        in_specs=[anywhere] * 2,
+        out_specs=[anywhere] * 2,
+        out_shape=(half, half),
+        scratch_shapes=[pltpu.VMEM(shape, jnp.float32)] * 2
+        + [pltpu.VMEM(shape, jnp.bfloat16)] * 2
+        + [pltpu.SemaphoreType.DMA((PARTS, 2))] * 2,
         name="halves",
     )(image_embeds, text_embeds)
 

time: 152 us -> 149 us (0.980)
  Pallas kernels: 40 us -> 36 us
  starting transfers between devices: 35.8 us -> 37.7 us
    pallas_call x2, Pallas kernels: 31 us -> 27.4 us  [pairs(): pl.pallas_call(functools.partial(pairs_kernel, count, last, last), grid=(...]
    ppermute x25, starting transfers between devices: 35.8 us -> 37.7 us  [send(): return lax.ppermute(value, AXES, pairs)]
    unnamed x18 -> x22, local copies, waits for them, and re-layouts: 7.09 us -> 7.14 us
  transfers between devices with their start and end apart: 25 -> 25, of which waited for: 9 -> 10; matrix products, arithmetic and copies ran while one was open for 7% -> 7% of each run, Pallas kernels for 22% -> 20%
where the time goes in v4:
time: 149 us
  waiting for transfers between devices  50.7 us (34%)
  starting transfers between devices  37.7 us (25%)
  Pallas kernels  36 us (24%)
  other arithmetic  12.5 us (8%)
  local copies, waits for them, and re-layouts  7.84 us (5%)
  between operations  4.04 us (3%)
    ppermute x25, waiting for transfers between devices, send(): return lax.ppermute(value, AXES, pairs)  50.7 us
    ppermute x25, starting transfers between devices, send(): return lax.ppermute(value, AXES, pairs)  37.7 us
    pallas_call x2, Pallas kernels, pairs(): pl.pallas_call(functools.partial(pairs_kernel, count, last, last), grid=(...  27.4 us
    unnamed x22, local copies, waits for them, and re-layouts  7.14 us
    pallas_call x2, Pallas kernels, tangent_part(): pl.pallas_call(tangent_kernel, in_specs=[pl.BlockSpec(memory_space=pltpu....  6.1 us
    convert_element_type x2, other arithmetic, packed(): return rows.astype(jnp.float16).reshape(BLOCK, -1)  4.5 us
    add x1, other arithmetic, on_device(): image_sum = image_sum + unpacked(rows)  3.07 us
  transfers between devices with their start and end apart: 25, of which 10 were waited for; matrix products, arithmetic and copies ran while one was open for 7% of the time, Pallas kernels for 20%

profile of v4, /device:TPU:0, one launch (start us, length us, event | category | flops | bytes accessed | tf_op | source)
XLA Modules:
  0.0 148.9 jit_solution(11547341178622008768)
XLA Ops:
  0.6 2.6 %halves.1 = (bf16[256,1152]{1,0:T(8,128)(2,1)}, bf16[256,1152]{1,0:T(8,128)(2,1)}) custom-call(f32[256,1152]{1,0:T(8,128)} %embeds_ref.2, f32[256,1152]{1,0:T(8,128)} %embeds_ref.3), custom_call_target="tpu_custom_call" | custom-call | tf_op jit(solution)/shard_map/halves/pallas_call | solution.py:129
  4.8 5.0 %collective-permute-start.3 = (bf16[256,1152]{1,0:T(8,128)(2,1)}, bf16[256,1152]{1,0:T(8,128)(2,1)S(1)}, u32[]{:S(2)}, u32[]{:S(2)}) collective-permute-start(bf16[256,1152]{1,0:T(8,128)(2,1)} %get-tuple-element.32.refs_5_), channel_id=1, source_target_pairs={{0,112},{1,113},{2,114},{3,115},{4,116},{5,117},{6,118},{7,119},{1... | collective-permute-start | bytes 1769480 | tf_op jit(solution)/shard_map/ppermute | solution.py:34
  9.9 1.7 %collective-permute-start.5 = (bf16[256,1152]{1,0:T(8,128)(2,1)}, bf16[256,1152]{1,0:T(8,128)(2,1)S(1)}, u32[]{:S(2)}, u32[]{:S(2)}) collective-permute-start(bf16[256,1152]{1,0:T(8,128)(2,1)} %get-tuple-element.32.refs_5_), channel_id=1, source_target_pairs={{0,120},{1,121},{2,122},{3,123},{4,124},{5,125},{6,126},{7,127},{1... | collective-permute-start | bytes 1769480 | tf_op jit(solution)/shard_map/ppermute | solution.py:34
  11.6 1.7 %collective-permute-start.1 = (bf16[256,1152]{1,0:T(8,128)(2,1)}, bf16[256,1152]{1,0:T(8,128)(2,1)S(1)}, u32[]{:S(2)}, u32[]{:S(2)}) collective-permute-start(bf16[256,1152]{1,0:T(8,128)(2,1)} %get-tuple-element.30.refs_1_), channel_id=1, source_target_pairs={{0,6},{1,7},{2,0},{3,1},{4,2},{5,3},{6,4},{7,5},{16,22},{17,23},{1... | collective-permute-start | bytes 1769480 | tf_op jit(solution)/shard_map/ppermute | solution.py:34
  13.3 1.8 %collective-permute-start.2 = (bf16[256,1152]{1,0:T(8,128)(2,1)}, bf16[256,1152]{1,0:T(8,128)(2,1)S(1)}, u32[]{:S(2)}, u32[]{:S(2)}) collective-permute-start(bf16[256,1152]{1,0:T(8,128)(2,1)} %get-tuple-element.30.refs_1_), channel_id=1, source_target_pairs={{0,4},{1,5},{2,6},{3,7},{4,0},{5,1},{6,2},{7,3},{16,20},{17,21},{1... | collective-permute-start | bytes 1769480 | tf_op jit(solution)/shard_map/ppermute | solution.py:34
  15.1 4.5 %collective-permute-done.refs_2_ = bf16[256,1152]{1,0:T(8,128)(2,1)S(1)} collective-permute-done((bf16[256,1152]{1,0:T(8,128)(2,1)}, bf16[256,1152]{1,0:T(8,128)(2,1)S(1)}, u32[]{:S(2)}, u32[]{:S(2)}) %collective-permute-start) | collective-permute-done | bytes 589856 | tf_op jit(solution)/shard_map/ppermute | solution.py:34
  19.7 13.2 %collective-permute-done.3.refs_6_ = bf16[256,1152]{1,0:T(8,128)(2,1)S(1)} collective-permute-done((bf16[256,1152]{1,0:T(8,128)(2,1)}, bf16[256,1152]{1,0:T(8,128)(2,1)S(1)}, u32[]{:S(2)}, u32[]{:S(2)}) %collective-permute-start.3) | collective-permute-done | bytes 589856 | tf_op jit(solution)/shard_map/ppermute | solution.py:34
  34.8 3.3 %collective-permute-done.1.refs_3_ = bf16[256,1152]{1,0:T(8,128)(2,1)S(1)} collective-permute-done((bf16[256,1152]{1,0:T(8,128)(2,1)}, bf16[256,1152]{1,0:T(8,128)(2,1)S(1)}, u32[]{:S(2)}, u32[]{:S(2)}) %collective-permute-start.1) | collective-permute-done | bytes 589856 | tf_op jit(solution)/shard_map/ppermute | solution.py:34
  38.1 1.9 %collective-permute-start.4 = (bf16[256,1152]{1,0:T(8,128)(2,1)}, bf16[256,1152]{1,0:T(8,128)(2,1)S(1)}, u32[]{:S(2)}, u32[]{:S(2)}) collective-permute-start(bf16[256,1152]{1,0:T(8,128)(2,1)} %get-tuple-element.32.refs_5_), channel_id=1, source_target_pairs={{0,8},{1,9},{2,10},{3,11},{4,12},{5,13},{6,14},{7,15},{16,24},{17,... | collective-permute-start | bytes 1769480 | tf_op jit(solution)/shard_map/ppermute | solution.py:34
  42.2 20.0 %pairs.2 = (f32[816,1152]{1,0:T(8,128)S(1)}, f32[816,1152]{1,0:T(8,128)}, f32[1024,1152]{1,0:T(8,128)S(1)}, f32[3,8,128]{2,1,0:T(8,128)S(1)}) custom-call(f32[3]{0:T(128)S(1)} %pad_maximum_fusion.refs_0_.scalars_ref, bf16[256,1152]{1,0:T(8,128)(2,1)S(1)} %copy-done.8, bf16[256,1152]{1,0:T(8,128)(2,1)S(1)} %collective-permute-done.refs_2_, ...), custom_call_target="tpu_custom_call" | custom-call | flops 10871635968 | bytes 1048576 | tf_op jit(solution)/shard_map/pairs/pallas_call | solution.py:293
  62.2 1.8 %copy-done = f32[816,1152]{1,0:T(8,128)} copy-done((f32[816,1152]{1,0:T(8,128)}, f32[816,1152]{1,0:T(8,128)S(1)}, u32[]{:S(2)}) %copy-start) | copy-done | bytes 3760152
  64.0 2.0 %collective-permute-done.9.refs_6_ = bf16[256,1152]{1,0:T(8,128)(2,1)S(1)} collective-permute-done((bf16[256,1152]{1,0:T(8,128)(2,1)S(1)}, bf16[256,1152]{1,0:T(8,128)(2,1)S(1)}, u32[]{:S(2)}, u32[]{:S(2)}) %collective-permute-start.9) | collective-permute-done | bytes 589856 | tf_op jit(solution)/shard_map/ppermute | solution.py:34
  66.1 7.4 %pairs.3 = (f32[272,1152]{1,0:T(8,128)S(1)}, f32[272,1152]{1,0:T(8,128)}, f32[256,1152]{1,0:T(8,128)S(1)}, f32[272,1152]{1,0:T(8,128)S(1)}, f32[272,1152]{1,0:T(8,128)S(1)}, /*index=5*/f32[272,1152]{1,0:T(8,128)S(1)}) custom-call(f32[3]{0:T(128)S(1)} %pad_maximum_fusion.refs_0_.scalars_ref, bf16[256,1152]{1,0:T(8,128)(2,1)S(1)} %copy-done.9, ...), custom_call_target="tpu_custom_call" | custom-call | flops 12079595520 | bytes 1048576 | tf_op jit(solution)/shard_map/pairs/pallas_call | solution.py:293
  78.1 2.9 %fusion.2 = (f16[272,1152]{1,0:T(8,128)(2,1)S(1)}, f16[272,1152]{1,0:T(8,128)(2,1)S(1)}) fusion(f32[816,1152]{1,0:T(8,128)} %collective-permute-done.10, f32[816,1152]{1,0:T(8,128)} %copy-done, f32[8,1152]{1,0:T(8,128)S(1)} %get-tuple-element.58, f32[8,1152]{1,0:T(8,128)S(1)} %get-tuple-element.57, pred[272]{0:T(512)(128)(4,1)S(1)} %iota.32, ...), kind=kLoop, calls=%fused_computation.3 | loop fusion | flops 2506752 | bytes 6414608 | tf_op jit(solution)/shard_map/convert_element_type | solution.py:343
  84.7 3.0 %collective-permute-start.13 = (f32[8,128]{1,0:T(8,128)S(1)}, f32[8,128]{1,0:T(8,128)S(1)}, u32[]{:S(2)}, u32[]{:S(2)}) collective-permute-start(f32[8,128]{1,0:T(8,128)S(1)} %add.62), channel_id=1, source_target_pairs={{0,4},{1,5},{2,6},{3,7},{4,0},{5,1},{6,2},{7,3},{16,20},{17,21},{1... | collective-permute-start | bytes 12296 | tf_op jit(solution)/shard_map/ppermute | solution.py:34
  91.5 1.7 %collective-permute-start.17 = (f16[272,1152]{1,0:T(8,128)(2,1)S(1)}, f16[272,1152]{1,0:T(8,128)(2,1)S(1)}, u32[]{:S(2)}, u32[]{:S(2)}) collective-permute-start(f16[272,1152]{1,0:T(8,128)(2,1)S(1)} %fusion.6), channel_id=1, source_target_pairs={{8,0},{9,1},{10,2},{11,3},{12,4},{13,5},{14,6},{15,7},{24,16},{25,... | collective-permute-start | bytes 1880072 | tf_op jit(solution)/shard_map/ppermute | solution.py:34
  93.2 3.6 %collective-permute-start.22 = (f16[272,1152]{1,0:T(8,128)(2,1)S(1)}, f16[272,1152]{1,0:T(8,128)(2,1)S(1)}, u32[]{:S(2)}, u32[]{:S(2)}) collective-permute-start(f16[272,1152]{1,0:T(8,128)(2,1)S(1)} %convert_element_type.51), channel_id=1, source_target_pairs={{2,0},{3,1},{4,2},{5,3},{6,4},{7,5},{0,6},{1,7},{18,16},{19,17},{2... | collective-permute-start | bytes 1880072 | tf_op jit(solution)/shard_map/ppermute | solution.py:34
  97.0 23.0 %collective-permute-done.16 = f16[272,1152]{1,0:T(8,128)(2,1)S(1)} collective-permute-done((f16[272,1152]{1,0:T(8,128)(2,1)S(1)}, f16[272,1152]{1,0:T(8,128)(2,1)S(1)}, u32[]{:S(2)}, u32[]{:S(2)}) %collective-permute-start.16) | collective-permute-done | bytes 626720 | tf_op jit(solution)/shard_map/ppermute | solution.py:34
  120.6 3.3 %collective-permute-start.24 = (f16[272,1152]{1,0:T(8,128)(2,1)S(1)}, f16[272,1152]{1,0:T(8,128)(2,1)}, u32[]{:S(2)}, u32[]{:S(2)}) collective-permute-start(f16[272,1152]{1,0:T(8,128)(2,1)S(1)} %convert_element_type.55), channel_id=1, source_target_pairs={{4,0},{5,1},{6,2},{7,3},{0,4},{1,5},{2,6},{3,7},{20,16},{21,17},{2... | collective-permute-start | bytes 1880072 | tf_op jit(solution)/shard_map/ppermute | solution.py:34
  125.2 3.1 %fusion.18.accum_ref = f32[256,1152]{1,0:T(8,128)} fusion(f32[272,1152]{1,0:T(8,128)S(1)} %convert_element_type.50, f32[272,1152]{1,0:T(8,128)S(1)} %convert_element_type.49, f32[272,1152]{1,0:T(8,128)S(1)} %convert_element_type.48, f32[816,1152]{1,0:T(8,128)} %collective-permute-done.10, f32[816,1152]{1,0:T(8,128)} %copy-done, f32[8,1152]{1,0:T(8,128)S(1)} %fusion.28, ...), kind=kLoop, calls=%fused_computation.26 | loop fusion | flops 2064384 | bytes 7188480 | tf_op jit(solution)/shard_map/add | solution.py:401
  129.1 3.4 %collective-permute-start.20 = (f32[8,128]{1,0:T(8,128)S(1)}, f32[8,128]{1,0:T(8,128)S(1)}, u32[]{:S(2)}, u32[]{:S(2)}) collective-permute-start(f32[8,128]{1,0:T(8,128)S(1)} %add.67), channel_id=1, source_target_pairs={{0,16},{1,17},{2,18},{3,19},{4,20},{5,21},{6,22},{7,23},{16,0},{17... | collective-permute-start | bytes 12296 | tf_op jit(solution)/shard_map/ppermute | solution.py:34
  134.0 3.8 %collective-permute-start.21 = (f32[8,128]{1,0:T(8,128)S(1)}, f32[8,128]{1,0:T(8,128)S(1)}, u32[]{:S(2)}, u32[]{:S(2)}) collective-permute-start(f32[8,128]{1,0:T(8,128)S(1)} %add.68), channel_id=1, source_target_pairs={{0,8},{1,9},{2,10},{3,11},{4,12},{5,13},{6,14},{7,15},{16,24},{17,... | collective-permute-start | bytes 12296 | tf_op jit(solution)/shard_map/ppermute | solution.py:34
  137.9 3.1 %tangent.2 = f32[256,1152]{1,0:T(8,128)} custom-call(f32[3]{0:T(128)} %copy-done.7, f32[256,1152]{1,0:T(8,128)} %embeds_ref.2, f32[256,1152]{1,0:T(8,128)} %fusion.18.accum_ref), custom_call_target="tpu_custom_call" | custom-call | tf_op jit(solution)/shard_map/tangent/pallas_call | solution.py:326
  144.7 3.0 %tangent.3 = f32[256,1152]{1,0:T(8,128)} custom-call(f32[3]{0:T(128)} %copy-done.7, f32[256,1152]{1,0:T(8,128)} %embeds_ref.3, f32[256,1152]{1,0:T(8,128)} %fusion.9.accum_ref), custom_call_target="tpu_custom_call" | custom-call | tf_op jit(solution)/shard_map/tangent/pallas_call | solution.py:326
  (88 shorter events, 24.0 us)
Async XLA Ops:
  3.2 16.4 %collective-permute-start = (bf16[256,1152]{1,0:T(8,128)(2,1)}, bf16[256,1152]{1,0:T(8,128)(2,1)S(1)}, u32[]{:S(2)}, u32[]{:S(2)}) collective-permute-start(bf16[256,1152]{1,0:T(8,128)(2,1)} %get-tuple-element.30.refs_1_), channel_id=1, source_target_pairs={{0,2},{1,3},{2,4},{3,5},{4,6},{5,7},{6,0},{7,1},{16,18},{17,19},{1... | collective-permute-start | bytes 1769480 | tf_op jit(solution)/shard_map/ppermute | solution.py:34
  4.8 28.0 %collective-permute-start.3 = (bf16[256,1152]{1,0:T(8,128)(2,1)}, bf16[256,1152]{1,0:T(8,128)(2,1)S(1)}, u32[]{:S(2)}, u32[]{:S(2)}) collective-permute-start(bf16[256,1152]{1,0:T(8,128)(2,1)} %get-tuple-element.32.refs_5_), channel_id=1, source_target_pairs={{0,112},{1,113},{2,114},{3,115},{4,116},{5,117},{6,118},{7,119},{1... | collective-permute-start | bytes 1769480 | tf_op jit(solution)/shard_map/ppermute | solution.py:34
  9.9 23.0 %collective-permute-start.5 = (bf16[256,1152]{1,0:T(8,128)(2,1)}, bf16[256,1152]{1,0:T(8,128)(2,1)S(1)}, u32[]{:S(2)}, u32[]{:S(2)}) collective-permute-start(bf16[256,1152]{1,0:T(8,128)(2,1)} %get-tuple-element.32.refs_5_), channel_id=1, source_target_pairs={{0,120},{1,121},{2,122},{3,123},{4,124},{5,125},{6,126},{7,127},{1... | collective-permute-start | bytes 1769480 | tf_op jit(solution)/shard_map/ppermute | solution.py:34
  11.6 26.5 %collective-permute-start.1 = (bf16[256,1152]{1,0:T(8,128)(2,1)}, bf16[256,1152]{1,0:T(8,128)(2,1)S(1)}, u32[]{:S(2)}, u32[]{:S(2)}) collective-permute-start(bf16[256,1152]{1,0:T(8,128)(2,1)} %get-tuple-element.30.refs_1_), channel_id=1, source_target_pairs={{0,6},{1,7},{2,0},{3,1},{4,2},{5,3},{6,4},{7,5},{16,22},{17,23},{1... | collective-permute-start | bytes 1769480 | tf_op jit(solution)/shard_map/ppermute | solution.py:34
  13.3 26.7 %collective-permute-start.2 = (bf16[256,1152]{1,0:T(8,128)(2,1)}, bf16[256,1152]{1,0:T(8,128)(2,1)S(1)}, u32[]{:S(2)}, u32[]{:S(2)}) collective-permute-start(bf16[256,1152]{1,0:T(8,128)(2,1)} %get-tuple-element.30.refs_1_), channel_id=1, source_target_pairs={{0,4},{1,5},{2,6},{3,7},{4,0},{5,1},{6,2},{7,3},{16,20},{17,21},{1... | collective-permute-start | bytes 1769480 | tf_op jit(solution)/shard_map/ppermute | solution.py:34
  19.7 20.4 %collective-permute-start.6 = (bf16[256,1152]{1,0:T(8,128)(2,1)}, bf16[256,1152]{1,0:T(8,128)(2,1)S(1)}, u32[]{:S(2)}, u32[]{:S(2)}) collective-permute-start(bf16[256,1152]{1,0:T(8,128)(2,1)} %get-tuple-element.32.refs_5_), channel_id=1, source_target_pairs={{0,1},{1,0},{2,3},{3,2},{4,5},{5,4},{6,7},{7,6},{16,17},{17,16},{1... | collective-permute-start | bytes 1769480 | tf_op jit(solution)/shard_map/ppermute | solution.py:34
  32.9 7.2 %collective-permute-start.7 = (bf16[256,1152]{1,0:T(8,128)(2,1)S(1)}, bf16[256,1152]{1,0:T(8,128)(2,1)S(1)}, u32[]{:S(2)}, u32[]{:S(2)}) collective-permute-start(bf16[256,1152]{1,0:T(8,128)(2,1)S(1)} %collective-permute-done.3.refs_6_), channel_id=1, source_target_pairs={{0,1},{1,0},{2,3},{3,2},{4,5},{5,4},{6,7},{7,6},{16,17},{17,16},{1... | collective-permute-start | bytes 1769480 | tf_op jit(solution)/shard_map/ppermute | solution.py:34
  32.9 7.2 %collective-permute-start.8 = (bf16[256,1152]{1,0:T(8,128)(2,1)S(1)}, bf16[256,1152]{1,0:T(8,128)(2,1)S(1)}, u32[]{:S(2)}, u32[]{:S(2)}) collective-permute-start(bf16[256,1152]{1,0:T(8,128)(2,1)S(1)} %collective-permute-done.5.refs_7_), channel_id=1, source_target_pairs={{0,1},{1,0},{2,3},{3,2},{4,5},{5,4},{6,7},{7,6},{16,17},{17,16},{1... | collective-permute-start | bytes 1769480 | tf_op jit(solution)/shard_map/ppermute | solution.py:34
  38.1 25.9 %collective-permute-start.4 = (bf16[256,1152]{1,0:T(8,128)(2,1)}, bf16[256,1152]{1,0:T(8,128)(2,1)S(1)}, u32[]{:S(2)}, u32[]{:S(2)}) collective-permute-start(bf16[256,1152]{1,0:T(8,128)(2,1)} %get-tuple-element.32.refs_5_), channel_id=1, source_target_pairs={{0,8},{1,9},{2,10},{3,11},{4,12},{5,13},{6,14},{7,15},{16,24},{17,... | collective-permute-start | bytes 1769480 | tf_op jit(solution)/shard_map/ppermute | solution.py:34
  64.0 2.0 %collective-permute-start.9 = (bf16[256,1152]{1,0:T(8,128)(2,1)S(1)}, bf16[256,1152]{1,0:T(8,128)(2,1)S(1)}, u32[]{:S(2)}, u32[]{:S(2)}) collective-permute-start(bf16[256,1152]{1,0:T(8,128)(2,1)S(1)} %collective-permute-done.4.refs_5_), channel_id=1, source_target_pairs={{0,1},{1,0},{2,3},{3,2},{4,5},{5,4},{6,7},{7,6},{16,17},{17,16},{1... | collective-permute-start | bytes 1769480 | tf_op jit(solution)/shard_map/ppermute | solution.py:34
  66.0 11.3 %collective-permute-start.10 = (f32[816,1152]{1,0:T(8,128)}, f32[816,1152]{1,0:T(8,128)}, u32[]{:S(2)}, u32[]{:S(2)}) collective-permute-start(f32[816,1152]{1,0:T(8,128)} %get-tuple-element.39), channel_id=1, source_target_pairs={{0,1},{1,0},{2,3},{3,2},{4,5},{5,4},{6,7},{7,6},{16,17},{17,16},{1... | collective-permute-start | bytes 11280392 | tf_op jit(solution)/shard_map/ppermute | solution.py:34
  76.7 4.3 %collective-permute-start.11 = (f32[272,1152]{1,0:T(8,128)}, f32[272,1152]{1,0:T(8,128)}, u32[]{:S(2)}, u32[]{:S(2)}) collective-permute-start(f32[272,1152]{1,0:T(8,128)} %get-tuple-element.40), channel_id=1, source_target_pairs={{0,1},{1,0},{2,3},{3,2},{4,5},{5,4},{6,7},{7,6},{16,17},{17,16},{1... | collective-permute-start | bytes 3760136 | tf_op jit(solution)/shard_map/ppermute | solution.py:34
  81.0 3.7 %collective-permute-start.12 = (f32[8,128]{1,0:T(8,128)S(1)}, f32[8,128]{1,0:T(8,128)S(1)}, u32[]{:S(2)}, u32[]{:S(2)}) collective-permute-start(f32[8,128]{1,0:T(8,128)S(1)} %slice.130), channel_id=1, source_target_pairs={{0,2},{1,3},{2,0},{3,1},{4,6},{5,7},{6,4},{7,5},{16,18},{17,19},{1... | collective-permute-start | bytes 12296 | tf_op jit(solution)/shard_map/ppermute | solution.py:34
  82.5 37.6 %collective-permute-start.15 = (f16[272,1152]{1,0:T(8,128)(2,1)S(1)}, f16[272,1152]{1,0:T(8,128)(2,1)S(1)}, u32[]{:S(2)}, u32[]{:S(2)}) collective-permute-start(f16[272,1152]{1,0:T(8,128)(2,1)S(1)} %get-tuple-element.42), channel_id=1, source_target_pairs={{112,0},{113,1},{114,2},{115,3},{116,4},{117,5},{118,6},{119,7},{8... | collective-permute-start | bytes 1880072 | tf_op jit(solution)/shard_map/ppermute | solution.py:34
  83.6 36.4 %collective-permute-start.16 = (f16[272,1152]{1,0:T(8,128)(2,1)S(1)}, f16[272,1152]{1,0:T(8,128)(2,1)S(1)}, u32[]{:S(2)}, u32[]{:S(2)}) collective-permute-start(f16[272,1152]{1,0:T(8,128)(2,1)S(1)} %get-tuple-element.43), channel_id=1, source_target_pairs={{120,0},{121,1},{122,2},{123,3},{124,4},{125,5},{126,6},{127,7},{0... | collective-permute-start | bytes 1880072 | tf_op jit(solution)/shard_map/ppermute | solution.py:34
  84.7 5.1 %collective-permute-start.13 = (f32[8,128]{1,0:T(8,128)S(1)}, f32[8,128]{1,0:T(8,128)S(1)}, u32[]{:S(2)}, u32[]{:S(2)}) collective-permute-start(f32[8,128]{1,0:T(8,128)S(1)} %add.62), channel_id=1, source_target_pairs={{0,4},{1,5},{2,6},{3,7},{4,0},{5,1},{6,2},{7,3},{16,20},{17,21},{1... | collective-permute-start | bytes 12296 | tf_op jit(solution)/shard_map/ppermute | solution.py:34
  91.5 28.8 %collective-permute-start.17 = (f16[272,1152]{1,0:T(8,128)(2,1)S(1)}, f16[272,1152]{1,0:T(8,128)(2,1)S(1)}, u32[]{:S(2)}, u32[]{:S(2)}) collective-permute-start(f16[272,1152]{1,0:T(8,128)(2,1)S(1)} %fusion.6), channel_id=1, source_target_pairs={{8,0},{9,1},{10,2},{11,3},{12,4},{13,5},{14,6},{15,7},{24,16},{25,... | collective-permute-start | bytes 1880072 | tf_op jit(solution)/shard_map/ppermute | solution.py:34
  93.2 27.3 %collective-permute-start.22 = (f16[272,1152]{1,0:T(8,128)(2,1)S(1)}, f16[272,1152]{1,0:T(8,128)(2,1)S(1)}, u32[]{:S(2)}, u32[]{:S(2)}) collective-permute-start(f16[272,1152]{1,0:T(8,128)(2,1)S(1)} %convert_element_type.51), channel_id=1, source_target_pairs={{2,0},{3,1},{4,2},{5,3},{6,4},{7,5},{0,6},{1,7},{18,16},{19,17},{2... | collective-permute-start | bytes 1880072 | tf_op jit(solution)/shard_map/ppermute | solution.py:34
  96.9 23.6 %collective-permute-start.23 = (f16[272,1152]{1,0:T(8,128)(2,1)S(1)}, f16[272,1152]{1,0:T(8,128)(2,1)S(1)}, u32[]{:S(2)}, u32[]{:S(2)}) collective-permute-start(f16[272,1152]{1,0:T(8,128)(2,1)S(1)} %convert_element_type.53), channel_id=1, source_target_pairs={{6,0},{7,1},{0,2},{1,3},{2,4},{3,5},{4,6},{5,7},{22,16},{23,17},{1... | collective-permute-start | bytes 1880072 | tf_op jit(solution)/shard_map/ppermute | solution.py:34
  120.3 3.7 %collective-permute-start.18 = (f32[8,128]{1,0:T(8,128)S(1)}, f32[8,128]{1,0:T(8,128)S(1)}, u32[]{:S(2)}, u32[]{:S(2)}) collective-permute-start(f32[8,128]{1,0:T(8,128)S(1)} %add.64), channel_id=1, source_target_pairs={{0,32},{1,33},{2,34},{3,35},{4,36},{5,37},{6,38},{7,39},{16,48},{1... | collective-permute-start | bytes 12296 | tf_op jit(solution)/shard_map/ppermute | solution.py:34
  120.6 21.5 %collective-permute-start.24 = (f16[272,1152]{1,0:T(8,128)(2,1)S(1)}, f16[272,1152]{1,0:T(8,128)(2,1)}, u32[]{:S(2)}, u32[]{:S(2)}) collective-permute-start(f16[272,1152]{1,0:T(8,128)(2,1)S(1)} %convert_element_type.55), channel_id=1, source_target_pairs={{4,0},{5,1},{6,2},{7,3},{0,4},{1,5},{2,6},{3,7},{20,16},{21,17},{2... | collective-permute-start | bytes 1880072 | tf_op jit(solution)/shard_map/ppermute | solution.py:34
  124.0 5.1 %collective-permute-start.19 = (f32[8,128]{1,0:T(8,128)S(1)}, f32[8,128]{1,0:T(8,128)S(1)}, u32[]{:S(2)}, u32[]{:S(2)}) collective-permute-start(f32[8,128]{1,0:T(8,128)S(1)} %add.66), channel_id=1, source_target_pairs={{0,64},{1,65},{2,66},{3,67},{4,68},{5,69},{6,70},{7,71},{16,80},{1... | collective-permute-start | bytes 12296 | tf_op jit(solution)/shard_map/ppermute | solution.py:34
  129.1 5.0 %collective-permute-start.20 = (f32[8,128]{1,0:T(8,128)S(1)}, f32[8,128]{1,0:T(8,128)S(1)}, u32[]{:S(2)}, u32[]{:S(2)}) collective-permute-start(f32[8,128]{1,0:T(8,128)S(1)} %add.67), channel_id=1, source_target_pairs={{0,16},{1,17},{2,18},{3,19},{4,20},{5,21},{6,22},{7,23},{16,0},{17... | collective-permute-start | bytes 12296 | tf_op jit(solution)/shard_map/ppermute | solution.py:34
  134.0 6.9 %collective-permute-start.21 = (f32[8,128]{1,0:T(8,128)S(1)}, f32[8,128]{1,0:T(8,128)S(1)}, u32[]{:S(2)}, u32[]{:S(2)}) collective-permute-start(f32[8,128]{1,0:T(8,128)S(1)} %add.68), channel_id=1, source_target_pairs={{0,8},{1,9},{2,10},{3,11},{4,12},{5,13},{6,14},{7,15},{16,24},{17,... | collective-permute-start | bytes 12296 | tf_op jit(solution)/shard_map/ppermute | solution.py:34
  (12 other events, 75.3 us)

commit v5 on v4

--- a/solution.py
+++ b/solution.py
@@ -230,11 +230,12 @@
     limit_ref[...] = jnp.maximum(limit_ref[...], largest(acc))
     mine_acc_ref[:ROWS, :] = acc[:ROWS]
     other_acc_ref[:ROWS, :] = acc[ROWS:]
-    row = lax.broadcasted_iota(jnp.int32, (8, width), 0)
-    sums = jnp.zeros((8, width), jnp.float32)
-    for place in range(3):
-        sums = jnp.where(row == place, jnp.sum(sums_ref[place]), sums)
     power = power_of(jnp.full((8, width), jnp.max(limit_ref[...])))
+    sums = power
+    if last:
+        row = lax.broadcasted_iota(jnp.int32, (8, width), 0)
+        for place in range(3):
+            sums = jnp.where(row == place, jnp.sum(sums_ref[place]), sums)
     for ref in (mine_acc_ref, other_acc_ref):
         ref[ROWS : ROWS + 8, :] = sums
         ref[ROWS + 8 :, :] = power

time: 149 us -> 149 us (level)
  no operation moved by 1% of the time
where the time goes in v5:
time: 149 us; the launch traced here: 148 us
  waiting for transfers between devices  50.8 us (34%)
  starting transfers between devices  37.7 us (25%)
  Pallas kernels  35.6 us (24%)
  other arithmetic  12.5 us (8%)
  local copies, waits for them, and re-layouts  7.84 us (5%)
  between operations  4.04 us (3%)
    ppermute x25, waiting for transfers between devices, send(): return lax.ppermute(value, AXES, pairs)  50.8 us
    ppermute x25, starting transfers between devices, send(): return lax.ppermute(value, AXES, pairs)  37.7 us
    pallas_call x2, Pallas kernels, pairs(): pl.pallas_call(functools.partial(pairs_kernel, count, last, last), grid=(...  26.9 us
    unnamed x22, local copies, waits for them, and re-layouts  7.14 us
    pallas_call x2, Pallas kernels, tangent_part(): pl.pallas_call(tangent_kernel, in_specs=[pl.BlockSpec(memory_space=pltpu....  6.1 us
    convert_element_type x2, other arithmetic, packed(): return rows.astype(jnp.float16).reshape(BLOCK, -1)  4.5 us
    add x1, other arithmetic, on_device(): image_sum = image_sum + unpacked(rows)  3.07 us
  transfers between devices with their start and end apart: 25, of which 10 were waited for; matrix products, arithmetic and copies ran while one was open for 7% of the time, Pallas kernels for 20%

profile of v5, /device:TPU:0, one launch (start us, length us, event | category | flops | bytes accessed | tf_op | source)
XLA Modules:
  0.0 148.5 jit_solution(8609512135812741456)
XLA Ops:
  0.6 2.6 %halves.1 = (bf16[256,1152]{1,0:T(8,128)(2,1)}, bf16[256,1152]{1,0:T(8,128)(2,1)}) custom-call(f32[256,1152]{1,0:T(8,128)} %embeds_ref.2, f32[256,1152]{1,0:T(8,128)} %embeds_ref.3), custom_call_target="tpu_custom_call" | custom-call | tf_op jit(solution)/shard_map/halves/pallas_call | solution.py:129
  4.8 5.0 %collective-permute-start.3 = (bf16[256,1152]{1,0:T(8,128)(2,1)}, bf16[256,1152]{1,0:T(8,128)(2,1)S(1)}, u32[]{:S(2)}, u32[]{:S(2)}) collective-permute-start(bf16[256,1152]{1,0:T(8,128)(2,1)} %get-tuple-element.32.refs_5_), channel_id=1, source_target_pairs={{0,112},{1,113},{2,114},{3,115},{4,116},{5,117},{6,118},{7,119},{1... | collective-permute-start | bytes 1769480 | tf_op jit(solution)/shard_map/ppermute | solution.py:34
  9.9 1.7 %collective-permute-start.5 = (bf16[256,1152]{1,0:T(8,128)(2,1)}, bf16[256,1152]{1,0:T(8,128)(2,1)S(1)}, u32[]{:S(2)}, u32[]{:S(2)}) collective-permute-start(bf16[256,1152]{1,0:T(8,128)(2,1)} %get-tuple-element.32.refs_5_), channel_id=1, source_target_pairs={{0,120},{1,121},{2,122},{3,123},{4,124},{5,125},{6,126},{7,127},{1... | collective-permute-start | bytes 1769480 | tf_op jit(solution)/shard_map/ppermute | solution.py:34
  11.6 1.7 %collective-permute-start.1 = (bf16[256,1152]{1,0:T(8,128)(2,1)}, bf16[256,1152]{1,0:T(8,128)(2,1)S(1)}, u32[]{:S(2)}, u32[]{:S(2)}) collective-permute-start(bf16[256,1152]{1,0:T(8,128)(2,1)} %get-tuple-element.30.refs_1_), channel_id=1, source_target_pairs={{0,6},{1,7},{2,0},{3,1},{4,2},{5,3},{6,4},{7,5},{16,22},{17,23},{1... | collective-permute-start | bytes 1769480 | tf_op jit(solution)/shard_map/ppermute | solution.py:34
  13.3 1.8 %collective-permute-start.2 = (bf16[256,1152]{1,0:T(8,128)(2,1)}, bf16[256,1152]{1,0:T(8,128)(2,1)S(1)}, u32[]{:S(2)}, u32[]{:S(2)}) collective-permute-start(bf16[256,1152]{1,0:T(8,128)(2,1)} %get-tuple-element.30.refs_1_), channel_id=1, source_target_pairs={{0,4},{1,5},{2,6},{3,7},{4,0},{5,1},{6,2},{7,3},{16,20},{17,21},{1... | collective-permute-start | bytes 1769480 | tf_op jit(solution)/shard_map/ppermute | solution.py:34
  15.1 4.5 %collective-permute-done.refs_2_ = bf16[256,1152]{1,0:T(8,128)(2,1)S(1)} collective-permute-done((bf16[256,1152]{1,0:T(8,128)(2,1)}, bf16[256,1152]{1,0:T(8,128)(2,1)S(1)}, u32[]{:S(2)}, u32[]{:S(2)}) %collective-permute-start) | collective-permute-done | bytes 589856 | tf_op jit(solution)/shard_map/ppermute | solution.py:34
  19.7 13.2 %collective-permute-done.3.refs_6_ = bf16[256,1152]{1,0:T(8,128)(2,1)S(1)} collective-permute-done((bf16[256,1152]{1,0:T(8,128)(2,1)}, bf16[256,1152]{1,0:T(8,128)(2,1)S(1)}, u32[]{:S(2)}, u32[]{:S(2)}) %collective-permute-start.3) | collective-permute-done | bytes 589856 | tf_op jit(solution)/shard_map/ppermute | solution.py:34
  34.8 3.3 %collective-permute-done.1.refs_3_ = bf16[256,1152]{1,0:T(8,128)(2,1)S(1)} collective-permute-done((bf16[256,1152]{1,0:T(8,128)(2,1)}, bf16[256,1152]{1,0:T(8,128)(2,1)S(1)}, u32[]{:S(2)}, u32[]{:S(2)}) %collective-permute-start.1) | collective-permute-done | bytes 589856 | tf_op jit(solution)/shard_map/ppermute | solution.py:34
  38.1 1.9 %collective-permute-start.4 = (bf16[256,1152]{1,0:T(8,128)(2,1)}, bf16[256,1152]{1,0:T(8,128)(2,1)S(1)}, u32[]{:S(2)}, u32[]{:S(2)}) collective-permute-start(bf16[256,1152]{1,0:T(8,128)(2,1)} %get-tuple-element.32.refs_5_), channel_id=1, source_target_pairs={{0,8},{1,9},{2,10},{3,11},{4,12},{5,13},{6,14},{7,15},{16,24},{17,... | collective-permute-start | bytes 1769480 | tf_op jit(solution)/shard_map/ppermute | solution.py:34
  42.2 19.9 %pairs.2 = (f32[816,1152]{1,0:T(8,128)S(1)}, f32[816,1152]{1,0:T(8,128)}, f32[1024,1152]{1,0:T(8,128)S(1)}, f32[3,8,128]{2,1,0:T(8,128)S(1)}) custom-call(f32[3]{0:T(128)S(1)} %pad_maximum_fusion.refs_0_.scalars_ref, bf16[256,1152]{1,0:T(8,128)(2,1)S(1)} %copy-done.8, bf16[256,1152]{1,0:T(8,128)(2,1)S(1)} %collective-permute-done.refs_2_, ...), custom_call_target="tpu_custom_call" | custom-call | flops 10871635968 | bytes 1048576 | tf_op jit(solution)/shard_map/pairs/pallas_call | solution.py:294
  62.1 1.8 %copy-done = f32[816,1152]{1,0:T(8,128)} copy-done((f32[816,1152]{1,0:T(8,128)}, f32[816,1152]{1,0:T(8,128)S(1)}, u32[]{:S(2)}) %copy-start) | copy-done | bytes 3760152
  63.9 2.0 %collective-permute-done.9.refs_6_ = bf16[256,1152]{1,0:T(8,128)(2,1)S(1)} collective-permute-done((bf16[256,1152]{1,0:T(8,128)(2,1)S(1)}, bf16[256,1152]{1,0:T(8,128)(2,1)S(1)}, u32[]{:S(2)}, u32[]{:S(2)}) %collective-permute-start.9) | collective-permute-done | bytes 589856 | tf_op jit(solution)/shard_map/ppermute | solution.py:34
  66.0 7.0 %pairs.3 = (f32[272,1152]{1,0:T(8,128)S(1)}, f32[272,1152]{1,0:T(8,128)}, f32[256,1152]{1,0:T(8,128)S(1)}, f32[272,1152]{1,0:T(8,128)S(1)}, f32[272,1152]{1,0:T(8,128)S(1)}, /*index=5*/f32[272,1152]{1,0:T(8,128)S(1)}) custom-call(f32[3]{0:T(128)S(1)} %pad_maximum_fusion.refs_0_.scalars_ref, bf16[256,1152]{1,0:T(8,128)(2,1)S(1)} %copy-done.9, ...), custom_call_target="tpu_custom_call" | custom-call | flops 12079595520 | bytes 1048576 | tf_op jit(solution)/shard_map/pairs/pallas_call | solution.py:294
  77.7 2.9 %fusion.2 = (f16[272,1152]{1,0:T(8,128)(2,1)S(1)}, f16[272,1152]{1,0:T(8,128)(2,1)S(1)}) fusion(f32[816,1152]{1,0:T(8,128)} %collective-permute-done.10, f32[816,1152]{1,0:T(8,128)} %copy-done, f32[8,1152]{1,0:T(8,128)S(1)} %get-tuple-element.58, f32[8,1152]{1,0:T(8,128)S(1)} %get-tuple-element.57, pred[272]{0:T(512)(128)(4,1)S(1)} %iota.32, ...), kind=kLoop, calls=%fused_computation.3 | loop fusion | flops 2506752 | bytes 6414608 | tf_op jit(solution)/shard_map/convert_element_type | solution.py:344
  84.3 3.0 %collective-permute-start.13 = (f32[8,128]{1,0:T(8,128)S(1)}, f32[8,128]{1,0:T(8,128)S(1)}, u32[]{:S(2)}, u32[]{:S(2)}) collective-permute-start(f32[8,128]{1,0:T(8,128)S(1)} %add.62), channel_id=1, source_target_pairs={{0,4},{1,5},{2,6},{3,7},{4,0},{5,1},{6,2},{7,3},{16,20},{17,21},{1... | collective-permute-start | bytes 12296 | tf_op jit(solution)/shard_map/ppermute | solution.py:34
  91.0 1.7 %collective-permute-start.17 = (f16[272,1152]{1,0:T(8,128)(2,1)S(1)}, f16[272,1152]{1,0:T(8,128)(2,1)S(1)}, u32[]{:S(2)}, u32[]{:S(2)}) collective-permute-start(f16[272,1152]{1,0:T(8,128)(2,1)S(1)} %fusion.6), channel_id=1, source_target_pairs={{8,0},{9,1},{10,2},{11,3},{12,4},{13,5},{14,6},{15,7},{24,16},{25,... | collective-permute-start | bytes 1880072 | tf_op jit(solution)/shard_map/ppermute | solution.py:34
  92.8 3.6 %collective-permute-start.22 = (f16[272,1152]{1,0:T(8,128)(2,1)S(1)}, f16[272,1152]{1,0:T(8,128)(2,1)S(1)}, u32[]{:S(2)}, u32[]{:S(2)}) collective-permute-start(f16[272,1152]{1,0:T(8,128)(2,1)S(1)} %convert_element_type.51), channel_id=1, source_target_pairs={{2,0},{3,1},{4,2},{5,3},{6,4},{7,5},{0,6},{1,7},{18,16},{19,17},{2... | collective-permute-start | bytes 1880072 | tf_op jit(solution)/shard_map/ppermute | solution.py:34
  96.6 23.0 %collective-permute-done.16 = f16[272,1152]{1,0:T(8,128)(2,1)S(1)} collective-permute-done((f16[272,1152]{1,0:T(8,128)(2,1)S(1)}, f16[272,1152]{1,0:T(8,128)(2,1)S(1)}, u32[]{:S(2)}, u32[]{:S(2)}) %collective-permute-start.16) | collective-permute-done | bytes 626720 | tf_op jit(solution)/shard_map/ppermute | solution.py:34
  120.2 3.3 %collective-permute-start.24 = (f16[272,1152]{1,0:T(8,128)(2,1)S(1)}, f16[272,1152]{1,0:T(8,128)(2,1)}, u32[]{:S(2)}, u32[]{:S(2)}) collective-permute-start(f16[272,1152]{1,0:T(8,128)(2,1)S(1)} %convert_element_type.55), channel_id=1, source_target_pairs={{4,0},{5,1},{6,2},{7,3},{0,4},{1,5},{2,6},{3,7},{20,16},{21,17},{2... | collective-permute-start | bytes 1880072 | tf_op jit(solution)/shard_map/ppermute | solution.py:34
  124.8 3.1 %fusion.18.accum_ref = f32[256,1152]{1,0:T(8,128)} fusion(f32[272,1152]{1,0:T(8,128)S(1)} %convert_element_type.50, f32[272,1152]{1,0:T(8,128)S(1)} %convert_element_type.49, f32[272,1152]{1,0:T(8,128)S(1)} %convert_element_type.48, f32[816,1152]{1,0:T(8,128)} %collective-permute-done.10, f32[816,1152]{1,0:T(8,128)} %copy-done, f32[8,1152]{1,0:T(8,128)S(1)} %fusion.28, ...), kind=kLoop, calls=%fused_computation.26 | loop fusion | flops 2064384 | bytes 7188480 | tf_op jit(solution)/shard_map/add | solution.py:402
  128.7 3.4 %collective-permute-start.20 = (f32[8,128]{1,0:T(8,128)S(1)}, f32[8,128]{1,0:T(8,128)S(1)}, u32[]{:S(2)}, u32[]{:S(2)}) collective-permute-start(f32[8,128]{1,0:T(8,128)S(1)} %add.67), channel_id=1, source_target_pairs={{0,16},{1,17},{2,18},{3,19},{4,20},{5,21},{6,22},{7,23},{16,0},{17... | collective-permute-start | bytes 12296 | tf_op jit(solution)/shard_map/ppermute | solution.py:34
  133.6 3.8 %collective-permute-start.21 = (f32[8,128]{1,0:T(8,128)S(1)}, f32[8,128]{1,0:T(8,128)S(1)}, u32[]{:S(2)}, u32[]{:S(2)}) collective-permute-start(f32[8,128]{1,0:T(8,128)S(1)} %add.68), channel_id=1, source_target_pairs={{0,8},{1,9},{2,10},{3,11},{4,12},{5,13},{6,14},{7,15},{16,24},{17,... | collective-permute-start | bytes 12296 | tf_op jit(solution)/shard_map/ppermute | solution.py:34
  137.5 3.1 %tangent.2 = f32[256,1152]{1,0:T(8,128)} custom-call(f32[3]{0:T(128)} %copy-done.7, f32[256,1152]{1,0:T(8,128)} %embeds_ref.2, f32[256,1152]{1,0:T(8,128)} %fusion.18.accum_ref), custom_call_target="tpu_custom_call" | custom-call | tf_op jit(solution)/shard_map/tangent/pallas_call | solution.py:327
  144.3 3.0 %tangent.3 = f32[256,1152]{1,0:T(8,128)} custom-call(f32[3]{0:T(128)} %copy-done.7, f32[256,1152]{1,0:T(8,128)} %embeds_ref.3, f32[256,1152]{1,0:T(8,128)} %fusion.9.accum_ref), custom_call_target="tpu_custom_call" | custom-call | tf_op jit(solution)/shard_map/tangent/pallas_call | solution.py:327
  (88 shorter events, 24.0 us)
Async XLA Ops:
  3.2 16.4 %collective-permute-start = (bf16[256,1152]{1,0:T(8,128)(2,1)}, bf16[256,1152]{1,0:T(8,128)(2,1)S(1)}, u32[]{:S(2)}, u32[]{:S(2)}) collective-permute-start(bf16[256,1152]{1,0:T(8,128)(2,1)} %get-tuple-element.30.refs_1_), channel_id=1, source_target_pairs={{0,2},{1,3},{2,4},{3,5},{4,6},{5,7},{6,0},{7,1},{16,18},{17,19},{1... | collective-permute-start | bytes 1769480 | tf_op jit(solution)/shard_map/ppermute | solution.py:34
  4.8 28.0 %collective-permute-start.3 = (bf16[256,1152]{1,0:T(8,128)(2,1)}, bf16[256,1152]{1,0:T(8,128)(2,1)S(1)}, u32[]{:S(2)}, u32[]{:S(2)}) collective-permute-start(bf16[256,1152]{1,0:T(8,128)(2,1)} %get-tuple-element.32.refs_5_), channel_id=1, source_target_pairs={{0,112},{1,113},{2,114},{3,115},{4,116},{5,117},{6,118},{7,119},{1... | collective-permute-start | bytes 1769480 | tf_op jit(solution)/shard_map/ppermute | solution.py:34
  9.9 23.0 %collective-permute-start.5 = (bf16[256,1152]{1,0:T(8,128)(2,1)}, bf16[256,1152]{1,0:T(8,128)(2,1)S(1)}, u32[]{:S(2)}, u32[]{:S(2)}) collective-permute-start(bf16[256,1152]{1,0:T(8,128)(2,1)} %get-tuple-element.32.refs_5_), channel_id=1, source_target_pairs={{0,120},{1,121},{2,122},{3,123},{4,124},{5,125},{6,126},{7,127},{1... | collective-permute-start | bytes 1769480 | tf_op jit(solution)/shard_map/ppermute | solution.py:34
  11.6 26.5 %collective-permute-start.1 = (bf16[256,1152]{1,0:T(8,128)(2,1)}, bf16[256,1152]{1,0:T(8,128)(2,1)S(1)}, u32[]{:S(2)}, u32[]{:S(2)}) collective-permute-start(bf16[256,1152]{1,0:T(8,128)(2,1)} %get-tuple-element.30.refs_1_), channel_id=1, source_target_pairs={{0,6},{1,7},{2,0},{3,1},{4,2},{5,3},{6,4},{7,5},{16,22},{17,23},{1... | collective-permute-start | bytes 1769480 | tf_op jit(solution)/shard_map/ppermute | solution.py:34
  13.3 26.7 %collective-permute-start.2 = (bf16[256,1152]{1,0:T(8,128)(2,1)}, bf16[256,1152]{1,0:T(8,128)(2,1)S(1)}, u32[]{:S(2)}, u32[]{:S(2)}) collective-permute-start(bf16[256,1152]{1,0:T(8,128)(2,1)} %get-tuple-element.30.refs_1_), channel_id=1, source_target_pairs={{0,4},{1,5},{2,6},{3,7},{4,0},{5,1},{6,2},{7,3},{16,20},{17,21},{1... | collective-permute-start | bytes 1769480 | tf_op jit(solution)/shard_map/ppermute | solution.py:34
  19.7 20.4 %collective-permute-start.6 = (bf16[256,1152]{1,0:T(8,128)(2,1)}, bf16[256,1152]{1,0:T(8,128)(2,1)S(1)}, u32[]{:S(2)}, u32[]{:S(2)}) collective-permute-start(bf16[256,1152]{1,0:T(8,128)(2,1)} %get-tuple-element.32.refs_5_), channel_id=1, source_target_pairs={{0,1},{1,0},{2,3},{3,2},{4,5},{5,4},{6,7},{7,6},{16,17},{17,16},{1... | collective-permute-start | bytes 1769480 | tf_op jit(solution)/shard_map/ppermute | solution.py:34
  32.9 7.2 %collective-permute-start.7 = (bf16[256,1152]{1,0:T(8,128)(2,1)S(1)}, bf16[256,1152]{1,0:T(8,128)(2,1)S(1)}, u32[]{:S(2)}, u32[]{:S(2)}) collective-permute-start(bf16[256,1152]{1,0:T(8,128)(2,1)S(1)} %collective-permute-done.3.refs_6_), channel_id=1, source_target_pairs={{0,1},{1,0},{2,3},{3,2},{4,5},{5,4},{6,7},{7,6},{16,17},{17,16},{1... | collective-permute-start | bytes 1769480 | tf_op jit(solution)/shard_map/ppermute | solution.py:34
  32.9 7.2 %collective-permute-start.8 = (bf16[256,1152]{1,0:T(8,128)(2,1)S(1)}, bf16[256,1152]{1,0:T(8,128)(2,1)S(1)}, u32[]{:S(2)}, u32[]{:S(2)}) collective-permute-start(bf16[256,1152]{1,0:T(8,128)(2,1)S(1)} %collective-permute-done.5.refs_7_), channel_id=1, source_target_pairs={{0,1},{1,0},{2,3},{3,2},{4,5},{5,4},{6,7},{7,6},{16,17},{17,16},{1... | collective-permute-start | bytes 1769480 | tf_op jit(solution)/shard_map/ppermute | solution.py:34
  38.1 25.8 %collective-permute-start.4 = (bf16[256,1152]{1,0:T(8,128)(2,1)}, bf16[256,1152]{1,0:T(8,128)(2,1)S(1)}, u32[]{:S(2)}, u32[]{:S(2)}) collective-permute-start(bf16[256,1152]{1,0:T(8,128)(2,1)} %get-tuple-element.32.refs_5_), channel_id=1, source_target_pairs={{0,8},{1,9},{2,10},{3,11},{4,12},{5,13},{6,14},{7,15},{16,24},{17,... | collective-permute-start | bytes 1769480 | tf_op jit(solution)/shard_map/ppermute | solution.py:34
  63.9 2.0 %collective-permute-start.9 = (bf16[256,1152]{1,0:T(8,128)(2,1)S(1)}, bf16[256,1152]{1,0:T(8,128)(2,1)S(1)}, u32[]{:S(2)}, u32[]{:S(2)}) collective-permute-start(bf16[256,1152]{1,0:T(8,128)(2,1)S(1)} %collective-permute-done.4.refs_5_), channel_id=1, source_target_pairs={{0,1},{1,0},{2,3},{3,2},{4,5},{5,4},{6,7},{7,6},{16,17},{17,16},{1... | collective-permute-start | bytes 1769480 | tf_op jit(solution)/shard_map/ppermute | solution.py:34
  65.9 10.9 %collective-permute-start.10 = (f32[816,1152]{1,0:T(8,128)}, f32[816,1152]{1,0:T(8,128)}, u32[]{:S(2)}, u32[]{:S(2)}) collective-permute-start(f32[816,1152]{1,0:T(8,128)} %get-tuple-element.39), channel_id=1, source_target_pairs={{0,1},{1,0},{2,3},{3,2},{4,5},{5,4},{6,7},{7,6},{16,17},{17,16},{1... | collective-permute-start | bytes 11280392 | tf_op jit(solution)/shard_map/ppermute | solution.py:34
  76.3 4.3 %collective-permute-start.11 = (f32[272,1152]{1,0:T(8,128)}, f32[272,1152]{1,0:T(8,128)}, u32[]{:S(2)}, u32[]{:S(2)}) collective-permute-start(f32[272,1152]{1,0:T(8,128)} %get-tuple-element.40), channel_id=1, source_target_pairs={{0,1},{1,0},{2,3},{3,2},{4,5},{5,4},{6,7},{7,6},{16,17},{17,16},{1... | collective-permute-start | bytes 3760136 | tf_op jit(solution)/shard_map/ppermute | solution.py:34
  80.6 3.7 %collective-permute-start.12 = (f32[8,128]{1,0:T(8,128)S(1)}, f32[8,128]{1,0:T(8,128)S(1)}, u32[]{:S(2)}, u32[]{:S(2)}) collective-permute-start(f32[8,128]{1,0:T(8,128)S(1)} %slice.130), channel_id=1, source_target_pairs={{0,2},{1,3},{2,0},{3,1},{4,6},{5,7},{6,4},{7,5},{16,18},{17,19},{1... | collective-permute-start | bytes 12296 | tf_op jit(solution)/shard_map/ppermute | solution.py:34
  82.1 37.6 %collective-permute-start.15 = (f16[272,1152]{1,0:T(8,128)(2,1)S(1)}, f16[272,1152]{1,0:T(8,128)(2,1)S(1)}, u32[]{:S(2)}, u32[]{:S(2)}) collective-permute-start(f16[272,1152]{1,0:T(8,128)(2,1)S(1)} %get-tuple-element.42), channel_id=1, source_target_pairs={{112,0},{113,1},{114,2},{115,3},{116,4},{117,5},{118,6},{119,7},{8... | collective-permute-start | bytes 1880072 | tf_op jit(solution)/shard_map/ppermute | solution.py:34
  83.2 36.5 %collective-permute-start.16 = (f16[272,1152]{1,0:T(8,128)(2,1)S(1)}, f16[272,1152]{1,0:T(8,128)(2,1)S(1)}, u32[]{:S(2)}, u32[]{:S(2)}) collective-permute-start(f16[272,1152]{1,0:T(8,128)(2,1)S(1)} %get-tuple-element.43), channel_id=1, source_target_pairs={{120,0},{121,1},{122,2},{123,3},{124,4},{125,5},{126,6},{127,7},{0... | collective-permute-start | bytes 1880072 | tf_op jit(solution)/shard_map/ppermute | solution.py:34
  84.3 5.1 %collective-permute-start.13 = (f32[8,128]{1,0:T(8,128)S(1)}, f32[8,128]{1,0:T(8,128)S(1)}, u32[]{:S(2)}, u32[]{:S(2)}) collective-permute-start(f32[8,128]{1,0:T(8,128)S(1)} %add.62), channel_id=1, source_target_pairs={{0,4},{1,5},{2,6},{3,7},{4,0},{5,1},{6,2},{7,3},{16,20},{17,21},{1... | collective-permute-start | bytes 12296 | tf_op jit(solution)/shard_map/ppermute | solution.py:34
  91.0 28.8 %collective-permute-start.17 = (f16[272,1152]{1,0:T(8,128)(2,1)S(1)}, f16[272,1152]{1,0:T(8,128)(2,1)S(1)}, u32[]{:S(2)}, u32[]{:S(2)}) collective-permute-start(f16[272,1152]{1,0:T(8,128)(2,1)S(1)} %fusion.6), channel_id=1, source_target_pairs={{8,0},{9,1},{10,2},{11,3},{12,4},{13,5},{14,6},{15,7},{24,16},{25,... | collective-permute-start | bytes 1880072 | tf_op jit(solution)/shard_map/ppermute | solution.py:34
  92.8 27.3 %collective-permute-start.22 = (f16[272,1152]{1,0:T(8,128)(2,1)S(1)}, f16[272,1152]{1,0:T(8,128)(2,1)S(1)}, u32[]{:S(2)}, u32[]{:S(2)}) collective-permute-start(f16[272,1152]{1,0:T(8,128)(2,1)S(1)} %convert_element_type.51), channel_id=1, source_target_pairs={{2,0},{3,1},{4,2},{5,3},{6,4},{7,5},{0,6},{1,7},{18,16},{19,17},{2... | collective-permute-start | bytes 1880072 | tf_op jit(solution)/shard_map/ppermute | solution.py:34
  96.5 23.6 %collective-permute-start.23 = (f16[272,1152]{1,0:T(8,128)(2,1)S(1)}, f16[272,1152]{1,0:T(8,128)(2,1)S(1)}, u32[]{:S(2)}, u32[]{:S(2)}) collective-permute-start(f16[272,1152]{1,0:T(8,128)(2,1)S(1)} %convert_element_type.53), channel_id=1, source_target_pairs={{6,0},{7,1},{0,2},{1,3},{2,4},{3,5},{4,6},{5,7},{22,16},{23,17},{1... | collective-permute-start | bytes 1880072 | tf_op jit(solution)/shard_map/ppermute | solution.py:34
  119.9 3.7 %collective-permute-start.18 = (f32[8,128]{1,0:T(8,128)S(1)}, f32[8,128]{1,0:T(8,128)S(1)}, u32[]{:S(2)}, u32[]{:S(2)}) collective-permute-start(f32[8,128]{1,0:T(8,128)S(1)} %add.64), channel_id=1, source_target_pairs={{0,32},{1,33},{2,34},{3,35},{4,36},{5,37},{6,38},{7,39},{16,48},{1... | collective-permute-start | bytes 12296 | tf_op jit(solution)/shard_map/ppermute | solution.py:34
  120.2 21.5 %collective-permute-start.24 = (f16[272,1152]{1,0:T(8,128)(2,1)S(1)}, f16[272,1152]{1,0:T(8,128)(2,1)}, u32[]{:S(2)}, u32[]{:S(2)}) collective-permute-start(f16[272,1152]{1,0:T(8,128)(2,1)S(1)} %convert_element_type.55), channel_id=1, source_target_pairs={{4,0},{5,1},{6,2},{7,3},{0,4},{1,5},{2,6},{3,7},{20,16},{21,17},{2... | collective-permute-start | bytes 1880072 | tf_op jit(solution)/shard_map/ppermute | solution.py:34
  123.6 5.1 %collective-permute-start.19 = (f32[8,128]{1,0:T(8,128)S(1)}, f32[8,128]{1,0:T(8,128)S(1)}, u32[]{:S(2)}, u32[]{:S(2)}) collective-permute-start(f32[8,128]{1,0:T(8,128)S(1)} %add.66), channel_id=1, source_target_pairs={{0,64},{1,65},{2,66},{3,67},{4,68},{5,69},{6,70},{7,71},{16,80},{1... | collective-permute-start | bytes 12296 | tf_op jit(solution)/shard_map/ppermute | solution.py:34
  128.7 5.0 %collective-permute-start.20 = (f32[8,128]{1,0:T(8,128)S(1)}, f32[8,128]{1,0:T(8,128)S(1)}, u32[]{:S(2)}, u32[]{:S(2)}) collective-permute-start(f32[8,128]{1,0:T(8,128)S(1)} %add.67), channel_id=1, source_target_pairs={{0,16},{1,17},{2,18},{3,19},{4,20},{5,21},{6,22},{7,23},{16,0},{17... | collective-permute-start | bytes 12296 | tf_op jit(solution)/shard_map/ppermute | solution.py:34
  133.6 6.9 %collective-permute-start.21 = (f32[8,128]{1,0:T(8,128)S(1)}, f32[8,128]{1,0:T(8,128)S(1)}, u32[]{:S(2)}, u32[]{:S(2)}) collective-permute-start(f32[8,128]{1,0:T(8,128)S(1)} %add.68), channel_id=1, source_target_pairs={{0,8},{1,9},{2,10},{3,11},{4,12},{5,13},{6,14},{7,15},{16,24},{17,... | collective-permute-start | bytes 12296 | tf_op jit(solution)/shard_map/ppermute | solution.py:34
  (12 other events, 75.1 us)
